TPU v7x, 128 devices: a whole 4x4x4 slice. The times are simulated.
128 devices in a mesh: blk: 16 (over x, z_lo, core), rep: 8 (over y, z_hi).
Axes of the slice: x: 4, y: 4, z: 4 (z_hi: 2, z_lo: 2; z = z_hi * 2 + z_lo), core: 2. Of those that a mesh axis runs over, the one named last changes fastest.
Arguments:
- features: float32 [49152, 602], P(('blk', 'rep')), may hold values from -6 to 6
- weight: float32 [602, 256], replicated, may hold values from -0.25 to 0.25
- cotangent: float32 [49152, 256], P(('blk', 'rep')), may hold values from -0.10825317 to 0.10825317
- degree: int32 [49152], P(('blk', 'rep')), may hold values from 2 to 13
- tile_row: int32 [16, 8, 256], P('blk', 'rep'), may hold values from 0 to 23, as said below
- tile_col: int32 [16, 8, 256], P('blk', 'rep'), may hold values from 0 to 47
- edge_dst: int32 [16, 8, 256, 256], P('blk', 'rep'), may hold values from 0 to 127
- edge_src: int32 [16, 8, 256, 256], P('blk', 'rep'), may hold values from 0 to 127
- tile_live: int32 [16, 8], P('blk', 'rep'), may hold values from 64 to 256, as said below
Outputs:
- hidden: float32 [49152, 256], P(('blk', 'rep'))
- weight_grad: float32 [602, 256], replicated
Inputs may be any that keep to these rules, and one draw needn't show every extreme that they name: On each device the pairs (tile_row, tile_col) of its 256 slots are all different. `tile_live`: at least one device has all 256 slots live.
All inputs are finite; a program needn't handle non-finite values.
Results may differ from a plain program's by a relative error of at most 0.0003.
Values sent between devices are 32-bit elements; how exact they have to be, the bound alone decides.
No kernel may reach another device: no remote copies, remote signals or barrier semaphores. Data moves between devices by JAX's collectives and lax.ppermute only.
A program may use at most 192 MiB of HBM per device.

v0:
```python
from functools import partial

import jax
import jax.numpy as jnp
from jax import lax
from jax.sharding import PartitionSpec as P

TILE = 128


HIGH = lax.Precision.HIGHEST
activation = partial(jax.nn.gelu, approximate=True)
stride_tiles = 32


def build_tiles(edge_dst, edge_src):
    slot_count = edge_dst.shape[2]
    dst_flat = edge_dst.reshape(slot_count // stride_tiles, stride_tiles, -1)
    src_flat = edge_src.reshape(slot_count // stride_tiles, stride_tiles, -1)
    node_ids = jnp.arange(TILE, dtype=jnp.int32)

    def one_group(item):
        dst_ids, src_ids = item
        dst_onehot = (dst_ids[..., None] == node_ids).astype(jnp.bfloat16)
        src_onehot = (src_ids[..., None] == node_ids).astype(jnp.bfloat16)
        return jnp.einsum(
            "tei,tej->tij", dst_onehot, src_onehot, preferred_element_type=jnp.float32
        )

    grouped = lax.map(one_group, (dst_flat, src_flat))
    return grouped.reshape(slot_count, TILE, TILE)


def aggregate(tiles, row_ids, col_ids, live_count, source, target_blocks, transpose):
    hidden_width = source.shape[2]
    source_blocks = source.shape[0]
    source_range = jnp.arange(source_blocks, dtype=jnp.int32)
    target_range = jnp.arange(target_blocks, dtype=jnp.int32)

    def one_block(block, totals):
        start = block * stride_tiles
        tile_block = lax.dynamic_slice_in_dim(tiles, start, stride_tiles, 0)
        block_rows = lax.dynamic_slice_in_dim(row_ids, start, stride_tiles, 0)
        block_cols = lax.dynamic_slice_in_dim(col_ids, start, stride_tiles, 0)
        keep_mask = (start + jnp.arange(stride_tiles) < live_count).astype(jnp.float32)[:, None]
        if transpose:
            pick_ids = block_rows
            place_ids = block_cols
        else:
            pick_ids = block_cols
            place_ids = block_rows
        pick_table = (pick_ids[:, None] == source_range[None, :]).astype(jnp.float32)
        inputs = jnp.einsum(
            "tb,bjh->tjh", pick_table, source, precision=HIGH, preferred_element_type=jnp.float32
        )
        if transpose:
            output = jnp.einsum(
                "tji,tjh->tih",
                tile_block,
                inputs,
                precision=HIGH,
                preferred_element_type=jnp.float32,
            )
        else:
            output = jnp.einsum(
                "tij,tjh->tih",
                tile_block,
                inputs,
                precision=HIGH,
                preferred_element_type=jnp.float32,
            )
        place_table = (place_ids[:, None] == target_range[None, :]).astype(jnp.float32) * keep_mask
        return totals + jnp.einsum(
            "tb,tih->bih", place_table, output, precision=HIGH, preferred_element_type=jnp.float32
        )

    step_count = (live_count + stride_tiles - 1) // stride_tiles
    start_totals = jnp.zeros((target_blocks, TILE, hidden_width), jnp.float32)
    return lax.fori_loop(0, step_count, one_block, start_totals)


def local(features, weight, cotangent, degree, tile_row, tile_col, edge_dst, edge_src, tile_live):
    own_rows = features.shape[0]
    hidden_width = weight.shape[1]
    own_blocks = own_rows // TILE
    group_blocks = own_blocks * lax.axis_size("rep")
    cycle_blocks = own_blocks * lax.axis_size("blk")
    scales = lax.rsqrt(degree.astype(jnp.float32))[:, None]
    row_ids = tile_row.reshape(-1)
    col_ids = tile_col.reshape(-1)
    live_count = tile_live.reshape(())
    scaled = jnp.dot(features, weight, precision=HIGH, preferred_element_type=jnp.float32) * scales
    cycle_rows = lax.all_gather(scaled, "blk", axis=0, tiled=True)
    tiles = build_tiles(edge_dst, edge_src)
    sums = aggregate(
        tiles,
        row_ids,
        col_ids,
        live_count,
        cycle_rows.reshape(cycle_blocks, TILE, hidden_width),
        group_blocks,
        False,
    )
    sums = sums.reshape(group_blocks * TILE, hidden_width)
    own_sums = lax.psum_scatter(sums, "rep", scatter_dimension=0, tiled=True)
    pre = (own_sums + scaled) * scales
    hidden, pull = jax.vjp(activation, pre)
    (own_grad,) = pull(cotangent)
    back_own = own_grad * scales
    back_group = lax.all_gather(back_own, "rep", axis=0, tiled=True)
    reverse = aggregate(
        tiles,
        row_ids,
        col_ids,
        live_count,
        back_group.reshape(group_blocks, TILE, hidden_width),
        cycle_blocks,
        True,
    )
    reverse = reverse.reshape(cycle_blocks * TILE, hidden_width)
    column_grad = lax.psum_scatter(reverse, "blk", scatter_dimension=0, tiled=True)
    grad_rows = (column_grad + back_own) * scales
    local_grad = jnp.einsum(
        "ni,nh->ih", features, grad_rows, precision=HIGH, preferred_element_type=jnp.float32
    )
    weight_grad = lax.psum(local_grad, ("blk", "rep"))
    return (hidden, weight_grad)


def solution(mesh):
    return jax.shard_map(
        local,
        mesh=mesh,
        in_specs=(
            P(("blk", "rep"), None),
            P(),
            P(("blk", "rep"), None),
            P(("blk", "rep")),
            P("blk", "rep", None),
            P("blk", "rep", None),
            P("blk", "rep", None, None),
            P("blk", "rep", None, None),
            P("blk", "rep"),
        ),
        out_specs=(P(("blk", "rep"), None), P()),
        check_vma=False,
    )
```

profile of v0, /device:TPU:1, one launch (start us, length us, event | category | flops | bytes accessed | tf_op | source)
XLA Modules:
  0.0 878.1 jit_solution(339844692921733894)
XLA Ops:
  12.7 27.2 %while.36 = (s32[]{:T(128)}, f32[8,32,128,128]{3,2,1,0:T(8,128)}, s32[8,32,256]{2,1,0:T(8,128)}, s32[8,32,256]{2,1,0:T(8,128)}, s32[]{:T(128)}) while((s32[]{:T(128)}, f32[8,32,128,128]{3,2,1,0:T(8,128)}, s32[8,32,256]{2,1,0:T(8,128)}, s32[8,32,256]{2,1,0:T(8,128)}, s32[]{:T(128)}) %tuple.89), condition=%wide.region_1.2_spmd.clone.clone, body=%wide.region_0.1_spmd.clone.clone.sunk | while | flops 270532608 | bytes 2293837 | solution.py:30
  39.9 18.2 %all-gather.3.cloned.1.call-done = f32[6144,256]{1,0:T(8,128)} async-done(((f32[384,256]{1,0:T(8,128)}), f32[6144,256]{1,0:T(8,128)}) %all-gather.3.cloned.1.call-update) | async-done | bytes 6291472 | tf_op jit(solution)/shard_map/all_gather | solution.py:93
  60.0 141.6 %while.34 = (s32[]{:T(128)}, f32[24,128,256]{2,0,1:T(8,128)}, s32[]{:T(128)}, s32[256]{0:T(256)S(1)}, s32[]{:T(128)}, /*index=5*/f32[256,128,128]{2,1,0:T(8,128)...) while((s32[]{:T(128)}, f32[24,128,256]{2,0,1:T(8,128)}, ...), condition=%wide.region_3.4_spmd.clone, body=%wide.region_2.3_spmd.clone.sunk | while | flops 2517371904 | bytes 56624376 | solution.py:79
  60.5 8.9 %fusion.90 = f32[32,128,256]{2,0,1:T(8,128)S(1)} fusion(f32[48,128,256]{2,1,0:T(8,128)} %get-tuple-element.424, s32[32]{0:T(128)S(1)} %dynamic_slice.49), kind=kOutput, calls=%fused_computation.5.clone.1 | convolution fusion | flops 603981312 | bytes 10485888 | tf_op jit(solution)/shard_map/while/body/tb,bjh->tjh/dot_general | solution.py:53
  69.4 7.8 fusion.91
  86.1 8.9 %fusion.90 = f32[32,128,256]{2,0,1:T(8,128)S(1)} fusion(f32[48,128,256]{2,1,0:T(8,128)} %get-tuple-element.424, s32[32]{0:T(128)S(1)} %dynamic_slice.49), kind=kOutput, calls=%fused_computation.5.clone.1 | convolution fusion | flops 603981312 | bytes 10485888 | tf_op jit(solution)/shard_map/while/body/tb,bjh->tjh/dot_general | solution.py:53
  95.0 7.8 fusion.91
  111.7 8.9 %fusion.90 = f32[32,128,256]{2,0,1:T(8,128)S(1)} fusion(f32[48,128,256]{2,1,0:T(8,128)} %get-tuple-element.424, s32[32]{0:T(128)S(1)} %dynamic_slice.49), kind=kOutput, calls=%fused_computation.5.clone.1 | convolution fusion | flops 603981312 | bytes 10485888 | tf_op jit(solution)/shard_map/while/body/tb,bjh->tjh/dot_general | solution.py:53
  120.6 7.8 fusion.91
  137.3 8.9 %fusion.90 = f32[32,128,256]{2,0,1:T(8,128)S(1)} fusion(f32[48,128,256]{2,1,0:T(8,128)} %get-tuple-element.424, s32[32]{0:T(128)S(1)} %dynamic_slice.49), kind=kOutput, calls=%fused_computation.5.clone.1 | convolution fusion | flops 603981312 | bytes 10485888 | tf_op jit(solution)/shard_map/while/body/tb,bjh->tjh/dot_general | solution.py:53
  146.3 7.8 fusion.91
  163.0 8.9 %fusion.90 = f32[32,128,256]{2,0,1:T(8,128)S(1)} fusion(f32[48,128,256]{2,1,0:T(8,128)} %get-tuple-element.424, s32[32]{0:T(128)S(1)} %dynamic_slice.49), kind=kOutput, calls=%fused_computation.5.clone.1 | convolution fusion | flops 603981312 | bytes 10485888 | tf_op jit(solution)/shard_map/while/body/tb,bjh->tjh/dot_general | solution.py:53
  171.9 7.8 fusion.91
  206.3 155.9 %reduce-scatter.3.cloned.1.call-done = f32[384,256]{1,0:T(8,128)} async-done(((f32[3072,256]{1,0:T(8,128)}), f32[384,256]{1,0:T(8,128)}) %reduce-scatter.3.cloned.1.call-update) | async-done | bytes 393232 | tf_op jit(solution)/shard_map/reduce_scatter | solution.py:105
  364.6 63.6 %all-gather.5.cloned.1.call-done = f32[3072,256]{1,0:T(8,128)} async-done(((f32[384,256]{1,0:T(8,128)}), f32[3072,256]{1,0:T(8,128)}) %all-gather.5.cloned.1.call-update) | async-done | bytes 3145744 | tf_op jit(solution)/shard_map/all_gather | solution.py:110
  431.6 126.2 %while.35 = (s32[]{:T(128)}, f32[48,128,256]{2,0,1:T(8,128)}, s32[]{:T(128)}, s32[256]{0:T(256)S(1)}, s32[]{:T(128)}, /*index=5*/f32[256,128,128]{2,1,0:T(8,128)...) while((s32[]{:T(128)}, f32[48,128,256]{2,0,1:T(8,128)}, ...), condition=%wide.region_6.7_spmd.clone, body=%wide.region_5.6_spmd.clone.sunk | while | flops 2518159360 | bytes 78644488 | solution.py:79
  446.1 8.1 fusion.101
  471.4 8.1 fusion.101
  496.6 8.1 fusion.101
  521.9 8.1 fusion.101
  547.1 8.1 fusion.101
  557.9 9.1 %copy.13 = f32[48,128,256]{2,1,0:T(8,128)} copy(f32[48,128,256]{2,0,1:T(8,128)} %get-tuple-element.140) | data formatting | bytes 12582912 | tf_op jit(solution)/shard_map/while | solution.py:79
  567.0 150.9 %reduce-scatter.5.cloned.1.call-done = f32[384,256]{1,0:T(8,128)} async-done(((f32[6144,256]{1,0:T(8,128)}), f32[384,256]{1,0:T(8,128)}) %reduce-scatter.5.cloned.1.call-update) | async-done | bytes 393232 | tf_op jit(solution)/shard_map/reduce_scatter | solution.py:121
  721.0 148.5 %all-reduce.2.cloned.1.call-done = f32[602,256]{1,0:T(8,128)} async-done(((f32[602,256]{1,0:T(8,128)}), f32[602,256]{1,0:T(8,128)}) %all-reduce.2.cloned.1.call-update) | async-done | bytes 616464 | tf_op jit(solution)/shard_map/psum | solution.py:126
  (147 shorter events, 179.3 us)
Async XLA Ops:
  7.2 50.9 %all-gather.3.cloned.1.call-start = ((), (), s32[]{:S(2)}) async-start(), calls=%async_computation.2 | async-start | bytes 6684672 | tf_op jit(solution)/shard_map/all_gather | solution.py:93
  12.0 350.3 %reduce-scatter.3.cloned.1.call-start = ((), (), s32[]{:S(2)}) async-start(), calls=%async_computation.3 | async-start | bytes 3538944 | tf_op jit(solution)/shard_map/reduce_scatter | solution.py:105
  12.7 47.3 %copy-start.7 = (s32[1,1,256]{2,1,0:T(1,128)S(1)}, s32[1,1,256]{2,1,0:T(1,128)}, u32[]{:S(2)}) copy-start(s32[1,1,256]{2,1,0:T(1,128)} %param.19) | copy-start | bytes 3076
  12.7 47.3 %copy-start.8 = (s32[1,1,256]{2,1,0:T(1,128)S(1)}, s32[1,1,256]{2,1,0:T(1,128)}, u32[]{:S(2)}) copy-start(s32[1,1,256]{2,1,0:T(1,128)} %param.20) | copy-start | bytes 3076
  69.4 8.6 copy-start.2
  95.0 8.6 copy-start.2
  120.6 8.6 copy-start.2
  146.2 8.6 copy-start.2
  171.9 8.6 copy-start.2
  201.6 160.6 %copy-start.4 = (f32[384,256]{1,0:T(8,128)S(1)}, f32[384,256]{1,0:T(8,128)}, u32[]{:S(2)}) copy-start(f32[384,256]{1,0:T(8,128)} %convolution_multiply_fusion) | copy-start | bytes 1179652
  201.6 160.6 %copy-start.6 = (f32[384,256]{1,0:T(8,128)S(1)}, f32[384,256]{1,0:T(8,128)}, u32[]{:S(2)}) copy-start(f32[384,256]{1,0:T(8,128)} %param.17) | copy-start | bytes 1179652
  206.3 221.9 %all-gather.5.cloned.1.call-start = ((), (), s32[]{:S(2)}) async-start(), calls=%async_computation.4 | async-start | bytes 3538944 | tf_op jit(solution)/shard_map/all_gather | solution.py:110
  364.5 353.4 %reduce-scatter.5.cloned.1.call-start = ((), (), s32[]{:S(2)}) async-start(), calls=%async_computation.5 | async-start | bytes 6684672 | tf_op jit(solution)/shard_map/reduce_scatter | solution.py:121
  431.7 14.4 %slice-start = ((s8[6291456]{0:T(1024)(128)(4,1)}), s8[4194304]{0:T(1024)(128)(4,1)S(1)}, s32[]{:S(2)}) async-start(s8[6291456]{0:T(1024)(128)(4,1)} %bitcast.46), calls=%async_computation.7 | async-start | bytes 8388608 | tf_op jit(solution)/shard_map/while
  437.7 8.4 slice-start.1
  456.9 14.4 %slice-start = ((s8[6291456]{0:T(1024)(128)(4,1)}), s8[4194304]{0:T(1024)(128)(4,1)S(1)}, s32[]{:S(2)}) async-start(s8[6291456]{0:T(1024)(128)(4,1)} %bitcast.46), calls=%async_computation.7 | async-start | bytes 8388608 | tf_op jit(solution)/shard_map/while
  462.9 8.4 slice-start.1
  482.2 14.4 %slice-start = ((s8[6291456]{0:T(1024)(128)(4,1)}), s8[4194304]{0:T(1024)(128)(4,1)S(1)}, s32[]{:S(2)}) async-start(s8[6291456]{0:T(1024)(128)(4,1)} %bitcast.46), calls=%async_computation.7 | async-start | bytes 8388608 | tf_op jit(solution)/shard_map/while
  488.2 8.4 slice-start.1
  507.4 14.4 %slice-start = ((s8[6291456]{0:T(1024)(128)(4,1)}), s8[4194304]{0:T(1024)(128)(4,1)S(1)}, s32[]{:S(2)}) async-start(s8[6291456]{0:T(1024)(128)(4,1)} %bitcast.46), calls=%async_computation.7 | async-start | bytes 8388608 | tf_op jit(solution)/shard_map/while
  513.4 8.4 slice-start.1
  532.7 14.4 %slice-start = ((s8[6291456]{0:T(1024)(128)(4,1)}), s8[4194304]{0:T(1024)(128)(4,1)S(1)}, s32[]{:S(2)}) async-start(s8[6291456]{0:T(1024)(128)(4,1)} %bitcast.46), calls=%async_computation.7 | async-start | bytes 8388608 | tf_op jit(solution)/shard_map/while
  567.0 150.9 %copy-start.5 = (f32[384,256]{1,0:T(8,128)S(1)}, f32[384,256]{1,0:T(8,128)}, u32[]{:S(2)}) copy-start(f32[384,256]{1,0:T(8,128)} %get-tuple-element.247) | copy-start | bytes 1179652
  567.0 302.5 %all-reduce.2.cloned.1.call-start = ((), (), s32[]{:S(2)}) async-start(), calls=%async_computation.6 | async-start | bytes 1245184 | tf_op jit(solution)/shard_map/psum | solution.py:126
  (12 other events, 31.5 us)
Sparse Core Ops, SparseCore 0:
  12.1 45.9 all-gather.2
  206.4 155.8 reduce-scatter.2
  365.4 62.7 all-gather.4
  567.1 150.7 reduce-scatter.4
  723.7 145.6 all-reduce.1
where the time goes:
time: 876 us; the launch traced here: 878 us
  waiting for transfers between devices  537 us (61%)
  matrix products  252 us (29%)
  local copies, waits for them, and re-layouts  51 us (6%)
  between operations  14.7 us (2%)
  loops' own time  14 us (2%)
  other arithmetic  9.52 us (1%)
    reduce_scatter x1, waiting for transfers between devices, local(): own_sums = lax.psum_scatter(sums, 'rep', scatter_dimension=0, tiled=True)  156 us
    reduce_scatter x1, waiting for transfers between devices, local(): lax.psum_scatter(reverse, 'blk', scatter_dimension=0, tiled=True)  151 us
    psum x1, waiting for transfers between devices, local(): weight_grad = lax.psum(local_grad, ('blk', 'rep'))  148 us
    dot_general x10, matrix products, one_block(): jnp.einsum('tb,bjh->tjh', pick_table, source, precision=HIGH, preferred_e...  74.5 us
    dot_general x10, matrix products, one_block(): jnp.einsum('tb,tih->bih', place_table, output, precision=HIGH, preferred_...  72.3 us
    all_gather x1, waiting for transfers between devices, local(): back_group = lax.all_gather(back_own, 'rep', axis=0, tiled=True)  63.6 us
    dot_general x5, matrix products, one_block(): jnp.einsum('tij,tjh->tih', tile_block, inputs, precision=HIGH, preferred_...  39 us
    dot_general x5, matrix products, one_block(): jnp.einsum('tji,tjh->tih', tile_block, inputs, precision=HIGH, preferred_...  38.3 us
  transfers between devices with their start and end apart: 5, of which 5 were waited for; matrix products, arithmetic and copies ran while one was open for 3% of the time, Pallas kernels for 0%

commit v1 on v0

v1 whole, which is shorter than its diff:
```python
from functools import partial

import jax
import jax.numpy as jnp
from jax import lax
from jax.experimental import pallas as pl
from jax.experimental.pallas import tpu as pltpu
from jax.sharding import PartitionSpec as P

TILE = 128
HIGH = lax.Precision.HIGHEST
activation = partial(jax.nn.gelu, approximate=True)
CHUNK = 32
UNROLL = 4
VMEM_LIMIT = 60 * 1024 * 1024


def tile_kernel(live_ref, dst_ref, src_ref, out_ref):
    first = pl.program_id(0) * CHUNK
    node_ids = lax.broadcasted_iota(jnp.int32, (TILE, dst_ref.shape[1]), 0)
    for t in range(CHUNK):
        dst_ids = jnp.where(first + t < live_ref[0], dst_ref[t : t + 1, :], TILE)
        dst_hot = (dst_ids == node_ids).astype(jnp.bfloat16)
        src_hot = (src_ref[t : t + 1, :] == node_ids).astype(jnp.bfloat16)
        counts = lax.dot_general(
            dst_hot, src_hot, (((1,), (1,)), ((), ())), preferred_element_type=jnp.float32
        )
        out_ref[t] = counts.astype(jnp.bfloat16)


def build_tiles(live, edge_dst, edge_src):
    slots, edges = edge_dst.shape
    return pl.pallas_call(
        tile_kernel,
        grid_spec=pltpu.PrefetchScalarGridSpec(
            num_scalar_prefetch=1,
            grid=(slots // CHUNK,),
            in_specs=[pl.BlockSpec((CHUNK, edges), lambda g, live: (g, 0))] * 2,
            out_specs=pl.BlockSpec((CHUNK, TILE, TILE), lambda g, live: (g, 0, 0)),
        ),
        out_shape=jax.ShapeDtypeStruct((slots, TILE, TILE), jnp.bfloat16),
        compiler_params=pltpu.CompilerParams(vmem_limit_bytes=VMEM_LIMIT),
        cost_estimate=pl.CostEstimate(
            flops=2 * slots * TILE * TILE * edges, bytes_accessed=10**7, transcendentals=0
        ),
    )(live, edge_dst, edge_src)


def aggregate_kernel(transpose, live_ref, pick_ref, place_ref, tiles_ref, source_ref, out_ref, split):
    step = pl.program_id(0)
    first = step * CHUNK

    @pl.when(step == 0)
    def _():
        out_ref[...] = jnp.zeros_like(out_ref)

        def split_block(b, carry):
            value = source_ref[b]
            high = value.astype(jnp.bfloat16)
            split[b, :TILE] = high
            split[b, TILE:] = (value - high.astype(jnp.float32)).astype(jnp.bfloat16)
            return carry

        lax.fori_loop(0, source_ref.shape[0], split_block, 0)

    left = jnp.clip(live_ref[0] - first, 0, CHUNK)

    def some_tiles(group, carry):
        products = []
        for k in range(UNROLL):
            t = group * UNROLL + k
            tile = tiles_ref[t]
            picked = split[pick_ref[first + t]]
            twice = jnp.concatenate([tile, tile], axis=0 if transpose else 1)
            products.append(
                lax.dot_general(
                    twice,
                    picked,
                    (((0 if transpose else 1,), (0,)), ((), ())),
                    preferred_element_type=jnp.float32,
                )
            )
        for k in range(UNROLL):
            out_ref[place_ref[first + group * UNROLL + k]] += products[k]
        return carry

    lax.fori_loop(0, (left + UNROLL - 1) // UNROLL, some_tiles, 0)


def aggregate(tiles, live, pick_ids, place_ids, source, target_blocks, transpose):
    slots = tiles.shape[0]
    source_blocks, _, width = source.shape
    return pl.pallas_call(
        partial(aggregate_kernel, transpose),
        grid_spec=pltpu.PrefetchScalarGridSpec(
            num_scalar_prefetch=3,
            grid=(slots // CHUNK,),
            in_specs=[
                pl.BlockSpec((CHUNK, TILE, TILE), lambda g, *_: (g, 0, 0)),
                pl.BlockSpec((source_blocks, TILE, width), lambda g, *_: (0, 0, 0)),
            ],
            out_specs=pl.BlockSpec((target_blocks, TILE, width), lambda g, *_: (0, 0, 0)),
            scratch_shapes=[pltpu.VMEM((source_blocks, 2 * TILE, width), jnp.bfloat16)],
        ),
        out_shape=jax.ShapeDtypeStruct((target_blocks, TILE, width), jnp.float32),
        compiler_params=pltpu.CompilerParams(vmem_limit_bytes=VMEM_LIMIT),
        cost_estimate=pl.CostEstimate(
            flops=4 * slots * TILE * TILE * width, bytes_accessed=2 * 10**7, transcendentals=0
        ),
    )(live, pick_ids, place_ids, tiles, source)


def local(features, weight, cotangent, degree, tile_row, tile_col, edge_dst, edge_src, tile_live):
    own_rows = features.shape[0]
    hidden_width = weight.shape[1]
    own_blocks = own_rows // TILE
    group_blocks = own_blocks * lax.axis_size("rep")
    cycle_blocks = own_blocks * lax.axis_size("blk")
    scales = lax.rsqrt(degree.astype(jnp.float32))[:, None]
    row_ids = tile_row.reshape(-1)
    col_ids = tile_col.reshape(-1)
    live = tile_live.reshape(1)
    slots, edges = edge_dst.shape[2:]
    scaled = jnp.dot(features, weight, precision=HIGH, preferred_element_type=jnp.float32) * scales
    cycle_rows = lax.all_gather(scaled, "blk", axis=0, tiled=True)
    tiles = build_tiles(live, edge_dst.reshape(slots, edges), edge_src.reshape(slots, edges))
    sums = aggregate(
        tiles,
        live,
        col_ids,
        row_ids,
        cycle_rows.reshape(cycle_blocks, TILE, hidden_width),
        group_blocks,
        False,
    )
    sums = sums.reshape(group_blocks * TILE, hidden_width)
    own_sums = lax.psum_scatter(sums, "rep", scatter_dimension=0, tiled=True)
    pre = (own_sums + scaled) * scales
    hidden, pull = jax.vjp(activation, pre)
    (own_grad,) = pull(cotangent)
    back_own = own_grad * scales
    back_group = lax.all_gather(back_own, "rep", axis=0, tiled=True)
    reverse = aggregate(
        tiles,
        live,
        row_ids,
        col_ids,
        back_group.reshape(group_blocks, TILE, hidden_width),
        cycle_blocks,
        True,
    )
    reverse = reverse.reshape(cycle_blocks * TILE, hidden_width)
    column_grad = lax.psum_scatter(reverse, "blk", scatter_dimension=0, tiled=True)
    grad_rows = (column_grad + back_own) * scales
    local_grad = jnp.einsum(
        "ni,nh->ih", features, grad_rows, precision=HIGH, preferred_element_type=jnp.float32
    )
    weight_grad = lax.psum(local_grad, ("blk", "rep"))
    return (hidden, weight_grad)


def solution(mesh):
    return jax.shard_map(
        local,
        mesh=mesh,
        in_specs=(
            P(("blk", "rep"), None),
            P(),
            P(("blk", "rep"), None),
            P(("blk", "rep")),
            P("blk", "rep", None),
            P("blk", "rep", None),
            P("blk", "rep", None, None),
            P("blk", "rep", None, None),
            P("blk", "rep"),
        ),
        out_specs=(P(("blk", "rep"), None), P()),
        check_vma=False,
    )
```

time: 876 us -> 484 us (0.55)
  matrix products: 252 us -> 6.61 us
  waiting for transfers between devices: 537 us -> 404 us
  Pallas kernels: 0 us -> 52.8 us
  local copies, waits for them, and re-layouts: 51 us -> 2.35 us
  loops' own time: 14 us -> 0 us
    dot_general x38 -> x0, matrix products: 245 us -> none  [the longest x10 74.5 us: one_block(): jnp.einsum('tb,bjh->tjh', pick_table, source, precision=HIGH, preferred_e...]
    reduce_scatter x1, waiting for transfers between devices: 156 us -> 79.7 us  [local(): own_sums = lax.psum_scatter(sums, 'rep', scatter_dimension=0, tiled=True)]
    reduce_scatter x1, waiting for transfers between devices: 151 us -> 75.1 us  [local(): lax.psum_scatter(reverse, 'blk', scatter_dimension=0, tiled=True)]
    pallas_call x0 -> x3, Pallas kernels: none -> 52.8 us  [the longest x2 43.9 us: aggregate(): pl.pallas_call(partial(aggregate_kernel, transpose), grid_spec=pltpu.Pref...]
    while x52 -> x0, local copies, waits for them, and re-layouts: 35.5 us -> none
    all_gather x1, waiting for transfers between devices: 18.2 us -> 36.6 us  [local(): cycle_rows = lax.all_gather(scaled, 'blk', axis=0, tiled=True)]
    another operation x3 -> x0, loops' own time: 14 us -> none  [the longest x2 14 us: aggregate(): return lax.fori_loop(0, step_count, one_block, start_totals)]
  transfers between devices with their start and end apart: 5 -> 5, of which waited for: 5 -> 5; matrix products, arithmetic and copies ran while one was open for 3% -> 0% of each run, Pallas kernels for 0% -> 2%
where the time goes in v1:
time: 484 us
  waiting for transfers between devices  404 us (83%)
  Pallas kernels  52.8 us (11%)
  between operations  14.4 us (3%)
  matrix products  6.61 us (1%)
    psum x1, waiting for transfers between devices, local(): weight_grad = lax.psum(local_grad, ('blk', 'rep'))  149 us
    reduce_scatter x1, waiting for transfers between devices, local(): own_sums = lax.psum_scatter(sums, 'rep', scatter_dimension=0, tiled=True)  79.7 us
    reduce_scatter x1, waiting for transfers between devices, local(): lax.psum_scatter(reverse, 'blk', scatter_dimension=0, tiled=True)  75.1 us
    all_gather x1, waiting for transfers between devices, local(): back_group = lax.all_gather(back_own, 'rep', axis=0, tiled=True)  63.6 us
    pallas_call x2, Pallas kernels, aggregate(): pl.pallas_call(partial(aggregate_kernel, transpose), grid_spec=pltpu.Pref...  43.9 us
    all_gather x1, waiting for transfers between devices, local(): cycle_rows = lax.all_gather(scaled, 'blk', axis=0, tiled=True)  36.6 us
  transfers between devices with their start and end apart: 5, of which 5 were waited for; matrix products, arithmetic and copies ran while one was open for 0% of the time, Pallas kernels for 2%

profile of v1, /device:TPU:1, one launch (start us, length us, event | category | flops | bytes accessed | tf_op | source)
XLA Modules:
  0.0 483.6 jit_solution(14824685614903221645)
XLA Ops:
  7.2 0.0 all-gather.3.cloned.1.call-start
  7.2 0.8 convert_rsqrt_fusion
  8.0 0.4 copy-done
  8.4 3.6 convolution_multiply_fusion
  11.9 0.0 all-gather.3.cloned.1.call-update
  12.0 0.0 reduce-scatter.3.cloned.1.call-start
  12.6 8.9 %shard_map.104.tiles_ref = bf16[256,128,128]{2,1,0:T(8,128)(2,1)} custom-call(s32[1]{0:T(128)} %bitcast.14.live_ref, s32[256,256]{1,0:T(8,128)} %bitcast.21, s32[256,256]{1,0:T(8,128)} %bitcast.22), custom_call_target="tpu_custom_call" | custom-call | flops 2147483648 | bytes 10000000 | tf_op jit(solution)/shard_map/pallas_call | solution.py:33
  21.5 36.6 %all-gather.3.cloned.1.call-done = f32[6144,256]{1,0:T(8,128)} async-done(((f32[384,256]{1,0:T(8,128)}), f32[6144,256]{1,0:T(8,128)}) %all-gather.3.cloned.1.call-update) | async-done | bytes 6291472 | tf_op jit(solution)/shard_map/all_gather | solution.py:125
  58.1 21.4 %shard_map.105 = f32[24,128,256]{2,1,0:T(8,128)} custom-call(s32[1]{0:T(128)} %bitcast.15.live_ref, s32[256]{0:T(256)} %bitcast.23, s32[256]{0:T(256)} %bitcast.25, bf16[256,128,128]{2,1,0:T(8,128)(2,1)} %shard_map.104.tiles_ref, f32[48,128,256]{2,1,0:T(8,128)} %bitcast.19), custom_call_target="tpu_custom_call" | custom-call | flops 4294967296 | bytes 20000000 | tf_op jit(solution)/shard_map/pallas_call | solution.py:93
  79.5 0.0 reduce-scatter.3.cloned.1.call-update
  79.5 0.0 all-gather.5.cloned.1.call-start
  79.6 79.7 %reduce-scatter.3.cloned.1.call-done = f32[384,256]{1,0:T(8,128)} async-done(((f32[3072,256]{1,0:T(8,128)}), f32[384,256]{1,0:T(8,128)}) %reduce-scatter.3.cloned.1.call-update) | async-done | bytes 393232 | tf_op jit(solution)/shard_map/reduce_scatter | solution.py:137
  159.3 2.2 fusion.6
  161.5 0.0 all-gather.5.cloned.1.call-update
  161.5 0.0 reduce-scatter.5.cloned.1.call-start
  161.6 63.6 %all-gather.5.cloned.1.call-done = f32[3072,256]{1,0:T(8,128)} async-done(((f32[384,256]{1,0:T(8,128)}), f32[3072,256]{1,0:T(8,128)}) %all-gather.5.cloned.1.call-update) | async-done | bytes 3145744 | tf_op jit(solution)/shard_map/all_gather | solution.py:142
  225.2 22.5 %shard_map.106 = f32[48,128,256]{2,1,0:T(8,128)} custom-call(s32[1]{0:T(128)} %bitcast.16.live_ref, s32[256]{0:T(256)} %bitcast.26, s32[256]{0:T(256)} %bitcast.24, bf16[256,128,128]{2,1,0:T(8,128)(2,1)} %shard_map.104.tiles_ref, f32[24,128,256]{2,1,0:T(8,128)} %bitcast.20), custom_call_target="tpu_custom_call" | custom-call | flops 4294967296 | bytes 20000000 | tf_op jit(solution)/shard_map/pallas_call | solution.py:93
  247.6 0.0 reduce-scatter.5.cloned.1.call-update
  247.7 0.0 all-reduce.2.cloned.1.call-start
  247.7 75.1 %reduce-scatter.5.cloned.1.call-done = f32[384,256]{1,0:T(8,128)} async-done(((f32[6144,256]{1,0:T(8,128)}), f32[384,256]{1,0:T(8,128)}) %reduce-scatter.5.cloned.1.call-update) | async-done | bytes 393232 | tf_op jit(solution)/shard_map/reduce_scatter | solution.py:153
  322.8 3.1 convolution_bitcast_fusion
  325.9 0.0 all-reduce.2.cloned.1.call-update
  325.9 149.3 %all-reduce.2.cloned.1.call-done = f32[602,256]{1,0:T(8,128)} async-done(((f32[602,256]{1,0:T(8,128)}), f32[602,256]{1,0:T(8,128)}) %all-reduce.2.cloned.1.call-update) | async-done | bytes 616464 | tf_op jit(solution)/shard_map/psum | solution.py:158
  475.2 1.9 copy.13
  (7 shorter events, 0.0 us)
Async XLA Ops:
  7.2 1.2 copy-start
  7.2 50.9 %all-gather.3.cloned.1.call-start = ((), (), s32[]{:S(2)}) async-start(), calls=%async_computation.2 | async-start | bytes 6684672 | tf_op jit(solution)/shard_map/all_gather | solution.py:125
  12.0 147.3 %reduce-scatter.3.cloned.1.call-start = ((), (), s32[]{:S(2)}) async-start(), calls=%async_computation.3 | async-start | bytes 3538944 | tf_op jit(solution)/shard_map/reduce_scatter | solution.py:137
  58.1 101.2 %copy-start.1 = (f32[384,256]{1,0:T(8,128)S(1)}, f32[384,256]{1,0:T(8,128)}, u32[]{:S(2)}) copy-start(f32[384,256]{1,0:T(8,128)} %convolution_multiply_fusion) | copy-start | bytes 1179652
  58.1 101.2 %copy-start.3 = (f32[384,256]{1,0:T(8,128)S(1)}, f32[384,256]{1,0:T(8,128)}, u32[]{:S(2)}) copy-start(f32[384,256]{1,0:T(8,128)} %param.11) | copy-start | bytes 1179652
  79.5 145.6 %all-gather.5.cloned.1.call-start = ((), (), s32[]{:S(2)}) async-start(), calls=%async_computation.4 | async-start | bytes 3538944 | tf_op jit(solution)/shard_map/all_gather | solution.py:142
  161.5 161.3 %reduce-scatter.5.cloned.1.call-start = ((), (), s32[]{:S(2)}) async-start(), calls=%async_computation.5 | async-start | bytes 6684672 | tf_op jit(solution)/shard_map/reduce_scatter | solution.py:153
  247.6 75.2 %copy-start.2 = (f32[384,256]{1,0:T(8,128)S(1)}, f32[384,256]{1,0:T(8,128)}, u32[]{:S(2)}) copy-start(f32[384,256]{1,0:T(8,128)} %get-tuple-element.2) | copy-start | bytes 1179652
  247.7 227.5 %all-reduce.2.cloned.1.call-start = ((), (), s32[]{:S(2)}) async-start(), calls=%async_computation.6 | async-start | bytes 1245184 | tf_op jit(solution)/shard_map/psum | solution.py:158
Sparse Core Ops, SparseCore 0:
  12.1 45.9 all-gather.2
  79.7 79.5 reduce-scatter.2
  162.4 62.6 all-gather.4
  247.8 75.0 reduce-scatter.4
  328.7 146.4 all-reduce.1

commit v2 on v1

v2 whole, which is shorter than its diff:
```python
from functools import partial

import jax
import jax.numpy as jnp
from jax import lax
from jax.experimental import pallas as pl
from jax.experimental.pallas import tpu as pltpu
from jax.sharding import Mesh
from jax.sharding import PartitionSpec as P

TILE = 128
HIGH = lax.Precision.HIGHEST
activation = partial(jax.nn.gelu, approximate=True)
CHUNK = 32
UNROLL = 4
VMEM_LIMIT = 60 * 1024 * 1024
BLK = ("x", "zl", "core")
REP = ("y", "zh")


def tile_kernel(live_ref, dst_ref, src_ref, out_ref):
    first = pl.program_id(0) * CHUNK
    node_ids = lax.broadcasted_iota(jnp.int32, (TILE, dst_ref.shape[1]), 0)
    for t in range(CHUNK):
        dst_ids = jnp.where(first + t < live_ref[0], dst_ref[t : t + 1, :], TILE)
        dst_hot = (dst_ids == node_ids).astype(jnp.bfloat16)
        src_hot = (src_ref[t : t + 1, :] == node_ids).astype(jnp.bfloat16)
        counts = lax.dot_general(
            dst_hot, src_hot, (((1,), (1,)), ((), ())), preferred_element_type=jnp.float32
        )
        out_ref[t] = counts.astype(jnp.bfloat16)


def build_tiles(live, edge_dst, edge_src):
    slots, edges = edge_dst.shape
    return pl.pallas_call(
        tile_kernel,
        grid_spec=pltpu.PrefetchScalarGridSpec(
            num_scalar_prefetch=1,
            grid=(slots // CHUNK,),
            in_specs=[pl.BlockSpec((CHUNK, edges), lambda g, live: (g, 0))] * 2,
            out_specs=pl.BlockSpec((CHUNK, TILE, TILE), lambda g, live: (g, 0, 0)),
        ),
        out_shape=jax.ShapeDtypeStruct((slots, TILE, TILE), jnp.bfloat16),
        compiler_params=pltpu.CompilerParams(vmem_limit_bytes=VMEM_LIMIT),
        cost_estimate=pl.CostEstimate(
            flops=2 * slots * TILE * TILE * edges, bytes_accessed=10**7, transcendentals=0
        ),
    )(live, edge_dst, edge_src)


def aggregate_kernel(transpose, parts, targets, live_ref, pick_ref, place_ref, tiles_ref, *refs):
    sources, outs = refs[:parts], refs[parts : parts + targets]
    split, totals, sems = refs[parts + targets :]
    step = pl.program_id(0)
    first = step * CHUNK

    @pl.when(step == 0)
    def _():
        totals[...] = jnp.zeros_like(totals)

        for p, source_ref in enumerate(sources):
            count = source_ref.shape[0]

            def split_block(b, carry):
                value = source_ref[b]
                high = value.astype(jnp.bfloat16)
                split[p * count + b, :TILE] = high
                split[p * count + b, TILE:] = (value - high.astype(jnp.float32)).astype(jnp.bfloat16)
                return carry

            lax.fori_loop(0, count, split_block, 0)

    left = jnp.clip(live_ref[0] - first, 0, CHUNK)

    def some_tiles(group, carry):
        products = []
        for k in range(UNROLL):
            t = group * UNROLL + k
            tile = tiles_ref[t]
            picked = split[pick_ref[first + t]]
            twice = jnp.concatenate([tile, tile], axis=0 if transpose else 1)
            products.append(
                lax.dot_general(
                    twice,
                    picked,
                    (((0 if transpose else 1,), (0,)), ((), ())),
                    preferred_element_type=jnp.float32,
                )
            )
        for k in range(UNROLL):
            totals[place_ref[first + group * UNROLL + k]] += products[k]
        return carry

    lax.fori_loop(0, (left + UNROLL - 1) // UNROLL, some_tiles, 0)

    @pl.when(step == pl.num_programs(0) - 1)
    def _():
        copies = []
        for p, out_ref in enumerate(outs):
            count = out_ref.shape[0]
            copy = pltpu.make_async_copy(totals.at[pl.ds(p * count, count)], out_ref, sems.at[p])
            copy.start()
            copies.append(copy)
        for copy in copies:
            copy.wait()


def aggregate(tiles, live, pick_ids, place_ids, sources, target_blocks, transpose):
    slots = tiles.shape[0]
    source_blocks, _, width = sources[0].shape
    parts, targets = len(sources), len(target_blocks)
    return pl.pallas_call(
        partial(aggregate_kernel, transpose, parts, targets),
        grid_spec=pltpu.PrefetchScalarGridSpec(
            num_scalar_prefetch=3,
            grid=(slots // CHUNK,),
            in_specs=[pl.BlockSpec((CHUNK, TILE, TILE), lambda g, *_: (g, 0, 0))]
            + [pl.BlockSpec((source_blocks, TILE, width), lambda g, *_: (0, 0, 0))] * parts,
            out_specs=[pl.BlockSpec(memory_space=pl.ANY)] * targets,
            scratch_shapes=[
                pltpu.VMEM((parts * source_blocks, 2 * TILE, width), jnp.bfloat16),
                pltpu.VMEM((sum(target_blocks), TILE, width), jnp.float32),
                pltpu.SemaphoreType.DMA((targets,)),
            ],
        ),
        out_shape=[jax.ShapeDtypeStruct((b, TILE, width), jnp.float32) for b in target_blocks],
        compiler_params=pltpu.CompilerParams(vmem_limit_bytes=VMEM_LIMIT),
        cost_estimate=pl.CostEstimate(
            flops=4 * slots * TILE * TILE * width, bytes_accessed=2 * 10**7, transcendentals=0
        ),
    )(live, pick_ids, place_ids, tiles, *sources)


def exchange(value, axes):
    return lax.all_to_all(value, axes, 0, 0, tiled=True)


def gather(value, axes):
    return exchange(jnp.broadcast_to(value, (lax.axis_size(axes),) + value.shape), axes)


def swap_cores(value):
    return lax.ppermute(value, "core", [(0, 1), (1, 0)])


def sum_everywhere(value):
    rows, width = value.shape
    parts = lax.axis_size(BLK)
    part_rows = -(-rows // (8 * parts)) * 8
    value = jnp.pad(value, ((0, part_rows * parts - rows), (0, 0)))
    own = exchange(value.reshape(parts, part_rows, width), BLK).sum(0)
    own = gather(own, REP).sum(0)
    return gather(own, BLK).reshape(-1, width)[:rows]


def local(features, weight, cotangent, degree, tile_row, tile_col, edge_dst, edge_src, tile_live):
    own_rows = features.shape[0]
    hidden_width = weight.shape[1]
    own_blocks = own_rows // TILE
    group_blocks = own_blocks * lax.axis_size(REP)
    half_blocks = own_blocks * lax.axis_size(("x", "zl"))
    scales = lax.rsqrt(degree.astype(jnp.float32))[:, None]
    row_ids = tile_row.reshape(-1)
    owner, within = tile_col.reshape(-1) // own_blocks, tile_col.reshape(-1) % own_blocks
    col_ids = (owner % 2 ^ lax.axis_index("core")) * half_blocks + owner // 2 * own_blocks + within
    live = tile_live.reshape(1)
    slots, edges = edge_dst.shape[2:]
    blocks = (-1, TILE, hidden_width)
    scaled = jnp.dot(features, weight, precision=HIGH, preferred_element_type=jnp.float32) * scales
    near = gather(scaled, ("x", "zl"))
    far = swap_cores(near)
    tiles = build_tiles(live, edge_dst.reshape(slots, edges), edge_src.reshape(slots, edges))
    (sums,) = aggregate(
        tiles, live, col_ids, row_ids, [near.reshape(blocks), far.reshape(blocks)], [group_blocks], False
    )
    own_sums = exchange(sums.reshape(-1, own_rows, hidden_width), REP).sum(0)
    pre = (own_sums + scaled) * scales
    hidden, pull = jax.vjp(activation, pre)
    (own_grad,) = pull(cotangent)
    back_own = own_grad * scales
    back_group = gather(back_own, REP)
    near, far = aggregate(
        tiles, live, row_ids, col_ids, [back_group.reshape(blocks)], [half_blocks] * 2, True
    )
    near = near + swap_cores(far)
    column_grad = exchange(near.reshape(-1, own_rows, hidden_width), ("x", "zl")).sum(0)
    grad_rows = (column_grad + back_own) * scales
    local_grad = jnp.einsum(
        "ni,nh->ih", features, grad_rows, precision=HIGH, preferred_element_type=jnp.float32
    )
    return (hidden, sum_everywhere(local_grad))


def solution(mesh):
    mesh = Mesh(mesh.devices.reshape(4, 2, 2, 4, 2), BLK + REP)
    nodes = P(BLK + REP)
    tile = P(BLK, REP)
    return jax.shard_map(
        local,
        mesh=mesh,
        in_specs=(nodes, P(), nodes, nodes, tile, tile, tile, tile, tile),
        out_specs=(nodes, P()),
        check_vma=False,
    )
```

time: 484 us -> 294 us (0.61)
  waiting for transfers between devices: 404 us -> 5.5 us
  blocking collectives: 0 us -> 223 us
  Pallas kernels: 52.8 us -> 38.1 us
  between operations: 14.4 us -> 1.41 us
  starting transfers between devices: 0.21 us -> 9.06 us
  other arithmetic: 3 us -> 9.54 us
    all_to_all x0 -> x7, blocking collectives: none -> 223 us  [exchange(): return lax.all_to_all(value, axes, 0, 0, tiled=True)]
    reduce_scatter x2 -> x0, waiting for transfers between devices: 155 us -> none  [the longest x1 79.7 us: local(): own_sums = lax.psum_scatter(sums, 'rep', scatter_dimension=0, tiled=True)]
    psum x1 -> x0, waiting for transfers between devices: 149 us -> none  [local(): weight_grad = lax.psum(local_grad, ('blk', 'rep'))]
    all_gather x2 -> x0, waiting for transfers between devices: 100 us -> none  [the longest x1 63.6 us: local(): back_group = lax.all_gather(back_own, 'rep', axis=0, tiled=True)]
    pallas_call x2, Pallas kernels: 43.9 us -> 29.2 us  [aggregate(): pl.pallas_call(partial(aggregate_kernel, transpose, parts, targets), grid...]
    ppermute x0 -> x2, starting transfers between devices: none -> 9.06 us  [swap_cores(): return lax.ppermute(value, 'core', [(0, 1), (1, 0)])]
    ppermute x0 -> x2, waiting for transfers between devices: none -> 5.5 us  [swap_cores(): return lax.ppermute(value, 'core', [(0, 1), (1, 0)])]
  transfers between devices with their start and end apart: 5 -> 2, of which waited for: 5 -> 1; matrix products, arithmetic and copies ran while one was open for 0% -> 0% of each run, Pallas kernels for 2% -> 3%
where the time goes in v2:
time: 294 us; the launch traced here: 293 us
  blocking collectives  223 us (76%)
  Pallas kernels  38.1 us (13%)
  other arithmetic  9.54 us (3%)
  starting transfers between devices  9.06 us (3%)
  waiting for transfers between devices  5.5 us (2%)
  matrix products  4.06 us (1%)
    all_to_all x7, blocking collectives, exchange(): return lax.all_to_all(value, axes, 0, 0, tiled=True)  223 us
    pallas_call x2, Pallas kernels, aggregate(): pl.pallas_call(partial(aggregate_kernel, transpose, parts, targets), grid...  29.2 us
    ppermute x2, starting transfers between devices, swap_cores(): return lax.ppermute(value, 'core', [(0, 1), (1, 0)])  9.06 us
    pallas_call x1, Pallas kernels, build_tiles(): pl.pallas_call(tile_kernel, grid_spec=pltpu.PrefetchScalarGridSpec(num_sc...  8.85 us
  transfers between devices with their start and end apart: 2, of which 1 were waited for; matrix products, arithmetic and copies ran while one was open for 0% of the time, Pallas kernels for 3%

profile of v2, /device:TPU:1, one launch (start us, length us, event | category | flops | bytes accessed | tf_op | source)
XLA Modules:
  0.0 292.6 jit_solution(7453483082153308946)
XLA Ops:
  0.6 0.8 convert_rsqrt_fusion
  1.4 0.4 copy-done
  1.8 2.8 convolution_multiply_fusion
  4.9 43.2 %all_to_all.35 = f32[8,384,256]{2,1,0:T(8,128)} all-to-all(f32[8,384,256]{2,1,0:T(8,128)S(1)} %broadcast_in_dim.13), channel_id=1, replica_groups=mesh['x'=4,'zl'=2,'core'=2,'y'=4,'zh'=2] {'x','zl'}, dimensions={0} | all-to-all | bytes 6291456 | tf_op jit(solution)/shard_map/all_to_all | solution.py:136
  48.1 1.9 collective-permute-start
  50.7 8.8 %shard_map.104.tiles_ref = bf16[256,128,128]{2,1,0:T(8,128)(2,1)} custom-call(s32[1]{0:T(128)} %bitcast.18.live_ref, s32[256,256]{1,0:T(8,128)} %bitcast.26, s32[256,256]{1,0:T(8,128)} %bitcast.27), custom_call_target="tpu_custom_call" | custom-call | flops 2147483648 | bytes 10000000 | tf_op jit(solution)/shard_map/pallas_call | solution.py:36
  59.5 0.6 fusion.11.pick_ref.place_ref
  60.1 14.5 %shard_map.105 = f32[24,128,256]{2,1,0:T(8,128)} custom-call(s32[1]{0:T(128)} %bitcast.19.live_ref, s32[256]{0:T(256)} %fusion.11.pick_ref.place_ref, s32[256]{0:T(256)} %bitcast.30, bf16[256,128,128]{2,1,0:T(8,128)(2,1)} %shard_map.104.tiles_ref, f32[24,128,256]{2,1,0:T(8,128)} %bitcast.6.refs_0_, f32[24,128,256]{2,1,0:T(8,128)} %bitcast.7.refs_1_), custom_call_target="tpu_custom_call" | custom-call | flops 4294967296 | bytes 20000000 | tf_op jit(solution)/shard_map/pallas_call | solution.py:113
  74.7 50.6 %all_to_all.36 = f32[8,384,256]{2,1,0:T(8,128)} all-to-all(f32[8,384,256]{2,1,0:T(8,128)} %bitcast.22), channel_id=1, replica_groups=mesh['x'=4,'zl'=2,'core'=2,'y'=4,'zh'=2] {'y','zh'}, dimensions={0} | all-to-all | bytes 6291456 | tf_op jit(solution)/shard_map/all_to_all | solution.py:136
  125.2 2.2 reduce_sum.36
  127.4 1.1 fusion.6
  128.5 0.3 broadcast_in_dim.14
  128.8 40.7 %all_to_all.37 = f32[8,384,256]{2,1,0:T(8,128)} all-to-all(f32[8,384,256]{2,1,0:T(8,128)S(1)} %broadcast_in_dim.14), channel_id=1, replica_groups=mesh['x'=4,'zl'=2,'core'=2,'y'=4,'zh'=2] {'y','zh'}, dimensions={0} | all-to-all | bytes 6291456 | tf_op jit(solution)/shard_map/all_to_all | solution.py:136
  169.5 14.7 %shard_map.106 = (f32[24,128,256]{2,1,0:T(8,128)}, f32[24,128,256]{2,1,0:T(8,128)}) custom-call(s32[1]{0:T(128)} %bitcast.20.live_ref, s32[256]{0:T(256)} %bitcast.31, s32[256]{0:T(256)} %fusion.11.pick_ref.place_ref, bf16[256,128,128]{2,1,0:T(8,128)(2,1)} %shard_map.104.tiles_ref, f32[24,128,256]{2,1,0:T(8,128)} %bitcast.23), custom_call_target="tpu_custom_call" | custom-call | flops 4294967296 | bytes 20000000 | tf_op jit(solution)/shard_map/pallas_call | solution.py:113
  184.2 7.2 %collective-permute-start.1 = (f32[24,128,256]{2,1,0:T(8,128)}, f32[24,128,256]{2,1,0:T(8,128)S(1)}, u32[]{:S(2)}, u32[]{:S(2)}) collective-permute-start(f32[24,128,256]{2,1,0:T(8,128)} %get-tuple-element.5), channel_id=1, source_target_pairs={{0,8},{8,0},{1,9},{9,1},{2,10},{10,2},{3,11},{11,3},{4,12},{12,4},... | collective-permute-start | bytes 9437192 | tf_op jit(solution)/shard_map/ppermute | solution.py:144
  191.4 5.5 %collective-permute-done.1 = f32[24,128,256]{2,1,0:T(8,128)S(1)} collective-permute-done((f32[24,128,256]{2,1,0:T(8,128)}, f32[24,128,256]{2,1,0:T(8,128)S(1)}, u32[]{:S(2)}, u32[]{:S(2)}) %collective-permute-start.1) | collective-permute-done | bytes 3145760 | tf_op jit(solution)/shard_map/ppermute | solution.py:144
  196.9 2.6 add.43
  199.6 41.3 %all_to_all.38 = f32[8,384,256]{2,1,0:T(8,128)} all-to-all(f32[8,384,256]{2,1,0:T(8,128)S(1)} %bitcast.21), channel_id=1, replica_groups=mesh['x'=4,'zl'=2,'core'=2,'y'=4,'zh'=2] {'x','zl'}, dimensions={0} | all-to-all | bytes 6291456 | tf_op jit(solution)/shard_map/all_to_all | solution.py:136
  240.9 2.1 reduce_sum.37
  243.1 1.2 convolution_bitcast_fusion
  244.4 17.0 %all_to_all.39 = f32[16,40,256]{2,1,0:T(8,128)S(1)} all-to-all(f32[16,40,256]{2,1,0:T(8,128)S(1)} %bitcast.24), channel_id=1, replica_groups=mesh['x'=4,'zl'=2,'core'=2,'y'=4,'zh'=2] {'x','zl','core'}, dimensions={0} | all-to-all | bytes 1310720 | tf_op jit(solution)/shard_map/all_to_all | solution.py:136
  261.4 14.1 %all_to_all.40 = f32[8,40,256]{2,1,0:T(8,128)S(1)} all-to-all(f32[8,40,256]{2,1,0:T(8,128)S(1)} %broadcast_in_dim.15), channel_id=1, replica_groups=mesh['x'=4,'zl'=2,'core'=2,'y'=4,'zh'=2] {'y','zh'}, dimensions={0} | all-to-all | bytes 655360 | tf_op jit(solution)/shard_map/all_to_all | solution.py:136
  275.6 16.1 %all_to_all.41 = f32[16,40,256]{2,1,0:T(8,128)S(1)} all-to-all(f32[16,40,256]{2,1,0:T(8,128)S(1)} %broadcast_in_dim.16), channel_id=1, replica_groups=mesh['x'=4,'zl'=2,'core'=2,'y'=4,'zh'=2] {'x','zl','core'}, dimensions={0} | all-to-all | bytes 1310720 | tf_op jit(solution)/shard_map/all_to_all | solution.py:136
  291.7 0.9 slice.4
  (14 shorter events, 0.5 us)
Async XLA Ops:
  0.6 1.2 copy-start
  4.9 45.7 %copy-start.2 = (s32[1,1,256]{2,1,0:T(1,128)S(1)}, s32[1,1,256]{2,1,0:T(1,128)}, u32[]{:S(2)}) copy-start(s32[1,1,256]{2,1,0:T(1,128)} %param.14) | copy-start | bytes 3076
  48.1 12.0 %collective-permute-start = (f32[8,384,256]{2,1,0:T(8,128)}, f32[8,384,256]{2,1,0:T(8,128)}, u32[]{:S(2)}, u32[]{:S(2)}) collective-permute-start(f32[8,384,256]{2,1,0:T(8,128)} %all_to_all.35), channel_id=1, source_target_pairs={{0,8},{8,0},{1,9},{9,1},{2,10},{10,2},{3,11},{11,3},{4,12},{12,4},... | collective-permute-start | bytes 9437192 | tf_op jit(solution)/shard_map/ppermute | solution.py:144
  125.2 2.2 copy-start.1
  184.2 12.7 %collective-permute-start.1 = (f32[24,128,256]{2,1,0:T(8,128)}, f32[24,128,256]{2,1,0:T(8,128)S(1)}, u32[]{:S(2)}, u32[]{:S(2)}) collective-permute-start(f32[24,128,256]{2,1,0:T(8,128)} %get-tuple-element.5), channel_id=1, source_target_pairs={{0,8},{8,0},{1,9},{9,1},{2,10},{10,2},{3,11},{11,3},{4,12},{12,4},... | collective-permute-start | bytes 9437192 | tf_op jit(solution)/shard_map/ppermute | solution.py:144

commit v3 on v2

v3 whole, which is shorter than its diff:
```python
from functools import partial

import jax
import jax.numpy as jnp
from jax import lax
from jax.experimental import pallas as pl
from jax.experimental.pallas import tpu as pltpu
from jax.sharding import Mesh
from jax.sharding import PartitionSpec as P

TILE = 128
HIGH = lax.Precision.HIGHEST
activation = partial(jax.nn.gelu, approximate=True)
ROWS = 8
UNROLL = 4
VMEM_LIMIT = 24 * 1024 * 1024
BLK = ("x", "zl", "core")
REP = ("y", "zh")


def in_vmem(value):
    return pltpu.with_memory_space_constraint(value, pltpu.VMEM)


SMEM = pl.BlockSpec(memory_space=pltpu.SMEM)
VMEM = pl.BlockSpec(memory_space=pltpu.VMEM)


def tile_kernel(live_ref, dst_ref, src_ref, out_ref):
    live = live_ref[0]
    node_ids = lax.broadcasted_iota(jnp.int32, (TILE, dst_ref.shape[1]), 0)

    def some_slots(group, carry):
        first = pl.multiple_of(group * ROWS, ROWS)
        dst = dst_ref[pl.ds(first, ROWS)]
        src = src_ref[pl.ds(first, ROWS)]
        for k in range(ROWS):
            dst_ids = jnp.where(first + k < live, dst[k : k + 1], TILE)
            dst_hot = (dst_ids == node_ids).astype(jnp.bfloat16)
            src_hot = (src[k : k + 1] == node_ids).astype(jnp.bfloat16)
            counts = lax.dot_general(
                dst_hot, src_hot, (((1,), (1,)), ((), ())), preferred_element_type=jnp.float32
            )
            out_ref[first + k] = counts.astype(jnp.bfloat16)
        return carry

    lax.fori_loop(0, (live + ROWS - 1) // ROWS, some_slots, 0)


def build_tiles(live, edge_dst, edge_src):
    slots, edges = edge_dst.shape
    return pl.pallas_call(
        tile_kernel,
        in_specs=[SMEM, VMEM, VMEM],
        out_specs=VMEM,
        out_shape=pltpu.VMEM((slots, TILE, TILE), jnp.bfloat16),
        compiler_params=pltpu.CompilerParams(vmem_limit_bytes=VMEM_LIMIT),
        cost_estimate=pl.CostEstimate(
            flops=2 * slots * TILE * TILE * edges, bytes_accessed=10**7, transcendentals=0
        ),
    )(live, edge_dst, edge_src)


def aggregate_kernel(transpose, parts, live_ref, pick_ref, place_ref, tiles_ref, *refs):
    sources, (start_ref, out_ref, split) = refs[:parts], refs[parts:]
    out_ref[...] = jnp.zeros_like(out_ref)
    if transpose:
        out_ref[: start_ref.shape[0]] = start_ref[...]

    for p, source_ref in enumerate(sources):
        count = source_ref.shape[0]

        def split_block(b, carry):
            value = source_ref[b]
            high = value.astype(jnp.bfloat16)
            split[p * count + b, :TILE] = high
            split[p * count + b, TILE:] = (value - high.astype(jnp.float32)).astype(jnp.bfloat16)
            return carry

        lax.fori_loop(0, count, split_block, 0)

    def some_tiles(group, carry):
        first = group * UNROLL
        products = []
        for k in range(UNROLL):
            tile = tiles_ref[first + k]
            picked = split[pick_ref[first + k]]
            twice = jnp.concatenate([tile, tile], axis=0 if transpose else 1)
            products.append(
                lax.dot_general(
                    twice,
                    picked,
                    (((0 if transpose else 1,), (0,)), ((), ())),
                    preferred_element_type=jnp.float32,
                )
            )
        for k in range(UNROLL):
            out_ref[place_ref[first + k]] += products[k]
        return carry

    lax.fori_loop(0, (live_ref[0] + UNROLL - 1) // UNROLL, some_tiles, 0)


def aggregate(tiles, live, pick_ids, place_ids, sources, start, target_blocks, transpose):
    slots = tiles.shape[0]
    source_blocks, _, width = sources[0].shape
    parts = len(sources)
    return pl.pallas_call(
        partial(aggregate_kernel, transpose, parts),
        in_specs=[SMEM] * 3 + [VMEM] * (parts + 2),
        out_specs=VMEM,
        out_shape=pltpu.VMEM((target_blocks, TILE, width), jnp.float32),
        scratch_shapes=[pltpu.VMEM((parts * source_blocks, 2 * TILE, width), jnp.bfloat16)],
        compiler_params=pltpu.CompilerParams(vmem_limit_bytes=VMEM_LIMIT),
        cost_estimate=pl.CostEstimate(
            flops=4 * slots * TILE * TILE * width, bytes_accessed=2 * 10**7, transcendentals=0
        ),
    )(live, pick_ids, place_ids, in_vmem(tiles), *[in_vmem(v) for v in sources], in_vmem(start))


def gradient_kernel(*refs):
    features, (rows_ref, out_ref) = refs[:-2], refs[-2:]
    two, height, nodes = features[0].shape
    blocks = two * nodes // TILE
    width = out_ref.shape[1]
    piece = height // 2
    out_ref[...] = jnp.zeros_like(out_ref)
    for p, part_ref in enumerate(features):
        rows = rows_ref[p * blocks : (p + 1) * blocks].reshape(blocks * TILE, width)
        rows_high = rows.astype(jnp.bfloat16)
        rows_low = (rows - rows_high.astype(jnp.float32)).astype(jnp.bfloat16)
        right = jnp.concatenate([rows_high, rows_low, rows_high], axis=0)

        def one_piece(m, carry):
            at = pl.ds(pl.multiple_of(m * piece, 16), piece)
            part = jnp.concatenate([part_ref[z, at] for z in range(two)], axis=1)
            high = part.astype(jnp.bfloat16)
            low = (part - high.astype(jnp.float32)).astype(jnp.bfloat16)
            left = jnp.concatenate([high, high, low], axis=1)
            out_ref[at] += jnp.dot(left, right, preferred_element_type=jnp.float32)
            return carry

        lax.fori_loop(0, height // piece, one_piece, 0)


def gradient(features, rows, out_rows):
    width = rows.shape[2]
    return pl.pallas_call(
        gradient_kernel,
        in_specs=[VMEM] * (len(features) + 1),
        out_specs=VMEM,
        out_shape=pltpu.VMEM((out_rows, width), jnp.float32),
        compiler_params=pltpu.CompilerParams(vmem_limit_bytes=VMEM_LIMIT),
        cost_estimate=pl.CostEstimate(
            flops=6 * out_rows * rows.shape[0] * TILE * width, bytes_accessed=10**7, transcendentals=0
        ),
    )(*[in_vmem(f) for f in features], in_vmem(rows))


def exchange(value, axes):
    return lax.all_to_all(value, axes, 0, 0, tiled=True)


def gather(value, axes):
    return exchange(jnp.broadcast_to(value, (lax.axis_size(axes),) + value.shape), axes)


def swap_cores(value):
    return lax.ppermute(value, "core", [(0, 1), (1, 0)])


def sum_everywhere(value):
    rows, width = value.shape
    parts = lax.axis_size(BLK)
    part_rows = -(-rows // (8 * parts)) * 8
    value = jnp.pad(value, ((0, part_rows * parts - rows), (0, 0)))
    own = exchange(value.reshape(parts, part_rows, width), BLK).sum(0)
    own = gather(own, REP).sum(0)
    return gather(own, BLK).reshape(-1, width)[:rows]


def local(features, weight, cotangent, degree, tile_row, tile_col, edge_dst, edge_src, tile_live):
    own_rows, in_width = features.shape
    hidden_width = weight.shape[1]
    own_blocks = own_rows // TILE
    group_blocks = own_blocks * lax.axis_size(REP)
    cycle_blocks = own_blocks * lax.axis_size(BLK)
    blocks = (-1, TILE, hidden_width)
    scales = lax.rsqrt(degree.astype(jnp.float32))[:, None]
    row_ids = tile_row.reshape(-1)
    live = tile_live.reshape(1)
    slots, edges = edge_dst.shape[2:]
    owner, within = tile_col.reshape(-1) // own_blocks, tile_col.reshape(-1) % own_blocks
    other_core = owner % 2 ^ lax.axis_index("core")
    from_ids = other_core * (cycle_blocks // 2) + owner // 2 * own_blocks + within
    x_ahead = (owner // 4 - lax.axis_index("x")) % 4
    other_z = owner // 2 % 2 ^ lax.axis_index("zl")
    to_ids = ((other_core * 4 + x_ahead) * 2 + other_z) * own_blocks + within

    scaled = jnp.dot(features, weight, precision=HIGH, preferred_element_type=jnp.float32) * scales
    near = gather(scaled, ("x", "zl"))
    height = -(-in_width // 32) * 32
    turned = jnp.pad(features.T * scales.T, ((0, height - in_width), (0, 0)))
    turned, near = lax.optimization_barrier((turned, near))
    far = swap_cores(near)
    across = lax.ppermute(turned, "zl", [(0, 1), (1, 0)])
    tiles = build_tiles(live, edge_dst.reshape(slots, edges), edge_src.reshape(slots, edges))
    sums = aggregate(
        tiles, live, from_ids, row_ids, [near.reshape(blocks), far.reshape(blocks)],
        scaled.reshape(blocks), group_blocks, False,
    )
    across, sums = lax.optimization_barrier((across, sums))
    pair = jnp.stack([turned, across])
    cycle = [pair] + [
        lax.ppermute(pair, "x", [(i, (i - ahead) % 4) for i in range(4)]) for ahead in (1, 2, 3)
    ]
    own_sums = exchange(sums.reshape(-1, own_rows, hidden_width), REP).sum(0)
    pre = (own_sums + scaled) * scales
    hidden, pull = jax.vjp(activation, pre)
    (own_grad,) = pull(cotangent)
    back_own = own_grad * scales
    back_group = gather(back_own, REP)
    cycle, back_group = lax.optimization_barrier((cycle, back_group))
    cycle = cycle + [swap_cores(part) for part in cycle]
    reverse = aggregate(
        tiles, live, row_ids, to_ids, [back_group.reshape(blocks)],
        back_own.reshape(blocks), cycle_blocks, True,
    )
    cycle, reverse = lax.optimization_barrier((cycle, reverse))
    parts = lax.axis_size(BLK)
    out_rows = -(-in_width // (8 * parts)) * 8 * parts
    return (hidden, sum_everywhere(gradient(cycle, reverse, out_rows))[:in_width])


def solution(mesh):
    mesh = Mesh(mesh.devices.reshape(4, 2, 2, 4, 2), BLK + REP)
    nodes = P(BLK + REP)
    tile = P(BLK, REP)
    return jax.shard_map(
        local,
        mesh=mesh,
        in_specs=(nodes, P(), nodes, nodes, tile, tile, tile, tile, tile),
        out_specs=(nodes, P()),
        check_vma=False,
    )
```

time: 294 us -> 316 us (1.075)
  blocking collectives: 223 us -> 95.2 us
  waiting for transfers between devices: 5.5 us -> 129 us
  starting transfers between devices: 9.06 us -> 22.3 us
  Pallas kernels: 38.1 us -> 49.7 us
  local copies, waits for them, and re-layouts: 1.95 us -> 9.95 us
  other arithmetic: 9.54 us -> 5.85 us
    all_to_all x7 -> x4, blocking collectives: 223 us -> 95.2 us  [exchange(): return lax.all_to_all(value, axes, 0, 0, tiled=True)]
    ppermute x0 -> x4, waiting for transfers between devices: none -> 84 us  [the longest x3 78.8 us: local(): lax.ppermute(pair, 'x', [(i, (i - ahead) % 4) for i in range(4)])]
    all_to_all x0 -> x2, waiting for transfers between devices: none -> 44.7 us  [exchange(): return lax.all_to_all(value, axes, 0, 0, tiled=True)]
    pallas_call x3 -> x4, Pallas kernels: 38.1 us -> 49.7 us  [the longest x2 30.8 us: aggregate(): pl.pallas_call(partial(aggregate_kernel, transpose, parts), in_specs=[SME...]
    all_to_all x0 -> x2, starting transfers between devices: none -> 10.8 us  [exchange(): return lax.all_to_all(value, axes, 0, 0, tiled=True)]
    ppermute x2 -> x5, waiting for transfers between devices: 5.5 us -> 0.01 us  [swap_cores(): return lax.ppermute(value, 'core', [(0, 1), (1, 0)])]
    ppermute x0 -> x4, starting transfers between devices: none -> 5.14 us  [the longest x3 2.74 us: local(): lax.ppermute(pair, 'x', [(i, (i - ahead) % 4) for i in range(4)])]
    unnamed x6 -> x30, local copies, waits for them, and re-layouts: 0.44 us -> 5.03 us
  transfers between devices with their start and end apart: 2 -> 11, of which waited for: 1 -> 5; matrix products, arithmetic and copies ran while one was open for 0% -> 1% of each run, Pallas kernels for 3% -> 12%
where the time goes in v3:
time: 316 us
  waiting for transfers between devices  129 us (41%)
  blocking collectives  95.2 us (30%)
  Pallas kernels  49.7 us (16%)
  starting transfers between devices  22.3 us (7%)
  local copies, waits for them, and re-layouts  9.95 us (3%)
  other arithmetic  5.85 us (2%)
    all_to_all x4, blocking collectives, exchange(): return lax.all_to_all(value, axes, 0, 0, tiled=True)  95.2 us
    ppermute x3, waiting for transfers between devices, local(): lax.ppermute(pair, 'x', [(i, (i - ahead) % 4) for i in range(4)])  78.8 us
    all_to_all x2, waiting for transfers between devices, exchange(): return lax.all_to_all(value, axes, 0, 0, tiled=True)  44.7 us
    pallas_call x2, Pallas kernels, aggregate(): pl.pallas_call(partial(aggregate_kernel, transpose, parts), in_specs=[SME...  30.8 us
    pallas_call x1, Pallas kernels, gradient(): pl.pallas_call(gradient_kernel, in_specs=[VMEM] * (len(features) + 1), ou...  11.5 us
    all_to_all x2, starting transfers between devices, exchange(): return lax.all_to_all(value, axes, 0, 0, tiled=True)  10.8 us
    pallas_call x1, Pallas kernels, build_tiles(): pl.pallas_call(tile_kernel, in_specs=[SMEM, VMEM, VMEM], out_specs=VMEM,...  7.37 us
  transfers between devices with their start and end apart: 11, of which 5 were waited for; matrix products, arithmetic and copies ran while one was open for 1% of the time, Pallas kernels for 12%

profile of v3, /device:TPU:1, one launch (start us, length us, event | category | flops | bytes accessed | tf_op | source)
XLA Modules:
  0.0 316.1 jit_solution(1145780973986345032)
XLA Ops:
  1.7 2.9 convolution_multiply_fusion
  4.7 1.9 broadcast_in_dim.13
  6.6 6.3 %all-to-all-start = ((f32[8,384,256]{2,1,0:T(8,128)}), f32[8,384,256]{2,1,0:T(8,128)}, u32[]{:S(2)}, u32[]{:S(2)}) async-start(f32[8,384,256]{2,1,0:T(8,128)} %broadcast_in_dim.13), calls=%async_computation | async-start | bytes 6291456 | tf_op jit(solution)/shard_map/all_to_all | solution.py:161
  13.1 44.7 %all-to-all-done = f32[8,384,256]{2,1,0:T(8,128)} async-done(((f32[8,384,256]{2,1,0:T(8,128)}), f32[8,384,256]{2,1,0:T(8,128)}, u32[]{:S(2)}, u32[]{:S(2)}) %all-to-all-start) | async-done | bytes 3145760 | tf_op jit(solution)/shard_map/all_to_all | solution.py:161
  57.8 1.6 collective-permute-start.1
  60.1 7.4 %shard_map.104.tiles_ref = bf16[256,128,128]{2,1,0:T(8,128)(2,1)S(1)} custom-call(s32[1]{0:T(128)} %bitcast.20.live_ref, s32[256,256]{1,0:T(8,128)S(1)} %bitcast.27, s32[256,256]{1,0:T(8,128)S(1)} %bitcast.28), custom_call_target="tpu_custom_call" | custom-call | flops 2147483648 | bytes 10000000 | tf_op jit(solution)/shard_map/pallas_call | solution.py:52
  67.5 2.4 collective-permute-start
  70.0 15.5 %shard_map.105 = f32[24,128,256]{2,1,0:T(8,128)S(1)} custom-call(s32[1]{0:T(128)} %bitcast.21.live_ref, s32[256]{0:T(256)S(1)} %get-tuple-element.41.pick_ref, s32[256]{0:T(256)S(1)} %bitcast.29, bf16[256,128,128]{2,1,0:T(8,128)(2,1)S(1)} %shard_map.104.tiles_ref, f32[24,128,256]{2,1,0:T(8,128)} %bitcast.7.refs_0_, f32[24,128,256]{2,1,0:T(8,128)} %bitcast.8.refs_1_, ...), custom_call_target="tpu_custom_call" | custom-call | flops 4294967296 | bytes 20000000 | tf_op jit(solution)/shard_map/pallas_call | solution.py:108
  85.6 5.1 %collective-permute-done = f32[608,384]{1,0:T(8,128)S(1)} collective-permute-done((f32[608,384]{1,0:T(8,128)S(1)}, f32[608,384]{1,0:T(8,128)S(1)}, u32[]{:S(2)}, u32[]{:S(2)}) %collective-permute-start) | collective-permute-done | bytes 933920 | tf_op jit(solution)/shard_map/ppermute | solution.py:206
  90.7 45.5 %all_to_all.30 = f32[8,384,256]{2,1,0:T(8,128)} all-to-all(f32[8,384,256]{2,1,0:T(8,128)S(1)} %bitcast.23), channel_id=1, replica_groups=mesh['x'=4,'zl'=2,'core'=2,'y'=4,'zh'=2] {'y','zh'}, dimensions={0} | all-to-all | bytes 6291456 | tf_op jit(solution)/shard_map/all_to_all | solution.py:161
  136.2 2.2 reduce_sum.27
  139.5 2.0 broadcast_in_dim.14
  141.5 4.5 %all-to-all-start.2 = ((f32[8,384,256]{2,1,0:T(8,128)}), f32[8,384,256]{2,1,0:T(8,128)}, u32[]{:S(2)}, u32[]{:S(2)}) async-start(f32[8,384,256]{2,1,0:T(8,128)} %broadcast_in_dim.14), calls=%async_computation.2 | async-start | bytes 6291456 | tf_op jit(solution)/shard_map/all_to_all | solution.py:161
  148.2 2.1 collective-permute-start.2
  150.3 42.6 %collective-permute-done.4.refs_3_ = f32[2,608,384]{2,1,0:T(8,128)S(1)} collective-permute-done((f32[2,608,384]{2,1,0:T(8,128)S(1)}, f32[2,608,384]{2,1,0:T(8,128)S(1)}, u32[]{:S(2)}, u32[]{:S(2)}) %collective-permute-start.4) | collective-permute-done | bytes 1867808 | tf_op jit(solution)/shard_map/ppermute | solution.py:215
  193.0 33.1 %collective-permute-done.3.refs_2_ = f32[2,608,384]{2,1,0:T(8,128)S(1)} collective-permute-done((f32[2,608,384]{2,1,0:T(8,128)S(1)}, f32[2,608,384]{2,1,0:T(8,128)S(1)}, u32[]{:S(2)}, u32[]{:S(2)}) %collective-permute-start.3) | collective-permute-done | bytes 1867808 | tf_op jit(solution)/shard_map/ppermute | solution.py:215
  227.3 3.2 collective-permute-done.2.refs_1_
  230.5 4.1 %collective-permute-start.5 = (f32[2,608,384]{2,1,0:T(8,128)S(1)}, f32[2,608,384]{2,1,0:T(8,128)S(1)}, u32[]{:S(2)}, u32[]{:S(2)}) collective-permute-start(f32[2,608,384]{2,1,0:T(8,128)S(1)} %pad_maximum_fusion.refs_0_), channel_id=1, source_target_pairs={{0,8},{8,0},{1,9},{9,1},{2,10},{10,2},{3,11},{11,3},{4,12},{12,4},... | collective-permute-start | bytes 5603336 | tf_op jit(solution)/shard_map/ppermute | solution.py:169
  235.2 3.4 %copy-done.2 = bf16[256,128,128]{2,1,0:T(8,128)(2,1)S(1)} copy-done((bf16[256,128,128]{2,1,0:T(8,128)(2,1)S(1)}, bf16[256,128,128]{2,1,0:T(8,128)(2,1)}, u32[]{:S(2)}) %copy-start.2) | copy-done | bytes 8388632
  238.5 15.3 %shard_map.106.refs_8_ = f32[48,128,256]{2,1,0:T(8,128)S(1)} custom-call(s32[1]{0:T(128)} %bitcast.22.live_ref, s32[256]{0:T(256)S(1)} %bitcast.30, s32[256]{0:T(256)S(1)} %get-tuple-element.40.place_ref, bf16[256,128,128]{2,1,0:T(8,128)(2,1)S(1)} %copy-done.2, f32[24,128,256]{2,1,0:T(8,128)} %bitcast.13.refs_0_, f32[3,128,256]{2,1,0:T(8,128)S(1)} %bitcast.25), custom_call_target="tpu_custom_call" | custom-call | flops 4294967296 | bytes 20000000 | tf_op jit(solution)/shard_map/pallas_call | solution.py:108
  253.9 11.5 %shard_map.107 = f32[640,256]{1,0:T(8,128)S(1)} custom-call(f32[2,608,384]{2,1,0:T(8,128)S(1)} %pad_maximum_fusion.refs_0_, f32[2,608,384]{2,1,0:T(8,128)} %collective-permute-done.2.refs_1_, f32[2,608,384]{2,1,0:T(8,128)S(1)} %copy-done.9, f32[2,608,384]{2,1,0:T(8,128)S(1)} %copy-done.7, f32[2,608,384]{2,1,0:T(8,128)S(1)} %collective-permute-done.5.refs_4_, ...), custom_call_target="tpu_custom_call" | custom-call | flops 6039797760 | bytes 10000000 | tf_op jit(solution)/shard_map/pallas_call | solution.py:148
  265.4 17.7 %all_to_all.31 = f32[16,40,256]{2,1,0:T(8,128)S(1)} all-to-all(f32[16,40,256]{2,1,0:T(8,128)S(1)} %bitcast.26), channel_id=1, replica_groups=mesh['x'=4,'zl'=2,'core'=2,'y'=4,'zh'=2] {'x','zl','core'}, dimensions={0} | all-to-all | bytes 1310720 | tf_op jit(solution)/shard_map/all_to_all | solution.py:161
  283.1 15.9 %all_to_all.32 = f32[8,40,256]{2,1,0:T(8,128)S(1)} all-to-all(f32[8,40,256]{2,1,0:T(8,128)S(1)} %broadcast_in_dim.15), channel_id=1, replica_groups=mesh['x'=4,'zl'=2,'core'=2,'y'=4,'zh'=2] {'y','zh'}, dimensions={0} | all-to-all | bytes 655360 | tf_op jit(solution)/shard_map/all_to_all | solution.py:161
  299.1 16.1 %all_to_all.33 = f32[16,40,256]{2,1,0:T(8,128)S(1)} all-to-all(f32[16,40,256]{2,1,0:T(8,128)S(1)} %broadcast_in_dim.16), channel_id=1, replica_groups=mesh['x'=4,'zl'=2,'core'=2,'y'=4,'zh'=2] {'x','zl','core'}, dimensions={0} | all-to-all | bytes 1310720 | tf_op jit(solution)/shard_map/all_to_all | solution.py:161
  (53 shorter events, 7.5 us)
Async XLA Ops:
  6.6 6.3 %copy-start.11 = (f32[384,602]{0,1:T(8,128)S(1)}, f32[384,602]{0,1:T(8,128)}, u32[]{:S(2)}) copy-start(f32[384,602]{0,1:T(8,128)} %param.9) | copy-start | bytes 2774020
  6.6 51.2 %all-to-all-start = ((f32[8,384,256]{2,1,0:T(8,128)}), f32[8,384,256]{2,1,0:T(8,128)}, u32[]{:S(2)}, u32[]{:S(2)}) async-start(f32[8,384,256]{2,1,0:T(8,128)} %broadcast_in_dim.13), calls=%async_computation | async-start | bytes 6291456 | tf_op jit(solution)/shard_map/all_to_all | solution.py:161
  12.9 47.2 %copy-start.3 = (s32[1,1,256,256]{3,2,1,0:T(8,128)S(1)}, s32[1,1,256,256]{3,2,1,0:T(8,128)}, u32[]{:S(2)}) copy-start(s32[1,1,256,256]{3,2,1,0:T(8,128)} %param.15) | copy-start | bytes 786436
  12.9 47.2 %copy-start.4 = (s32[1,1,256,256]{3,2,1,0:T(8,128)S(1)}, s32[1,1,256,256]{3,2,1,0:T(8,128)}, u32[]{:S(2)}) copy-start(s32[1,1,256,256]{3,2,1,0:T(8,128)} %param.16) | copy-start | bytes 786436
  13.1 54.4 %copy-start.10 = (f32[608,384]{1,0:T(8,128)}, f32[608,384]{1,0:T(8,128)S(1)}, u32[]{:S(2)}) copy-start(f32[608,384]{1,0:T(8,128)S(1)} %pad.4) | copy-start | bytes 2801668
  57.8 12.2 %collective-permute-start.1 = (f32[8,384,256]{2,1,0:T(8,128)}, f32[8,384,256]{2,1,0:T(8,128)}, u32[]{:S(2)}, u32[]{:S(2)}) collective-permute-start(f32[8,384,256]{2,1,0:T(8,128)} %all-to-all-done), channel_id=1, source_target_pairs={{0,8},{8,0},{1,9},{9,1},{2,10},{10,2},{3,11},{11,3},{4,12},{12,4},... | collective-permute-start | bytes 9437192 | tf_op jit(solution)/shard_map/ppermute | solution.py:169
  60.1 9.8 %copy-start.14 = (s32[1,1,256]{2,1,0:T(1,128)S(1)}, s32[1,1,256]{2,1,0:T(1,128)}, u32[]{:S(2)}) copy-start(s32[1,1,256]{2,1,0:T(1,128)} %param.14) | copy-start | bytes 3076
  60.1 9.9 %copy-start.5 = (s32[1,1,256]{2,1,0:T(1,128)S(1)}, s32[1,1,256]{2,1,0:T(1,128)}, u32[]{:S(2)}) copy-start(s32[1,1,256]{2,1,0:T(1,128)} %param.13) | copy-start | bytes 3076
  67.5 18.0 %copy-start.1 = (bf16[256,128,128]{2,1,0:T(8,128)(2,1)}, bf16[256,128,128]{2,1,0:T(8,128)(2,1)S(1)}, u32[]{:S(2)}) copy-start(bf16[256,128,128]{2,1,0:T(8,128)(2,1)S(1)} %shard_map.104.tiles_ref) | copy-start | bytes 25165828
  67.5 23.2 %collective-permute-start = (f32[608,384]{1,0:T(8,128)S(1)}, f32[608,384]{1,0:T(8,128)S(1)}, u32[]{:S(2)}, u32[]{:S(2)}) collective-permute-start(f32[608,384]{1,0:T(8,128)S(1)} %pad.4), channel_id=1, source_target_pairs={{0,16},{16,0},{1,17},{17,1},{2,18},{18,2},{3,19},{19,3},{4,20},{20... | collective-permute-start | bytes 2801672 | tf_op jit(solution)/shard_map/ppermute | solution.py:206
  90.7 45.5 %copy-start.12 = (f32[608,384]{1,0:T(8,128)}, f32[608,384]{1,0:T(8,128)S(1)}, u32[]{:S(2)}) copy-start(f32[608,384]{1,0:T(8,128)S(1)} %collective-permute-done) | copy-start | bytes 2801668
  136.2 2.2 copy-start.13
  141.5 88.9 %all-to-all-start.2 = ((f32[8,384,256]{2,1,0:T(8,128)}), f32[8,384,256]{2,1,0:T(8,128)}, u32[]{:S(2)}, u32[]{:S(2)}) async-start(f32[8,384,256]{2,1,0:T(8,128)} %broadcast_in_dim.14), calls=%async_computation.2 | async-start | bytes 6291456 | tf_op jit(solution)/shard_map/all_to_all | solution.py:161
  147.6 45.4 %collective-permute-start.4 = (f32[2,608,384]{2,1,0:T(8,128)S(1)}, f32[2,608,384]{2,1,0:T(8,128)S(1)}, u32[]{:S(2)}, u32[]{:S(2)}) collective-permute-start(f32[2,608,384]{2,1,0:T(8,128)S(1)} %pad_maximum_fusion.refs_0_), channel_id=1, source_target_pairs={{0,32},{32,64},{64,96},{96,0},{1,33},{33,65},{65,97},{97,1},{2,34}... | collective-permute-start | bytes 5603336 | tf_op jit(solution)/shard_map/ppermute | solution.py:215
  147.7 78.4 %collective-permute-start.3 = (f32[2,608,384]{2,1,0:T(8,128)S(1)}, f32[2,608,384]{2,1,0:T(8,128)S(1)}, u32[]{:S(2)}, u32[]{:S(2)}) collective-permute-start(f32[2,608,384]{2,1,0:T(8,128)S(1)} %pad_maximum_fusion.refs_0_), channel_id=1, source_target_pairs={{0,64},{32,96},{64,0},{96,32},{1,65},{33,97},{65,1},{97,33},{2,66}... | collective-permute-start | bytes 5603336 | tf_op jit(solution)/shard_map/ppermute | solution.py:215
  148.2 82.3 %collective-permute-start.2 = (f32[2,608,384]{2,1,0:T(8,128)S(1)}, f32[2,608,384]{2,1,0:T(8,128)}, u32[]{:S(2)}, u32[]{:S(2)}) collective-permute-start(f32[2,608,384]{2,1,0:T(8,128)S(1)} %pad_maximum_fusion.refs_0_), channel_id=1, source_target_pairs={{0,96},{32,0},{64,32},{96,64},{1,97},{33,1},{65,33},{97,65},{2,98}... | collective-permute-start | bytes 5603336 | tf_op jit(solution)/shard_map/ppermute | solution.py:215
  193.0 33.1 %copy-start.6 = (f32[2,608,384]{2,1,0:T(8,128)}, f32[2,608,384]{2,1,0:T(8,128)S(1)}, u32[]{:S(2)}) copy-start(f32[2,608,384]{2,1,0:T(8,128)S(1)} %collective-permute-done.4.refs_3_) | copy-start | bytes 5603332
  230.5 23.4 %collective-permute-start.5 = (f32[2,608,384]{2,1,0:T(8,128)S(1)}, f32[2,608,384]{2,1,0:T(8,128)S(1)}, u32[]{:S(2)}, u32[]{:S(2)}) collective-permute-start(f32[2,608,384]{2,1,0:T(8,128)S(1)} %pad_maximum_fusion.refs_0_), channel_id=1, source_target_pairs={{0,8},{8,0},{1,9},{9,1},{2,10},{10,2},{3,11},{11,3},{4,12},{12,4},... | collective-permute-start | bytes 5603336 | tf_op jit(solution)/shard_map/ppermute | solution.py:169
  234.6 19.3 %collective-permute-start.6 = (f32[2,608,384]{2,1,0:T(8,128)}, f32[2,608,384]{2,1,0:T(8,128)S(1)}, u32[]{:S(2)}, u32[]{:S(2)}) collective-permute-start(f32[2,608,384]{2,1,0:T(8,128)} %collective-permute-done.2.refs_1_), channel_id=1, source_target_pairs={{0,8},{8,0},{1,9},{9,1},{2,10},{10,2},{3,11},{11,3},{4,12},{12,4},... | collective-permute-start | bytes 5603336 | tf_op jit(solution)/shard_map/ppermute | solution.py:169
  234.6 19.2 %collective-permute-start.7 = (f32[2,608,384]{2,1,0:T(8,128)}, f32[2,608,384]{2,1,0:T(8,128)S(1)}, u32[]{:S(2)}, u32[]{:S(2)}) collective-permute-start(f32[2,608,384]{2,1,0:T(8,128)} %copy-done.8), channel_id=1, source_target_pairs={{0,8},{8,0},{1,9},{9,1},{2,10},{10,2},{3,11},{11,3},{4,12},{12,4},... | collective-permute-start | bytes 5603336 | tf_op jit(solution)/shard_map/ppermute | solution.py:169
  235.1 18.8 %collective-permute-start.8 = (f32[2,608,384]{2,1,0:T(8,128)}, f32[2,608,384]{2,1,0:T(8,128)S(1)}, u32[]{:S(2)}, u32[]{:S(2)}) collective-permute-start(f32[2,608,384]{2,1,0:T(8,128)} %copy-done.6), channel_id=1, source_target_pairs={{0,8},{8,0},{1,9},{9,1},{2,10},{10,2},{3,11},{11,3},{4,12},{12,4},... | collective-permute-start | bytes 5603336 | tf_op jit(solution)/shard_map/ppermute | solution.py:169
  235.2 3.4 %copy-start.2 = (bf16[256,128,128]{2,1,0:T(8,128)(2,1)S(1)}, bf16[256,128,128]{2,1,0:T(8,128)(2,1)}, u32[]{:S(2)}) copy-start(bf16[256,128,128]{2,1,0:T(8,128)(2,1)} %copy-done.1) | copy-start | bytes 25165828
  238.5 15.4 %copy-start.7 = (f32[2,608,384]{2,1,0:T(8,128)S(1)}, f32[2,608,384]{2,1,0:T(8,128)}, u32[]{:S(2)}) copy-start(f32[2,608,384]{2,1,0:T(8,128)} %copy-done.6) | copy-start | bytes 5603332
  238.5 15.4 %copy-start.9 = (f32[2,608,384]{2,1,0:T(8,128)S(1)}, f32[2,608,384]{2,1,0:T(8,128)}, u32[]{:S(2)}) copy-start(f32[2,608,384]{2,1,0:T(8,128)} %copy-done.8) | copy-start | bytes 5603332
  (2 other events, 2.4 us)

commit v4 on v2

v4 whole, which is shorter than its diff:
```python
from functools import partial

import jax
import jax.numpy as jnp
from jax import lax
from jax.experimental import pallas as pl
from jax.experimental.pallas import tpu as pltpu
from jax.sharding import Mesh
from jax.sharding import PartitionSpec as P

TILE = 128
HIGH = lax.Precision.HIGHEST
activation = partial(jax.nn.gelu, approximate=True)
ROWS = 32
PIECE = 6
UNROLL = 32
VMEM_LIMIT = 24 * 1024 * 1024
BLK = ("x", "zl", "core")
REP = ("y", "zh")


def in_vmem(value):
    return pltpu.with_memory_space_constraint(value, pltpu.VMEM)


SMEM = pl.BlockSpec(memory_space=pltpu.SMEM)
VMEM = pl.BlockSpec(memory_space=pltpu.VMEM)


def tile_kernel(live_ref, dst_ref, src_ref, out_ref):
    live = live_ref[0]
    node_ids = lax.broadcasted_iota(jnp.int32, (TILE, dst_ref.shape[1]), 0)

    def some_slots(group, carry):
        first = pl.multiple_of(group * ROWS, ROWS)
        dst = dst_ref[pl.ds(first, ROWS)]
        src = src_ref[pl.ds(first, ROWS)]
        for k in range(ROWS):
            dst_ids = jnp.where(first + k < live, dst[k : k + 1], TILE)
            dst_hot = (dst_ids == node_ids).astype(jnp.bfloat16)
            src_hot = (src[k : k + 1] == node_ids).astype(jnp.bfloat16)
            counts = lax.dot_general(
                dst_hot, src_hot, (((1,), (1,)), ((), ())), preferred_element_type=jnp.float32
            )
            out_ref[first + k] = counts.astype(jnp.bfloat16)
        return carry

    lax.fori_loop(0, (live + ROWS - 1) // ROWS, some_slots, 0)


def build_tiles(live, edge_dst, edge_src):
    slots, edges = edge_dst.shape
    return pl.pallas_call(
        tile_kernel,
        in_specs=[SMEM, VMEM, VMEM],
        out_specs=VMEM,
        out_shape=pltpu.VMEM((slots, TILE, TILE), jnp.bfloat16),
        compiler_params=pltpu.CompilerParams(vmem_limit_bytes=VMEM_LIMIT),
        cost_estimate=pl.CostEstimate(
            flops=2 * slots * TILE * TILE * edges, bytes_accessed=10**7, transcendentals=0
        ),
    )(live, edge_dst, edge_src)


def aggregate_kernel(transpose, parts, targets, live_ref, pick_ref, place_ref, tiles_ref, *refs):
    sources, outs, (split, totals, landed, sems) = (
        refs[:parts],
        refs[parts : parts + targets],
        refs[parts + targets :],
    )
    pieces = [
        (p, b) for p, source_ref in enumerate(sources) for b in range(0, source_ref.shape[0], PIECE)
    ]
    copies = []
    for n, (p, b) in enumerate(pieces):
        copy = pltpu.make_async_copy(
            sources[p].at[pl.ds(b, PIECE)], landed.at[pl.ds(n * PIECE, PIECE)], sems.at[n]
        )
        copy.start()
        copies.append(copy)
    totals[...] = jnp.zeros_like(totals)

    for n, copy in enumerate(copies):
        copy.wait()

        def split_block(k, carry):
            value = landed[n * PIECE + k]
            high = value.astype(jnp.bfloat16)
            split[n * PIECE + k, :TILE] = high
            split[n * PIECE + k, TILE:] = (value - high.astype(jnp.float32)).astype(jnp.bfloat16)
            return carry

        lax.fori_loop(0, PIECE, split_block, 0)

    def some_tiles(group, carry):
        first = group * UNROLL
        products = []
        for k in range(UNROLL):
            tile = tiles_ref[first + k]
            picked = split[pick_ref[first + k]]
            twice = jnp.concatenate([tile, tile], axis=0 if transpose else 1)
            products.append(
                lax.dot_general(
                    twice,
                    picked,
                    (((0 if transpose else 1,), (0,)), ((), ())),
                    preferred_element_type=jnp.float32,
                )
            )
        for k in range(UNROLL):
            totals[place_ref[first + k]] += products[k]
        return carry

    lax.fori_loop(0, (live_ref[0] + UNROLL - 1) // UNROLL, some_tiles, 0)
    for p, out_ref in enumerate(outs):
        count = out_ref.shape[0]
        out_ref[...] = totals[p * count : (p + 1) * count]


def aggregate(tiles, live, pick_ids, place_ids, sources, target_blocks, transpose):
    slots = tiles.shape[0]
    source_blocks, _, width = sources[0].shape
    parts, targets = len(sources), len(target_blocks)
    return pl.pallas_call(
        partial(aggregate_kernel, transpose, parts, targets),
        in_specs=[SMEM] * 3 + [VMEM] + [pl.BlockSpec(memory_space=pl.ANY)] * parts,
        out_specs=[VMEM] * targets,
        out_shape=[pltpu.VMEM((b, TILE, width), jnp.float32) for b in target_blocks],
        scratch_shapes=[
            pltpu.VMEM((parts * source_blocks, 2 * TILE, width), jnp.bfloat16),
            pltpu.VMEM((sum(target_blocks), TILE, width), jnp.float32),
            pltpu.VMEM((parts * source_blocks, TILE, width), jnp.float32),
            pltpu.SemaphoreType.DMA((parts * source_blocks // PIECE,)),
        ],
        compiler_params=pltpu.CompilerParams(vmem_limit_bytes=VMEM_LIMIT),
        cost_estimate=pl.CostEstimate(
            flops=4 * slots * TILE * TILE * width, bytes_accessed=2 * 10**7, transcendentals=0
        ),
    )(live, pick_ids, place_ids, in_vmem(tiles), *sources)


def exchange(value, axes):
    return lax.all_to_all(value, axes, 0, 0, tiled=True)


def gather(value, axes):
    return exchange(jnp.broadcast_to(value, (lax.axis_size(axes),) + value.shape), axes)


def swap_cores(value):
    return lax.ppermute(value, "core", [(0, 1), (1, 0)])


def sum_everywhere(value):
    rows, width = value.shape
    parts = lax.axis_size(BLK)
    part_rows = -(-rows // (8 * parts)) * 8
    value = jnp.pad(value, ((0, part_rows * parts - rows), (0, 0)))
    own = exchange(value.reshape(parts, part_rows, width), BLK).sum(0)
    own = gather(own, REP).sum(0)
    return gather(own, BLK).reshape(-1, width)[:rows]


def local(features, weight, cotangent, degree, tile_row, tile_col, edge_dst, edge_src, tile_live):
    own_rows = features.shape[0]
    hidden_width = weight.shape[1]
    own_blocks = own_rows // TILE
    group_blocks = own_blocks * lax.axis_size(REP)
    half_blocks = own_blocks * lax.axis_size(("x", "zl"))
    scales = lax.rsqrt(degree.astype(jnp.float32))[:, None]
    row_ids = tile_row.reshape(-1)
    owner, within = tile_col.reshape(-1) // own_blocks, tile_col.reshape(-1) % own_blocks
    col_ids = (owner % 2 ^ lax.axis_index("core")) * half_blocks + owner // 2 * own_blocks + within
    live = tile_live.reshape(1)
    slots, edges = edge_dst.shape[2:]
    blocks = (-1, TILE, hidden_width)
    scaled = jnp.dot(features, weight, precision=HIGH, preferred_element_type=jnp.float32) * scales
    near = gather(scaled, ("x", "zl"))
    far = swap_cores(near)
    tiles = build_tiles(live, edge_dst.reshape(slots, edges), edge_src.reshape(slots, edges))
    (sums,) = aggregate(
        tiles, live, col_ids, row_ids, [near.reshape(blocks), far.reshape(blocks)], [group_blocks], False
    )
    own_sums = exchange(sums.reshape(-1, own_rows, hidden_width), REP).sum(0)
    pre = (own_sums + scaled) * scales
    hidden, pull = jax.vjp(activation, pre)
    (own_grad,) = pull(cotangent)
    back_own = own_grad * scales
    back_group = gather(back_own, REP)
    near, far = aggregate(
        tiles, live, row_ids, col_ids, [back_group.reshape(blocks)], [half_blocks] * 2, True
    )
    near = near + swap_cores(far)
    column_grad = exchange(near.reshape(-1, own_rows, hidden_width), ("x", "zl")).sum(0)
    grad_rows = (column_grad + back_own) * scales
    local_grad = jnp.einsum(
        "ni,nh->ih", features, grad_rows, precision=HIGH, preferred_element_type=jnp.float32
    )
    return (hidden, sum_everywhere(local_grad))


def solution(mesh):
    mesh = Mesh(mesh.devices.reshape(4, 2, 2, 4, 2), BLK + REP)
    nodes = P(BLK + REP)
    tile = P(BLK, REP)
    return jax.shard_map(
        local,
        mesh=mesh,
        in_specs=(nodes, P(), nodes, nodes, tile, tile, tile, tile, tile),
        out_specs=(nodes, P()),
        check_vma=False,
    )
```

time: 294 us -> 270 us (0.918)
  Pallas kernels: 38.1 us -> 16.6 us
  local copies, waits for them, and re-layouts: 1.95 us -> 5.36 us
    pallas_call x3, Pallas kernels: 38.1 us -> 16.6 us  [the longest x2 13.3 us: aggregate(): pl.pallas_call(partial(aggregate_kernel, transpose, parts, targets), in_s...]
    unnamed x6 -> x16, local copies, waits for them, and re-layouts: 0.44 us -> 3.85 us
  transfers between devices with their start and end apart: 2 -> 2, of which waited for: 1 -> 2; matrix products, arithmetic and copies ran while one was open for 0% -> 0% of each run, Pallas kernels for 3% -> 1%
where the time goes in v4:
time: 270 us
  blocking collectives  222 us (82%)
  Pallas kernels  16.6 us (6%)
  starting transfers between devices  7.36 us (3%)
  waiting for transfers between devices  6.9 us (3%)
  other arithmetic  6.86 us (3%)
  local copies, waits for them, and re-layouts  5.36 us (2%)
  matrix products  4.05 us (2%)
    all_to_all x7, blocking collectives, exchange(): return lax.all_to_all(value, axes, 0, 0, tiled=True)  222 us
    pallas_call x2, Pallas kernels, aggregate(): pl.pallas_call(partial(aggregate_kernel, transpose, parts, targets), in_s...  13.3 us
    ppermute x2, starting transfers between devices, swap_cores(): return lax.ppermute(value, 'core', [(0, 1), (1, 0)])  7.36 us
    ppermute x2, waiting for transfers between devices, swap_cores(): return lax.ppermute(value, 'core', [(0, 1), (1, 0)])  6.9 us
  transfers between devices with their start and end apart: 2, of which 2 were waited for; matrix products, arithmetic and copies ran while one was open for 0% of the time, Pallas kernels for 1%

profile of v4, /device:TPU:1, one launch (start us, length us, event | category | flops | bytes accessed | tf_op | source)
XLA Modules:
  0.0 270.2 jit_solution(17794950589448880440)
XLA Ops:
  0.6 0.8 convert_rsqrt_fusion
  1.4 0.4 copy-done
  1.8 2.8 %convolution_multiply_fusion = f32[384,256]{1,0:T(8,128)S(1)} fusion(f32[384,602]{0,1:T(8,128)S(1)} %copy-done, f32[602,256]{1,0:T(8,128)} %param.10, f32[384]{0:T(512)S(1)} %convert_rsqrt_fusion), kind=kOutput, calls=%fused_computation.1 | convolution fusion | flops 710246400 | bytes 1935872 | tf_op jit(solution)/shard_map/dot_general | solution.py:177
  5.0 43.3 %all_to_all.35 = f32[8,384,256]{2,1,0:T(8,128)} all-to-all(f32[8,384,256]{2,1,0:T(8,128)S(1)} %broadcast_in_dim.13), channel_id=1, replica_groups=mesh['x'=4,'zl'=2,'core'=2,'y'=4,'zh'=2] {'x','zl'}, dimensions={0} | all-to-all | bytes 6291456 | tf_op jit(solution)/shard_map/all_to_all | solution.py:143
  48.3 1.9 collective-permute-start
  50.9 3.2 %shard_map.104.tiles_ref = bf16[256,128,128]{2,1,0:T(8,128)(2,1)S(1)} custom-call(s32[1]{0:T(128)} %bitcast.18.live_ref, s32[256,256]{1,0:T(8,128)S(1)} %bitcast.23, s32[256,256]{1,0:T(8,128)S(1)} %bitcast.24), custom_call_target="tpu_custom_call" | custom-call | flops 2147483648 | bytes 10000000 | tf_op jit(solution)/shard_map/pallas_call | solution.py:53
  54.2 1.6 collective-permute-done
  55.8 7.7 %shard_map.105 = f32[24,128,256]{2,1,0:T(8,128)S(1)} custom-call(s32[1]{0:T(128)} %bitcast.19.live_ref, s32[256]{0:T(256)S(1)} %fusion.11.pick_ref.place_ref, s32[256]{0:T(256)S(1)} %bitcast.25, bf16[256,128,128]{2,1,0:T(8,128)(2,1)S(1)} %shard_map.104.tiles_ref, f32[24,128,256]{2,1,0:T(8,128)} %bitcast.6.refs_0_, f32[24,128,256]{2,1,0:T(8,128)} %bitcast.7.refs_1_), custom_call_target="tpu_custom_call" | custom-call | flops 4294967296 | bytes 20000000 | tf_op jit(solution)/shard_map/pallas_call | solution.py:124
  63.5 53.1 %all_to_all.36 = f32[8,384,256]{2,1,0:T(8,128)} all-to-all(f32[8,384,256]{2,1,0:T(8,128)S(1)} %bitcast.21), channel_id=1, replica_groups=mesh['x'=4,'zl'=2,'core'=2,'y'=4,'zh'=2] {'y','zh'}, dimensions={0} | all-to-all | bytes 6291456 | tf_op jit(solution)/shard_map/all_to_all | solution.py:143
  116.6 2.2 reduce_sum.36
  118.9 1.1 fusion.6
  120.2 40.3 %all_to_all.37 = f32[8,384,256]{2,1,0:T(8,128)S(1)} all-to-all(f32[8,384,256]{2,1,0:T(8,128)S(1)} %broadcast_in_dim.14), channel_id=1, replica_groups=mesh['x'=4,'zl'=2,'core'=2,'y'=4,'zh'=2] {'y','zh'}, dimensions={0} | all-to-all | bytes 6291456 | tf_op jit(solution)/shard_map/all_to_all | solution.py:143
  160.6 3.4 %copy-done.2 = bf16[256,128,128]{2,1,0:T(8,128)(2,1)S(1)} copy-done((bf16[256,128,128]{2,1,0:T(8,128)(2,1)S(1)}, bf16[256,128,128]{2,1,0:T(8,128)(2,1)}, u32[]{:S(2)}) %copy-start.2) | copy-done | bytes 8388632
  163.9 5.6 %shard_map.106 = (f32[24,128,256]{2,1,0:T(8,128)S(1)}, f32[24,128,256]{2,1,0:T(8,128)S(1)}) custom-call(s32[1]{0:T(128)} %bitcast.20.live_ref, s32[256]{0:T(256)S(1)} %bitcast.26, s32[256]{0:T(256)S(1)} %fusion.11.pick_ref.place_ref, bf16[256,128,128]{2,1,0:T(8,128)(2,1)S(1)} %copy-done.2, f32[24,128,256]{2,1,0:T(8,128)S(1)} %bitcast.22), custom_call_target="tpu_custom_call" | custom-call | flops 4294967296 | bytes 20000000 | tf_op jit(solution)/shard_map/pallas_call | solution.py:124
  169.5 5.5 %collective-permute-start.1 = (f32[24,128,256]{2,1,0:T(8,128)S(1)}, f32[24,128,256]{2,1,0:T(8,128)S(1)}, u32[]{:S(2)}, u32[]{:S(2)}) collective-permute-start(f32[24,128,256]{2,1,0:T(8,128)S(1)} %get-tuple-element.5), channel_id=1, source_target_pairs={{0,8},{8,0},{1,9},{9,1},{2,10},{10,2},{3,11},{11,3},{4,12},{12,4},... | collective-permute-start | bytes 9437192 | tf_op jit(solution)/shard_map/ppermute | solution.py:151
  175.0 5.3 %collective-permute-done.1 = f32[24,128,256]{2,1,0:T(8,128)S(1)} collective-permute-done((f32[24,128,256]{2,1,0:T(8,128)S(1)}, f32[24,128,256]{2,1,0:T(8,128)S(1)}, u32[]{:S(2)}, u32[]{:S(2)}) %collective-permute-start.1) | collective-permute-done | bytes 3145760 | tf_op jit(solution)/shard_map/ppermute | solution.py:151
  180.3 0.5 add.43
  180.8 40.6 %all_to_all.38 = f32[8,384,256]{2,1,0:T(8,128)} all-to-all(f32[8,384,256]{2,1,0:T(8,128)S(1)} %bitcast.27), channel_id=1, replica_groups=mesh['x'=4,'zl'=2,'core'=2,'y'=4,'zh'=2] {'x','zl'}, dimensions={0} | all-to-all | bytes 6291456 | tf_op jit(solution)/shard_map/all_to_all | solution.py:143
  221.5 2.2 reduce_sum.37
  223.6 1.2 convolution_bitcast_fusion
  224.9 16.0 %all_to_all.39 = f32[16,40,256]{2,1,0:T(8,128)S(1)} all-to-all(f32[16,40,256]{2,1,0:T(8,128)S(1)} %bitcast.28), channel_id=1, replica_groups=mesh['x'=4,'zl'=2,'core'=2,'y'=4,'zh'=2] {'x','zl','core'}, dimensions={0} | all-to-all | bytes 1310720 | tf_op jit(solution)/shard_map/all_to_all | solution.py:143
  241.0 12.1 %all_to_all.40 = f32[8,40,256]{2,1,0:T(8,128)S(1)} all-to-all(f32[8,40,256]{2,1,0:T(8,128)S(1)} %broadcast_in_dim.15), channel_id=1, replica_groups=mesh['x'=4,'zl'=2,'core'=2,'y'=4,'zh'=2] {'y','zh'}, dimensions={0} | all-to-all | bytes 655360 | tf_op jit(solution)/shard_map/all_to_all | solution.py:143
  253.2 16.1 %all_to_all.41 = f32[16,40,256]{2,1,0:T(8,128)S(1)} all-to-all(f32[16,40,256]{2,1,0:T(8,128)S(1)} %broadcast_in_dim.16), channel_id=1, replica_groups=mesh['x'=4,'zl'=2,'core'=2,'y'=4,'zh'=2] {'x','zl','core'}, dimensions={0} | all-to-all | bytes 1310720 | tf_op jit(solution)/shard_map/all_to_all | solution.py:143
  269.3 0.9 slice.4
  (24 shorter events, 0.8 us)
Async XLA Ops:
  0.6 1.2 copy-start
  4.9 45.9 %copy-start.7 = (s32[1,1,256]{2,1,0:T(1,128)S(1)}, s32[1,1,256]{2,1,0:T(1,128)}, u32[]{:S(2)}) copy-start(s32[1,1,256]{2,1,0:T(1,128)} %param.14) | copy-start | bytes 3076
  4.9 45.9 %copy-start.3 = (s32[1,1,256,256]{3,2,1,0:T(8,128)S(1)}, s32[1,1,256,256]{3,2,1,0:T(8,128)}, u32[]{:S(2)}) copy-start(s32[1,1,256,256]{3,2,1,0:T(8,128)} %param.15) | copy-start | bytes 786436
  5.0 45.9 %copy-start.4 = (s32[1,1,256,256]{3,2,1,0:T(8,128)S(1)}, s32[1,1,256,256]{3,2,1,0:T(8,128)}, u32[]{:S(2)}) copy-start(s32[1,1,256,256]{3,2,1,0:T(8,128)} %param.16) | copy-start | bytes 786436
  48.3 7.5 %collective-permute-start = (f32[8,384,256]{2,1,0:T(8,128)}, f32[8,384,256]{2,1,0:T(8,128)}, u32[]{:S(2)}, u32[]{:S(2)}) collective-permute-start(f32[8,384,256]{2,1,0:T(8,128)} %all_to_all.35), channel_id=1, source_target_pairs={{0,8},{8,0},{1,9},{9,1},{2,10},{10,2},{3,11},{11,3},{4,12},{12,4},... | collective-permute-start | bytes 9437192 | tf_op jit(solution)/shard_map/ppermute | solution.py:151
  50.9 4.9 %copy-start.5 = (s32[1,1,256]{2,1,0:T(1,128)S(1)}, s32[1,1,256]{2,1,0:T(1,128)}, u32[]{:S(2)}) copy-start(s32[1,1,256]{2,1,0:T(1,128)} %param.13) | copy-start | bytes 3076
  54.1 9.4 %copy-start.1 = (bf16[256,128,128]{2,1,0:T(8,128)(2,1)}, bf16[256,128,128]{2,1,0:T(8,128)(2,1)S(1)}, u32[]{:S(2)}) copy-start(bf16[256,128,128]{2,1,0:T(8,128)(2,1)S(1)} %shard_map.104.tiles_ref) | copy-start | bytes 25165828
  116.6 2.2 copy-start.6
  160.6 3.4 %copy-start.2 = (bf16[256,128,128]{2,1,0:T(8,128)(2,1)S(1)}, bf16[256,128,128]{2,1,0:T(8,128)(2,1)}, u32[]{:S(2)}) copy-start(bf16[256,128,128]{2,1,0:T(8,128)(2,1)} %copy-done.1) | copy-start | bytes 25165828
  169.5 10.8 %collective-permute-start.1 = (f32[24,128,256]{2,1,0:T(8,128)S(1)}, f32[24,128,256]{2,1,0:T(8,128)S(1)}, u32[]{:S(2)}, u32[]{:S(2)}) collective-permute-start(f32[24,128,256]{2,1,0:T(8,128)S(1)} %get-tuple-element.5), channel_id=1, source_target_pairs={{0,8},{8,0},{1,9},{9,1},{2,10},{10,2},{3,11},{11,3},{4,12},{12,4},... | collective-permute-start | bytes 9437192 | tf_op jit(solution)/shard_map/ppermute | solution.py:151

commit v5 on v4

v5 whole, which is shorter than its diff:
```python
from functools import partial

import jax
import jax.numpy as jnp
from jax import lax
from jax.experimental import pallas as pl
from jax.experimental.pallas import tpu as pltpu
from jax.sharding import Mesh
from jax.sharding import PartitionSpec as P

TILE = 128
HIGH = lax.Precision.HIGHEST
activation = partial(jax.nn.gelu, approximate=True)
ROWS = 32
PIECE = 6
PARTS = 2
UNROLL = 32
VMEM_LIMIT = 32 * 1024 * 1024
BLK = ("x", "zl", "core")
REP = ("y", "zh")


def in_vmem(value):
    return pltpu.with_memory_space_constraint(value, pltpu.VMEM)


def in_hbm(value):
    return pltpu.with_memory_space_constraint(value, pltpu.HBM)


SMEM = pl.BlockSpec(memory_space=pltpu.SMEM)
VMEM = pl.BlockSpec(memory_space=pltpu.VMEM)
ANY = pl.BlockSpec(memory_space=pl.ANY)


def tile_kernel(live_ref, dst_hbm, src_hbm, out_ref, dst_ref, src_ref, tiles, edge_sems, sems):
    live = live_ref[0]
    groups = (live + ROWS - 1) // ROWS
    node_ids = lax.broadcasted_iota(jnp.int32, (TILE, dst_ref.shape[1]), 0)

    def copies_in(group):
        at = pl.ds(pl.multiple_of(group * ROWS, ROWS), ROWS)
        return [
            pltpu.make_async_copy(dst_hbm.at[at], dst_ref.at[at], edge_sems.at[0, group]),
            pltpu.make_async_copy(src_hbm.at[at], src_ref.at[at], edge_sems.at[1, group]),
        ]

    def start_in(group, carry):
        for copy in copies_in(group):
            copy.start()
        return carry

    def copy_out(group):
        at = pl.ds(pl.multiple_of(group * ROWS, ROWS), ROWS)
        return pltpu.make_async_copy(tiles.at[at], out_ref.at[at], sems.at[group])

    def some_slots(group, carry):
        for copy in copies_in(group):
            copy.wait()
        first = pl.multiple_of(group * ROWS, ROWS)
        dst = dst_ref[pl.ds(first, ROWS)]
        src = src_ref[pl.ds(first, ROWS)]
        for k in range(ROWS):
            dst_ids = jnp.where(first + k < live, dst[k : k + 1], TILE)
            dst_hot = (dst_ids == node_ids).astype(jnp.bfloat16)
            src_hot = (src[k : k + 1] == node_ids).astype(jnp.bfloat16)
            counts = lax.dot_general(
                dst_hot, src_hot, (((1,), (1,)), ((), ())), preferred_element_type=jnp.float32
            )
            tiles[first + k] = counts.astype(jnp.bfloat16)
        copy_out(group).start()
        return carry

    lax.fori_loop(0, groups, start_in, 0)
    lax.fori_loop(0, groups, some_slots, 0)
    lax.fori_loop(0, groups, lambda group, carry: (copy_out(group).wait(), carry)[1], 0)


def build_tiles(live, edge_dst, edge_src):
    slots, edges = edge_dst.shape
    return pl.pallas_call(
        tile_kernel,
        in_specs=[SMEM, ANY, ANY],
        out_specs=ANY,
        out_shape=pltpu.HBM((slots, TILE, TILE), jnp.bfloat16),
        scratch_shapes=[
            pltpu.VMEM((slots, edges), jnp.int32),
            pltpu.VMEM((slots, edges), jnp.int32),
            pltpu.VMEM((slots, TILE, TILE), jnp.bfloat16),
            pltpu.SemaphoreType.DMA((2, slots // ROWS)),
            pltpu.SemaphoreType.DMA((slots // ROWS,)),
        ],
        compiler_params=pltpu.CompilerParams(vmem_limit_bytes=VMEM_LIMIT),
        cost_estimate=pl.CostEstimate(flops=10**6, bytes_accessed=10**5, transcendentals=0),
    )(live, in_hbm(edge_dst), in_hbm(edge_src))


def aggregate_kernel(transpose, parts, targets, live_ref, pick_ref, place_ref, tiles_ref, *refs):
    sources, outs = refs[:parts], refs[parts : parts + targets]
    split, totals, landed, tiles, sems, tile_sems = refs[parts + targets :]
    groups = (live_ref[0] + UNROLL - 1) // UNROLL

    def tile_copy(group):
        at = pl.ds(pl.multiple_of(group * UNROLL, UNROLL), UNROLL)
        return pltpu.make_async_copy(tiles_ref.at[at], tiles.at[at], tile_sems.at[group])

    pieces = [
        (p, b) for p, source_ref in enumerate(sources) for b in range(0, source_ref.shape[0], PIECE)
    ]
    copies = []
    for n, (p, b) in enumerate(pieces):
        copy = pltpu.make_async_copy(
            sources[p].at[pl.ds(b, PIECE)], landed.at[pl.ds(n * PIECE, PIECE)], sems.at[n]
        )
        copy.start()
        copies.append(copy)
    lax.fori_loop(0, groups, lambda group, carry: (tile_copy(group).start(), carry)[1], 0)
    totals[...] = jnp.zeros_like(totals)

    for n, copy in enumerate(copies):
        copy.wait()

        def split_block(k, carry):
            value = landed[n * PIECE + k]
            high = value.astype(jnp.bfloat16)
            split[n * PIECE + k, :TILE] = high
            split[n * PIECE + k, TILE:] = (value - high.astype(jnp.float32)).astype(jnp.bfloat16)
            return carry

        lax.fori_loop(0, PIECE, split_block, 0)

    def some_tiles(group, carry):
        tile_copy(group).wait()
        first = group * UNROLL
        products = []
        for k in range(UNROLL):
            tile = tiles[first + k]
            picked = split[pick_ref[first + k]]
            twice = jnp.concatenate([tile, tile], axis=0 if transpose else 1)
            products.append(
                lax.dot_general(
                    twice,
                    picked,
                    (((0 if transpose else 1,), (0,)), ((), ())),
                    preferred_element_type=jnp.float32,
                )
            )
        for k in range(UNROLL):
            totals[place_ref[first + k]] += products[k]
        return carry

    lax.fori_loop(0, groups, some_tiles, 0)
    for p, out_ref in enumerate(outs):
        count = out_ref.shape[0]
        out_ref[...] = totals[p * count : (p + 1) * count]


def aggregate(tiles, live, pick_ids, place_ids, sources, target_blocks, transpose):
    slots = tiles.shape[0]
    source_blocks, _, width = sources[0].shape
    parts, targets = len(sources), len(target_blocks)
    return pl.pallas_call(
        partial(aggregate_kernel, transpose, parts, targets),
        in_specs=[SMEM] * 3 + [ANY] * (1 + parts),
        out_specs=[VMEM] * targets,
        out_shape=[pltpu.VMEM((b, TILE, width), jnp.float32) for b in target_blocks],
        scratch_shapes=[
            pltpu.VMEM((parts * source_blocks, 2 * TILE, width), jnp.bfloat16),
            pltpu.VMEM((sum(target_blocks), TILE, width), jnp.float32),
            pltpu.VMEM((parts * source_blocks, TILE, width), jnp.float32),
            pltpu.VMEM(tiles.shape, jnp.bfloat16),
            pltpu.SemaphoreType.DMA((parts * source_blocks // PIECE,)),
            pltpu.SemaphoreType.DMA((slots // UNROLL,)),
        ],
        compiler_params=pltpu.CompilerParams(vmem_limit_bytes=VMEM_LIMIT),
        cost_estimate=pl.CostEstimate(
            flops=10**6, bytes_accessed=10**5, transcendentals=0
        ),
    )(live, pick_ids, place_ids, in_hbm(tiles), *sources)


def gradient_kernel(*refs):
    features, (rows_ref, out_ref) = refs[:-2], refs[-2:]
    height, nodes = features[0].shape
    blocks = PARTS * nodes // TILE
    width = out_ref.shape[1]
    out_ref[...] = jnp.zeros_like(out_ref)
    for p in range(0, len(features), PARTS):
        part = jnp.concatenate([f[...] for f in features[p : p + PARTS]], axis=1)
        first = p * nodes // TILE
        rows = rows_ref[first : first + blocks].reshape(blocks * TILE, width)
        rows_high = rows.astype(jnp.bfloat16)
        rows_low = (rows - rows_high.astype(jnp.float32)).astype(jnp.bfloat16)
        right = jnp.concatenate([rows_high, rows_low, rows_high], axis=0)
        high = part.astype(jnp.bfloat16)
        low = (part - high.astype(jnp.float32)).astype(jnp.bfloat16)
        left = jnp.concatenate([high, high, low], axis=1)
        out_ref[:height] += jnp.dot(left, right, preferred_element_type=jnp.float32)


def gradient(features, rows, out_rows):
    width = rows.shape[2]
    return pl.pallas_call(
        gradient_kernel,
        in_specs=[VMEM] * (len(features) + 1),
        out_specs=VMEM,
        out_shape=pltpu.VMEM((out_rows, width), jnp.float32),
        compiler_params=pltpu.CompilerParams(vmem_limit_bytes=VMEM_LIMIT),
        cost_estimate=pl.CostEstimate(
            flops=6 * out_rows * rows.shape[0] * TILE * width, bytes_accessed=10**7, transcendentals=0
        ),
    )(*[in_vmem(f) for f in features], in_vmem(rows))


def exchange(value, axes):
    return lax.all_to_all(value, axes, 0, 0, tiled=True)


def gather(value, axes):
    return exchange(jnp.broadcast_to(value, (lax.axis_size(axes),) + value.shape), axes)


def swap(value, axis):
    return lax.ppermute(value, axis, [(0, 1), (1, 0)])


def from_ahead(value, axis, steps):
    size = lax.axis_size(axis)
    return lax.ppermute(value, axis, [(i, (i - steps) % size) for i in range(size)])


def sum_everywhere(value):
    rows, width = value.shape
    parts = lax.axis_size(BLK)
    part_rows = -(-rows // (8 * parts)) * 8
    value = jnp.pad(value, ((0, part_rows * parts - rows), (0, 0)))
    own = exchange(value.reshape(parts, part_rows, width), BLK).sum(0)
    own = gather(own, REP).sum(0)
    return gather(own, BLK).reshape(-1, width)[:rows]


def local(features, weight, cotangent, degree, tile_row, tile_col, edge_dst, edge_src, tile_live):
    own_rows, in_width = features.shape
    hidden_width = weight.shape[1]
    own_blocks = own_rows // TILE
    group_blocks = own_blocks * lax.axis_size(REP)
    half_blocks = own_blocks * lax.axis_size(("x", "zl"))
    blocks = (-1, TILE, hidden_width)
    scales = lax.rsqrt(degree.astype(jnp.float32))[:, None]
    row_ids = tile_row.reshape(-1)
    live = tile_live.reshape(1)
    slots, edges = edge_dst.shape[2:]
    owner, within = tile_col.reshape(-1) // own_blocks, tile_col.reshape(-1) % own_blocks
    other_core = owner % 2 ^ lax.axis_index("core")
    from_ids = other_core * half_blocks + owner // 2 * own_blocks + within
    x_ahead = (owner // 4 - lax.axis_index("x")) % 4
    other_z = owner // 2 % 2 ^ lax.axis_index("zl")
    to_ids = other_core * half_blocks + (x_ahead * 2 + other_z) * own_blocks + within

    scaled = jnp.dot(features, weight, precision=HIGH, preferred_element_type=jnp.float32) * scales
    height = -(-in_width // 32) * 32
    here = jnp.pad(features.T * scales.T, ((0, height - in_width), (0, 0)))
    scaled, here = lax.optimization_barrier((scaled, here))
    near = gather(scaled, ("x", "zl"))
    here, near = lax.optimization_barrier((here, near))
    far = swap(near, "core")
    across = swap(here, "zl")
    here_x = [from_ahead(here, "x", steps) for steps in (1, 2, 3)]
    tiles = build_tiles(live, edge_dst.reshape(slots, edges), edge_src.reshape(slots, edges))

    def forward(near, far, scaled, cotangent):
        sources = [near.reshape(blocks), far.reshape(blocks)]
        (sums,) = aggregate(tiles, live, from_ids, row_ids, sources, [group_blocks], False)
        own_sums = exchange(sums.reshape(-1, own_rows, hidden_width), REP).sum(0)
        hidden, pull = jax.vjp(activation, (own_sums + scaled) * scales)
        return hidden, pull(cotangent)[0] * scales

    def never(near, far, scaled, cotangent):
        return scaled + cotangent, scaled - cotangent

    hidden, back_own = lax.cond(live[0] > 0, forward, never, near, far, scaled, cotangent)
    across, here_x, back_own = lax.optimization_barrier((across, here_x, back_own))
    across_x = [from_ahead(across, "x", steps) for steps in (1, 2, 3)]
    back_group = lax.cond(
        live[0] > 0,
        lambda back: gather(back, REP),
        lambda back: jnp.broadcast_to(back, (lax.axis_size(REP),) + back.shape),
        back_own,
    )
    across_x, back_group = lax.optimization_barrier((across_x, back_group))
    kept, sent = aggregate(
        tiles, live, row_ids, to_ids, [back_group.reshape(blocks)], [half_blocks] * 2, True
    )
    kept = kept + swap(sent, "core")
    kept = kept + jnp.pad(back_own.reshape(blocks), ((0, half_blocks - own_blocks), (0, 0), (0, 0)))
    held = [part for pair in zip([here, *here_x], [across, *across_x]) for part in pair]
    parts = lax.axis_size(BLK)
    out_rows = -(-in_width // (8 * parts)) * 8 * parts
    return (hidden, sum_everywhere(gradient(held, kept, out_rows))[:in_width])


def solution(mesh):
    mesh = Mesh(mesh.devices.reshape(4, 2, 2, 4, 2), BLK + REP)
    nodes = P(BLK + REP)
    tile = P(BLK, REP)
    return jax.shard_map(
        local,
        mesh=mesh,
        in_specs=(nodes, P(), nodes, nodes, tile, tile, tile, tile, tile),
        out_specs=(nodes, P()),
        check_vma=False,
    )
```

time: 270 us -> 242 us (0.90)
  blocking collectives: 222 us -> 172 us
  Pallas kernels: 16.6 us -> 27.7 us
  starting transfers between devices: 7.36 us -> 18.2 us
    all_to_all x7 -> x6, blocking collectives: 222 us -> 172 us  [exchange(): return lax.all_to_all(value, axes, 0, 0, tiled=True)]
    ppermute x2 -> x9, starting transfers between devices: 7.36 us -> 18.2 us  [the longest x6 9.69 us: from_ahead(): lax.ppermute(value, axis, [(i, (i - steps) % size) for i in range(size)])]
    pallas_call x1 -> x2, Pallas kernels: 3.25 us -> 11.5 us  [the longest x1 6.09 us: build_tiles(): pl.pallas_call(tile_kernel, in_specs=[SMEM, ANY, ANY], out_specs=ANY, out...]
    unnamed x16 -> x12, local copies, waits for them, and re-layouts: 3.85 us -> 0.04 us
    pallas_call x2, Pallas kernels: 13.3 us -> 16.2 us  [aggregate(): pl.pallas_call(partial(aggregate_kernel, transpose, parts, targets), in_s...]
    ppermute x2 -> x9, waiting for transfers between devices: 6.9 us -> 6.74 us  [the longest x3 5.29 us: swap(): return lax.ppermute(value, axis, [(0, 1), (1, 0)])]
  transfers between devices with their start and end apart: 2 -> 9, of which waited for: 2 -> 2; matrix products, arithmetic and copies ran while one was open for 0% -> 3% of each run, Pallas kernels for 1% -> 6%
where the time goes in v5:
time: 242 us; the launch traced here: 241 us
  blocking collectives  172 us (71%)
  Pallas kernels  27.7 us (11%)
  starting transfers between devices  18.2 us (8%)
  other arithmetic  8.94 us (4%)
  waiting for transfers between devices  6.74 us (3%)
  local copies, waits for them, and re-layouts  3.41 us (1%)
  matrix products  2.92 us (1%)
    all_to_all x6, blocking collectives, exchange(): return lax.all_to_all(value, axes, 0, 0, tiled=True)  172 us
    pallas_call x2, Pallas kernels, aggregate(): pl.pallas_call(partial(aggregate_kernel, transpose, parts, targets), in_s...  16.2 us
    ppermute x6, starting transfers between devices, from_ahead(): lax.ppermute(value, axis, [(i, (i - steps) % size) for i in range(size)])  9.69 us
    ppermute x3, starting transfers between devices, swap(): return lax.ppermute(value, axis, [(0, 1), (1, 0)])  8.53 us
    pallas_call x1, Pallas kernels, build_tiles(): pl.pallas_call(tile_kernel, in_specs=[SMEM, ANY, ANY], out_specs=ANY, out...  6.09 us
    pallas_call x1, Pallas kernels, gradient(): pl.pallas_call(gradient_kernel, in_specs=[VMEM] * (len(features) + 1), ou...  5.37 us
    ppermute x3, waiting for transfers between devices, swap(): return lax.ppermute(value, axis, [(0, 1), (1, 0)])  5.29 us
  transfers between devices with their start and end apart: 9, of which 2 were waited for; matrix products, arithmetic and copies ran while one was open for 3% of the time, Pallas kernels for 6%

profile of v5, /device:TPU:1, one launch (start us, length us, event | category | flops | bytes accessed | tf_op | source)
XLA Modules:
  0.0 241.4 jit_solution(18293503579386630033)
XLA Ops:
  1.4 1.3 multiply_bitcast_fusion
  2.7 2.9 %convolution_multiply_fusion = f32[384,256]{1,0:T(8,128)S(1)} fusion(f32[384,602]{0,1:T(8,128)} %param.13, f32[602,256]{1,0:T(8,128)S(1)} %copy-done, f32[384]{0:T(512)S(1)} %convert_rsqrt_fusion), kind=kOutput, calls=%fused_computation.13 | convolution fusion | flops 710246400 | bytes 1935872 | tf_op jit(solution)/shard_map/dot_general | solution.py:260
  5.9 43.2 %all_to_all.30 = f32[8,384,256]{2,1,0:T(8,128)} all-to-all(f32[8,384,256]{2,1,0:T(8,128)S(1)} %broadcast_in_dim.17), channel_id=1, replica_groups=mesh['x'=4,'zl'=2,'core'=2,'y'=4,'zh'=2] {'x','zl'}, dimensions={0} | all-to-all | bytes 6291456 | tf_op jit(solution)/shard_map/all_to_all | solution.py:216
  49.1 1.9 collective-permute-start
  55.0 6.1 %shard_map.104.tiles_ref = bf16[256,128,128]{2,1,0:T(8,128)(2,1)} custom-call(s32[1]{0:T(128)} %bitcast.18.live_ref, s32[256,256]{1,0:T(8,128)} %bitcast.24, s32[256,256]{1,0:T(8,128)} %bitcast.25), custom_call_target="tpu_custom_call" | custom-call | flops 1000000 | bytes 100000 | tf_op jit(solution)/shard_map/pallas_call | solution.py:81
  61.3 58.7 %conditional.2 = (f32[384,256]{1,0:T(8,128)}, f32[384,256]{1,0:T(8,128)}) conditional(s32[]{:T(128)} %bitcast.3, (f32[384,256]{1,0:T(8,128)S(1)}, f32[384,256]{1,0:T(8,128)S(1)}) %tuple.45, (s32[256]{0:T(256)S(1)}, s32[256]{0:T(256)S(1)}, s32[256]{0:T(256)S(1)}, f32[8,384,256]{2,1,0:T(8,128)}, f32[8,384,256]{2,1,0:T(8,128)}, /*index=5*/s32[1]{0:T(128)}, ...), branch_computations={%region_0.1_spmd, %region_1.3_spmd} | conditional | flops 3949888 | bytes 15047916 | solution.py:281
  62.2 8.8 %branch_1_fun.1 = f32[24,128,256]{2,1,0:T(8,128)S(1)} custom-call(s32[1]{0:T(128)} %get-tuple-element.39.live_ref, s32[256]{0:T(256)S(1)} %add_add_fusion.pick_ref, s32[256]{0:T(256)S(1)} %get-tuple-element.43.place_ref, bf16[256,128,128]{2,1,0:T(8,128)(2,1)} %get-tuple-element.44.tiles_ref, f32[24,128,256]{2,1,0:T(8,128)} %bitcast.refs_0_, ...), custom_call_target="tpu_custom_call" | custom-call | flops 1000000 | bytes 100000 | tf_op jit(solution)/shard_map/cond/branch_1_fun/pallas_call | solution.py:162
  70.9 43.7 %all_to_all.28 = f32[8,384,256]{2,1,0:T(8,128)} all-to-all(f32[8,384,256]{2,1,0:T(8,128)S(1)} %bitcast.20), channel_id=1, replica_groups=mesh['x'=4,'zl'=2,'core'=2,'y'=4,'zh'=2] {'y','zh'}, dimensions={0} | all-to-all | bytes 6291456 | tf_op jit(solution)/shard_map/cond/branch_1_fun/all_to_all | solution.py:216
  114.6 2.9 %reduce_sum.24 = f32[384,256]{1,0:T(8,128)} reduce(f32[8,384,256]{2,1,0:T(8,128)} %all_to_all.28, f32[]{:T(128)} %constant.83.clone), dimensions={0}, to_apply=%region_2.2 | reduce | flops 688128 | bytes 3538948 | tf_op jit(solution)/shard_map/cond/branch_1_fun/reduce_sum | solution.py:274
  117.5 2.5 %fusion.6 = (f32[384,256]{1,0:T(8,128)}, f32[384,256]{1,0:T(8,128)}) fusion(f32[384,256]{1,0:T(8,128)} %copy-done.5, f32[384]{0:T(512)S(1)} %get-tuple-element.48, f32[384,256]{1,0:T(8,128)} %reduce_sum.24, f32[384,256]{1,0:T(8,128)} %copy-done.3), kind=kLoop, calls=%fused_computation.8 | loop fusion | flops 2260992 | bytes 1967616 | tf_op jit(solution)/shard_map/cond/branch_1_fun/mul | solution.py:276
  120.0 1.6 collective-permute-start.5
  121.6 6.0 %collective-permute-start.6 = (f32[608,384]{1,0:T(8,128)S(1)}, f32[608,384]{1,0:T(8,128)}, u32[]{:S(2)}, u32[]{:S(2)}) collective-permute-start(f32[608,384]{1,0:T(8,128)S(1)} %collective-permute-done.1.refs_1_), channel_id=1, source_target_pairs={{0,64},{32,96},{64,0},{96,32},{1,65},{33,97},{65,1},{97,33},{2,66}... | collective-permute-start | bytes 2801672 | tf_op jit(solution)/shard_map/ppermute | solution.py:229
  127.6 39.8 %conditional.3 = (f32[8,384,256]{2,1,0:T(8,128)}) conditional(s32[]{:T(128)} %bitcast.3, f32[384,256]{1,0:T(8,128)} %get-tuple-element.77, f32[384,256]{1,0:T(8,128)} %get-tuple-element.77), branch_computations={%region_3.4_spmd, %region_4.5_spmd} | conditional | bytes 9830408 | solution.py:284
  127.6 1.3 broadcast_in_dim.13
  128.8 38.6 %all_to_all.29 = f32[8,384,256]{2,1,0:T(8,128)} all-to-all(f32[8,384,256]{2,1,0:T(8,128)S(1)} %broadcast_in_dim.13), channel_id=1, replica_groups=mesh['x'=4,'zl'=2,'core'=2,'y'=4,'zh'=2] {'y','zh'}, dimensions={0} | all-to-all | bytes 6291456 | tf_op jit(solution)/shard_map/cond/branch_1_fun/all_to_all | solution.py:216
  167.4 1.4 collective-permute-done.7.refs_7_
  168.8 7.5 %shard_map.105 = (f32[24,128,256]{2,1,0:T(8,128)S(1)}, f32[24,128,256]{2,1,0:T(8,128)S(1)}) custom-call(s32[1]{0:T(128)} %bitcast.19.live_ref, s32[256]{0:T(256)S(1)} %bitcast.27, s32[256]{0:T(256)S(1)} %get-tuple-element.86.place_ref, bf16[256,128,128]{2,1,0:T(8,128)(2,1)} %shard_map.104.tiles_ref, f32[24,128,256]{2,1,0:T(8,128)} %bitcast.22), custom_call_target="tpu_custom_call" | custom-call | flops 1000000 | bytes 100000 | tf_op jit(solution)/shard_map/pallas_call | solution.py:162
  176.3 5.5 %collective-permute-start.8 = (f32[24,128,256]{2,1,0:T(8,128)S(1)}, f32[24,128,256]{2,1,0:T(8,128)S(1)}, u32[]{:S(2)}, u32[]{:S(2)}) collective-permute-start(f32[24,128,256]{2,1,0:T(8,128)S(1)} %get-tuple-element.85), channel_id=1, source_target_pairs={{0,8},{8,0},{1,9},{9,1},{2,10},{10,2},{3,11},{11,3},{4,12},{12,4},... | collective-permute-start | bytes 9437192 | tf_op jit(solution)/shard_map/ppermute | solution.py:224
  181.8 5.3 %collective-permute-done.8 = f32[24,128,256]{2,1,0:T(8,128)S(1)} collective-permute-done((f32[24,128,256]{2,1,0:T(8,128)S(1)}, f32[24,128,256]{2,1,0:T(8,128)S(1)}, u32[]{:S(2)}, u32[]{:S(2)}) %collective-permute-start.8) | collective-permute-done | bytes 3145760 | tf_op jit(solution)/shard_map/ppermute | solution.py:224
  187.1 1.4 pad_add_fusion.refs_8_
  188.5 5.4 %shard_map.106 = f32[640,256]{1,0:T(8,128)S(1)} custom-call(f32[608,384]{1,0:T(8,128)S(1)} %pad.8.refs_0_, f32[608,384]{1,0:T(8,128)S(1)} %collective-permute-done.1.refs_1_, f32[608,384]{1,0:T(8,128)S(1)} %collective-permute-done.2.refs_2_, f32[608,384]{1,0:T(8,128)} %collective-permute-done.5.refs_3_, f32[608,384]{1,0:T(8,128)} %collective-permute-done.3.refs_4_, ...), custom_call_target="tpu_custom_call" | custom-call | flops 3019898880 | bytes 10000000 | tf_op jit(solution)/shard_map/pallas_call | solution.py:203
  193.9 18.0 %all_to_all.31 = f32[16,40,256]{2,1,0:T(8,128)S(1)} all-to-all(f32[16,40,256]{2,1,0:T(8,128)S(1)} %bitcast.21), channel_id=1, replica_groups=mesh['x'=4,'zl'=2,'core'=2,'y'=4,'zh'=2] {'x','zl','core'}, dimensions={0} | all-to-all | bytes 1310720 | tf_op jit(solution)/shard_map/all_to_all | solution.py:216
  212.0 12.4 %all_to_all.32 = f32[8,40,256]{2,1,0:T(8,128)S(1)} all-to-all(f32[8,40,256]{2,1,0:T(8,128)S(1)} %broadcast_in_dim.18), channel_id=1, replica_groups=mesh['x'=4,'zl'=2,'core'=2,'y'=4,'zh'=2] {'y','zh'}, dimensions={0} | all-to-all | bytes 655360 | tf_op jit(solution)/shard_map/all_to_all | solution.py:216
  224.4 16.1 %all_to_all.33 = f32[16,40,256]{2,1,0:T(8,128)S(1)} all-to-all(f32[16,40,256]{2,1,0:T(8,128)S(1)} %broadcast_in_dim.19), channel_id=1, replica_groups=mesh['x'=4,'zl'=2,'core'=2,'y'=4,'zh'=2] {'x','zl','core'}, dimensions={0} | all-to-all | bytes 1310720 | tf_op jit(solution)/shard_map/all_to_all | solution.py:216
  (41 shorter events, 6.4 us)
Async XLA Ops:
  0.6 2.0 copy-start
  5.6 43.6 %copy-start.1 = (f32[384,256]{1,0:T(8,128)}, f32[384,256]{1,0:T(8,128)S(1)}, u32[]{:S(2)}) copy-start(f32[384,256]{1,0:T(8,128)S(1)} %convolution_multiply_fusion) | copy-start | bytes 1179652
  49.1 12.1 %collective-permute-start = (f32[8,384,256]{2,1,0:T(8,128)}, f32[8,384,256]{2,1,0:T(8,128)}, u32[]{:S(2)}, u32[]{:S(2)}) collective-permute-start(f32[8,384,256]{2,1,0:T(8,128)} %all_to_all.30), channel_id=1, source_target_pairs={{0,8},{8,0},{1,9},{9,1},{2,10},{10,2},{3,11},{11,3},{4,12},{12,4},... | collective-permute-start | bytes 9437192 | tf_op jit(solution)/shard_map/ppermute | solution.py:224
  51.0 69.0 %collective-permute-start.1 = (f32[608,384]{1,0:T(8,128)S(1)}, f32[608,384]{1,0:T(8,128)S(1)}, u32[]{:S(2)}, u32[]{:S(2)}) collective-permute-start(f32[608,384]{1,0:T(8,128)S(1)} %pad.8.refs_0_), channel_id=1, source_target_pairs={{0,16},{16,0},{1,17},{17,1},{2,18},{18,2},{3,19},{19,3},{4,20},{20... | collective-permute-start | bytes 2801672 | tf_op jit(solution)/shard_map/ppermute | solution.py:224
  52.2 67.8 %collective-permute-start.2 = (f32[608,384]{1,0:T(8,128)S(1)}, f32[608,384]{1,0:T(8,128)S(1)}, u32[]{:S(2)}, u32[]{:S(2)}) collective-permute-start(f32[608,384]{1,0:T(8,128)S(1)} %pad.8.refs_0_), channel_id=1, source_target_pairs={{0,96},{32,0},{64,32},{96,64},{1,97},{33,1},{65,33},{97,65},{2,98}... | collective-permute-start | bytes 2801672 | tf_op jit(solution)/shard_map/ppermute | solution.py:229
  53.1 66.9 %collective-permute-start.3 = (f32[608,384]{1,0:T(8,128)S(1)}, f32[608,384]{1,0:T(8,128)}, u32[]{:S(2)}, u32[]{:S(2)}) collective-permute-start(f32[608,384]{1,0:T(8,128)S(1)} %pad.8.refs_0_), channel_id=1, source_target_pairs={{0,64},{32,96},{64,0},{96,32},{1,65},{33,97},{65,1},{97,33},{2,66}... | collective-permute-start | bytes 2801672 | tf_op jit(solution)/shard_map/ppermute | solution.py:229
  54.3 65.7 %collective-permute-start.4 = (f32[608,384]{1,0:T(8,128)S(1)}, f32[608,384]{1,0:T(8,128)}, u32[]{:S(2)}, u32[]{:S(2)}) collective-permute-start(f32[608,384]{1,0:T(8,128)S(1)} %pad.8.refs_0_), channel_id=1, source_target_pairs={{0,32},{32,64},{64,96},{96,0},{1,33},{33,65},{65,97},{97,1},{2,34}... | collective-permute-start | bytes 2801672 | tf_op jit(solution)/shard_map/ppermute | solution.py:229
  55.0 6.1 %copy-start.7 = (s32[1,1,256]{2,1,0:T(1,128)S(1)}, s32[1,1,256]{2,1,0:T(1,128)}, u32[]{:S(2)}) copy-start(s32[1,1,256]{2,1,0:T(1,128)} %param.18) | copy-start | bytes 3076
  55.0 6.2 %copy-start.2 = (f32[384,256]{1,0:T(8,128)S(1)}, f32[384,256]{1,0:T(8,128)}, u32[]{:S(2)}) copy-start(f32[384,256]{1,0:T(8,128)} %copy-done.1) | copy-start | bytes 1179652
  55.0 6.2 %copy-start.4 = (f32[384,256]{1,0:T(8,128)S(1)}, f32[384,256]{1,0:T(8,128)}, u32[]{:S(2)}) copy-start(f32[384,256]{1,0:T(8,128)} %param.15) | copy-start | bytes 1179652
  55.0 6.2 %copy-start.6 = (s32[1,1,256]{2,1,0:T(1,128)S(1)}, s32[1,1,256]{2,1,0:T(1,128)}, u32[]{:S(2)}) copy-start(s32[1,1,256]{2,1,0:T(1,128)} %param.17) | copy-start | bytes 3076
  61.3 0.7 copy-start.3
  61.3 0.9 copy-start.5
  120.0 47.4 %collective-permute-start.5 = (f32[608,384]{1,0:T(8,128)S(1)}, f32[608,384]{1,0:T(8,128)}, u32[]{:S(2)}, u32[]{:S(2)}) collective-permute-start(f32[608,384]{1,0:T(8,128)S(1)} %collective-permute-done.1.refs_1_), channel_id=1, source_target_pairs={{0,96},{32,0},{64,32},{96,64},{1,97},{33,1},{65,33},{97,65},{2,98}... | collective-permute-start | bytes 2801672 | tf_op jit(solution)/shard_map/ppermute | solution.py:229
  121.6 45.8 %collective-permute-start.6 = (f32[608,384]{1,0:T(8,128)S(1)}, f32[608,384]{1,0:T(8,128)}, u32[]{:S(2)}, u32[]{:S(2)}) collective-permute-start(f32[608,384]{1,0:T(8,128)S(1)} %collective-permute-done.1.refs_1_), channel_id=1, source_target_pairs={{0,64},{32,96},{64,0},{96,32},{1,65},{33,97},{65,1},{97,33},{2,66}... | collective-permute-start | bytes 2801672 | tf_op jit(solution)/shard_map/ppermute | solution.py:229
  127.6 41.3 %collective-permute-start.7 = (f32[608,384]{1,0:T(8,128)S(1)}, f32[608,384]{1,0:T(8,128)}, u32[]{:S(2)}, u32[]{:S(2)}) collective-permute-start(f32[608,384]{1,0:T(8,128)S(1)} %collective-permute-done.1.refs_1_), channel_id=1, source_target_pairs={{0,32},{32,64},{64,96},{96,0},{1,33},{33,65},{65,97},{97,1},{2,34}... | collective-permute-start | bytes 2801672 | tf_op jit(solution)/shard_map/ppermute | solution.py:229
  176.3 10.8 %collective-permute-start.8 = (f32[24,128,256]{2,1,0:T(8,128)S(1)}, f32[24,128,256]{2,1,0:T(8,128)S(1)}, u32[]{:S(2)}, u32[]{:S(2)}) collective-permute-start(f32[24,128,256]{2,1,0:T(8,128)S(1)} %get-tuple-element.85), channel_id=1, source_target_pairs={{0,8},{8,0},{1,9},{9,1},{2,10},{10,2},{3,11},{11,3},{4,12},{12,4},... | collective-permute-start | bytes 9437192 | tf_op jit(solution)/shard_map/ppermute | solution.py:224

commit v6 on v5

--- a/solution.py
+++ b/solution.py
@@ -14,6 +14,7 @@
 ROWS = 32
 PIECE = 6
 PARTS = 2
+STRIP = 128
 UNROLL = 32
 VMEM_LIMIT = 32 * 1024 * 1024
 BLK = ("x", "zl", "core")
@@ -36,7 +37,11 @@
 def tile_kernel(live_ref, dst_hbm, src_hbm, out_ref, dst_ref, src_ref, tiles, edge_sems, sems):
     live = live_ref[0]
     groups = (live + ROWS - 1) // ROWS
-    node_ids = lax.broadcasted_iota(jnp.int32, (TILE, dst_ref.shape[1]), 0)
+    node_ids = lax.broadcasted_iota(jnp.int32, (TILE, dst_ref.shape[1]), 0).astype(jnp.float32).astype(jnp.bfloat16)
+    one, zero = jnp.ones((), jnp.bfloat16), jnp.zeros((), jnp.bfloat16)
+
+    def one_hot(ids):
+        return jnp.where(ids.astype(jnp.float32).astype(jnp.bfloat16) == node_ids, one, zero)
 
     def copies_in(group):
         at = pl.ds(pl.multiple_of(group * ROWS, ROWS), ROWS)
@@ -62,10 +67,11 @@
         src = src_ref[pl.ds(first, ROWS)]
         for k in range(ROWS):
             dst_ids = jnp.where(first + k < live, dst[k : k + 1], TILE)
-            dst_hot = (dst_ids == node_ids).astype(jnp.bfloat16)
-            src_hot = (src[k : k + 1] == node_ids).astype(jnp.bfloat16)
             counts = lax.dot_general(
-                dst_hot, src_hot, (((1,), (1,)), ((), ())), preferred_element_type=jnp.float32
+                one_hot(dst_ids),
+                one_hot(src[k : k + 1]),
+                (((1,), (1,)), ((), ())),
+                preferred_element_type=jnp.float32,
             )
             tiles[first + k] = counts.astype(jnp.bfloat16)
         copy_out(group).start()
@@ -97,7 +103,8 @@
 
 def aggregate_kernel(transpose, parts, targets, live_ref, pick_ref, place_ref, tiles_ref, *refs):
     sources, outs = refs[:parts], refs[parts : parts + targets]
-    split, totals, landed, tiles, sems, tile_sems = refs[parts + targets :]
+    split, landed, tiles, sems, tile_sems, *more = refs[parts + targets :]
+    totals = more[0] if more else outs[0]
     groups = (live_ref[0] + UNROLL - 1) // UNROLL
 
     def tile_copy(group):
@@ -150,9 +157,10 @@
         return carry
 
     lax.fori_loop(0, groups, some_tiles, 0)
-    for p, out_ref in enumerate(outs):
-        count = out_ref.shape[0]
-        out_ref[...] = totals[p * count : (p + 1) * count]
+    if more:
+        for p, out_ref in enumerate(outs):
+            count = out_ref.shape[0]
+            out_ref[...] = totals[p * count : (p + 1) * count]
 
 
 def aggregate(tiles, live, pick_ids, place_ids, sources, target_blocks, transpose):
@@ -166,12 +174,12 @@
         out_shape=[pltpu.VMEM((b, TILE, width), jnp.float32) for b in target_blocks],
         scratch_shapes=[
             pltpu.VMEM((parts * source_blocks, 2 * TILE, width), jnp.bfloat16),
-            pltpu.VMEM((sum(target_blocks), TILE, width), jnp.float32),
             pltpu.VMEM((parts * source_blocks, TILE, width), jnp.float32),
             pltpu.VMEM(tiles.shape, jnp.bfloat16),
             pltpu.SemaphoreType.DMA((parts * source_blocks // PIECE,)),
             pltpu.SemaphoreType.DMA((slots // UNROLL,)),
-        ],
+        ]
+        + [pltpu.VMEM((sum(target_blocks), TILE, width), jnp.float32)] * (targets > 1),
         compiler_params=pltpu.CompilerParams(vmem_limit_bytes=VMEM_LIMIT),
         cost_estimate=pl.CostEstimate(
             flops=10**6, bytes_accessed=10**5, transcendentals=0
@@ -179,8 +187,34 @@
     )(live, pick_ids, place_ids, in_hbm(tiles), *sources)
 
 
+def activate_kernel(parts_ref, scaled_ref, cotangent_ref, scales_ref, hidden_ref, back_ref):
+    scales = jnp.concatenate([scales_ref[...]] * (hidden_ref.shape[1] // TILE), axis=1)
+    pre = (parts_ref[...].sum(0) + scaled_ref[...]) * scales
+    hidden, pull = jax.vjp(activation, pre)
+    hidden_ref[...] = hidden
+    back_ref[...] = pull(cotangent_ref[...])[0] * scales
+
+
+def activate(parts, scaled, cotangent, scales):
+    count, rows, width = parts.shape
+    block = pl.BlockSpec((STRIP, width), lambda g: (g, 0))
+    return pl.pallas_call(
+        activate_kernel,
+        grid=(rows // STRIP,),
+        in_specs=[
+            pl.BlockSpec((count, STRIP, width), lambda g: (0, g, 0)),
+            block,
+            block,
+            pl.BlockSpec((STRIP, TILE), lambda g: (g, 0)),
+        ],
+        out_specs=[block, block],
+        out_shape=[jax.ShapeDtypeStruct((rows, width), jnp.float32)] * 2,
+        compiler_params=pltpu.CompilerParams(vmem_limit_bytes=VMEM_LIMIT),
+    )(parts, scaled, cotangent, scales)
+
+
 def gradient_kernel(*refs):
-    features, (rows_ref, out_ref) = refs[:-2], refs[-2:]
+    features, (core_ref, rows_ref, mine_ref, other_ref, out_ref) = refs[:-5], refs[-5:]
     height, nodes = features[0].shape
     blocks = PARTS * nodes // TILE
     width = out_ref.shape[1]
@@ -196,20 +230,24 @@
         low = (part - high.astype(jnp.float32)).astype(jnp.bfloat16)
         left = jnp.concatenate([high, high, low], axis=1)
         out_ref[:height] += jnp.dot(left, right, preferred_element_type=jnp.float32)
-
-
-def gradient(features, rows, out_rows):
+    half = mine_ref.shape[0]
+    mine_ref[...] = out_ref[pl.ds(pl.multiple_of(core_ref[0] * half, half), half)]
+    other_ref[...] = out_ref[pl.ds(pl.multiple_of((1 - core_ref[0]) * half, half), half)]
+
+
+def gradient(features, core, rows, out_rows):
     width = rows.shape[2]
     return pl.pallas_call(
         gradient_kernel,
-        in_specs=[VMEM] * (len(features) + 1),
-        out_specs=VMEM,
-        out_shape=pltpu.VMEM((out_rows, width), jnp.float32),
+        in_specs=[VMEM] * len(features) + [SMEM, VMEM],
+        out_specs=[VMEM] * 2,
+        out_shape=[pltpu.VMEM((out_rows // 2, width), jnp.float32)] * 2,
+        scratch_shapes=[pltpu.VMEM((out_rows, width), jnp.float32)],
         compiler_params=pltpu.CompilerParams(vmem_limit_bytes=VMEM_LIMIT),
         cost_estimate=pl.CostEstimate(
             flops=6 * out_rows * rows.shape[0] * TILE * width, bytes_accessed=10**7, transcendentals=0
         ),
-    )(*[in_vmem(f) for f in features], in_vmem(rows))
+    )(*[in_vmem(f) for f in features], core.reshape(1), in_vmem(rows))
 
 
 def exchange(value, axes):
@@ -229,14 +267,16 @@
     return lax.ppermute(value, axis, [(i, (i - steps) % size) for i in range(size)])
 
 
-def sum_everywhere(value):
-    rows, width = value.shape
-    parts = lax.axis_size(BLK)
-    part_rows = -(-rows // (8 * parts)) * 8
-    value = jnp.pad(value, ((0, part_rows * parts - rows), (0, 0)))
-    own = exchange(value.reshape(parts, part_rows, width), BLK).sum(0)
+def sum_everywhere(mine, other):
+    rows, width = mine.shape
+    mine = mine + swap(other, "core")
+    own = exchange(mine.reshape(-1, rows // lax.axis_size(("x", "zl")), width), ("x", "zl")).sum(0)
     own = gather(own, REP).sum(0)
-    return gather(own, BLK).reshape(-1, width)[:rows]
+    mine = gather(own, ("x", "zl")).reshape(rows, width)
+    other = swap(mine, "core")
+    return jnp.where(
+        lax.axis_index("core") == 0, jnp.concatenate([mine, other]), jnp.concatenate([other, mine])
+    )
 
 
 def local(features, weight, cotangent, degree, tile_row, tile_col, edge_dst, edge_src, tile_live):
@@ -260,7 +300,8 @@
     scaled = jnp.dot(features, weight, precision=HIGH, preferred_element_type=jnp.float32) * scales
     height = -(-in_width // 32) * 32
     here = jnp.pad(features.T * scales.T, ((0, height - in_width), (0, 0)))
-    scaled, here = lax.optimization_barrier((scaled, here))
+    wide_scales = jnp.broadcast_to(scales, (own_rows, TILE))
+    scaled, here, wide_scales = lax.optimization_barrier((scaled, here, wide_scales))
     near = gather(scaled, ("x", "zl"))
     here, near = lax.optimization_barrier((here, near))
     far = swap(near, "core")
@@ -268,17 +309,15 @@
     here_x = [from_ahead(here, "x", steps) for steps in (1, 2, 3)]
     tiles = build_tiles(live, edge_dst.reshape(slots, edges), edge_src.reshape(slots, edges))
 
-    def forward(near, far, scaled, cotangent):
+    def forward(near, far, scaled, cotangent, wide_scales):
         sources = [near.reshape(blocks), far.reshape(blocks)]
         (sums,) = aggregate(tiles, live, from_ids, row_ids, sources, [group_blocks], False)
-        own_sums = exchange(sums.reshape(-1, own_rows, hidden_width), REP).sum(0)
-        hidden, pull = jax.vjp(activation, (own_sums + scaled) * scales)
-        return hidden, pull(cotangent)[0] * scales
-
-    def never(near, far, scaled, cotangent):
+        return activate(exchange(sums.reshape(-1, own_rows, hidden_width), REP), scaled, cotangent, wide_scales)
+
+    def never(near, far, scaled, cotangent, wide_scales):
         return scaled + cotangent, scaled - cotangent
 
-    hidden, back_own = lax.cond(live[0] > 0, forward, never, near, far, scaled, cotangent)
+    hidden, back_own = lax.cond(live[0] > 0, forward, never, near, far, scaled, cotangent, wide_scales)
     across, here_x, back_own = lax.optimization_barrier((across, here_x, back_own))
     across_x = [from_ahead(across, "x", steps) for steps in (1, 2, 3)]
     back_group = lax.cond(
@@ -296,7 +335,8 @@
     held = [part for pair in zip([here, *here_x], [across, *across_x]) for part in pair]
     parts = lax.axis_size(BLK)
     out_rows = -(-in_width // (8 * parts)) * 8 * parts
-    return (hidden, sum_everywhere(gradient(held, kept, out_rows))[:in_width])
+    halves = gradient(held, lax.axis_index("core"), kept, out_rows)
+    return (hidden, sum_everywhere(*halves)[:in_width])
 
 
 def solution(mesh):

time: 242 us -> 231 us (0.955)
  starting transfers between devices: 18.2 us -> 12.1 us
  other arithmetic: 8.94 us -> 3.49 us
  blocking collectives: 172 us -> 168 us
  Pallas kernels: 27.7 us -> 31.3 us
    ppermute x6, starting transfers between devices: 9.69 us -> 4.51 us  [from_ahead(): lax.ppermute(value, axis, [(i, (i - steps) % size) for i in range(size)])]
    all_to_all x6, blocking collectives: 172 us -> 168 us  [exchange(): return lax.all_to_all(value, axes, 0, 0, tiled=True)]
    ppermute x3 -> x5, waiting for transfers between devices: 5.29 us -> 8.4 us  [swap(): return lax.ppermute(value, axis, [(0, 1), (1, 0)])]
    reduce_sum x2 -> x1, other arithmetic: 2.92 us -> 0.02 us  [sum_everywhere(): exchange(mine.reshape(-1, rows // lax.axis_size(('x', 'zl')), width), ('x...]
    mul x1 -> x0, other arithmetic: 2.48 us -> none  [forward(): return (hidden, pull(cotangent)[0] * scales)]
    pallas_call x1 -> x2, Pallas kernels: 5.37 us -> 7.2 us  [the longest x1 5.41 us: gradient(): pl.pallas_call(gradient_kernel, in_specs=[VMEM] * len(features) + [SMEM,...]
    ppermute x3 -> x5, starting transfers between devices: 8.53 us -> 7.55 us  [swap(): return lax.ppermute(value, axis, [(0, 1), (1, 0)])]
  transfers between devices with their start and end apart: 9 -> 11, of which waited for: 2 -> 3; matrix products, arithmetic and copies ran while one was open for 3% -> 1% of each run, Pallas kernels for 6% -> 8%
where the time goes in v6:
time: 231 us
  blocking collectives  168 us (73%)
  Pallas kernels  31.3 us (14%)
  starting transfers between devices  12.1 us (5%)
  waiting for transfers between devices  8.42 us (4%)
  other arithmetic  3.49 us (2%)
  local copies, waits for them, and re-layouts  3.23 us (1%)
  matrix products  2.92 us (1%)
    all_to_all x6, blocking collectives, exchange(): return lax.all_to_all(value, axes, 0, 0, tiled=True)  168 us
    pallas_call x2, Pallas kernels, aggregate(): pl.pallas_call(partial(aggregate_kernel, transpose, parts, targets), in_s...  17.7 us
    ppermute x5, waiting for transfers between devices, swap(): return lax.ppermute(value, axis, [(0, 1), (1, 0)])  8.4 us
    ppermute x5, starting transfers between devices, swap(): return lax.ppermute(value, axis, [(0, 1), (1, 0)])  7.55 us
    pallas_call x1, Pallas kernels, build_tiles(): pl.pallas_call(tile_kernel, in_specs=[SMEM, ANY, ANY], out_specs=ANY, out...  6.4 us
    pallas_call x1, Pallas kernels, gradient(): pl.pallas_call(gradient_kernel, in_specs=[VMEM] * len(features) + [SMEM,...  5.41 us
  transfers between devices with their start and end apart: 11, of which 3 were waited for; matrix products, arithmetic and copies ran while one was open for 1% of the time, Pallas kernels for 8%

profile of v6, /device:TPU:1, one launch (start us, length us, event | category | flops | bytes accessed | tf_op | source)
XLA Modules:
  0.0 231.5 jit_solution(17775509178617442305)
XLA Ops:
  1.4 1.3 multiply_bitcast_fusion
  2.7 2.9 %convolution_multiply_fusion = f32[384,256]{1,0:T(8,128)S(1)} fusion(f32[384,602]{0,1:T(8,128)} %param.13, f32[602,256]{1,0:T(8,128)S(1)} %copy-done, f32[384]{0:T(512)S(1)} %convert_rsqrt_fusion), kind=kOutput, calls=%fused_computation.2 | convolution fusion | flops 710246400 | bytes 1935872 | tf_op jit(solution)/shard_map/dot_general | solution.py:300
  6.7 43.2 %all_to_all.30 = f32[8,384,256]{2,1,0:T(8,128)} all-to-all(f32[8,384,256]{2,1,0:T(8,128)S(1)} %broadcast_in_dim.22), channel_id=1, replica_groups=mesh['x'=4,'zl'=2,'core'=2,'y'=4,'zh'=2] {'x','zl'}, dimensions={0} | all-to-all | bytes 6291456 | tf_op jit(solution)/shard_map/all_to_all | solution.py:254
  49.9 1.9 collective-permute-start
  51.8 1.2 collective-permute-start.1
  53.9 1.2 collective-permute-start.3
  55.8 6.4 %shard_map.104.tiles_ref = bf16[256,128,128]{2,1,0:T(8,128)(2,1)} custom-call(s32[1]{0:T(128)} %bitcast.19.live_ref, s32[256,256]{1,0:T(8,128)} %bitcast.27, s32[256,256]{1,0:T(8,128)} %bitcast.28), custom_call_target="tpu_custom_call" | custom-call | flops 1000000 | bytes 100000 | tf_op jit(solution)/shard_map/pallas_call | solution.py:87
  62.4 62.0 %conditional.2 = ((f32[384,256]{1,0:T(8,128)}, f32[384,256]{1,0:T(8,128)})) conditional(s32[]{:T(128)} %bitcast.3, (f32[384,256]{1,0:T(8,128)S(1)}, f32[384,256]{1,0:T(8,128)S(1)}) %tuple.45, (s32[256]{0:T(256)S(1)}, s32[256]{0:T(256)S(1)}, s32[256]{0:T(256)S(1)}, f32[8,384,256]{2,1,0:T(8,128)}, f32[8,384,256]{2,1,0:T(8,128)}, /*index=5*/s32[1]{0:T(128)}, ...), branch_computations={%region_0.1_spmd, %region_1.2_spmd} | conditional | flops 1000768 | bytes 13473588 | solution.py:320
  63.1 9.3 %branch_1_fun.2 = f32[24,128,256]{2,1,0:T(8,128)S(1)} custom-call(s32[1]{0:T(128)} %get-tuple-element.38.live_ref, s32[256]{0:T(256)S(1)} %add_add_fusion.pick_ref, s32[256]{0:T(256)S(1)} %get-tuple-element.42.place_ref, bf16[256,128,128]{2,1,0:T(8,128)(2,1)} %get-tuple-element.43.tiles_ref, f32[24,128,256]{2,1,0:T(8,128)} %bitcast.refs_0_, ...), custom_call_target="tpu_custom_call" | custom-call | flops 1000000 | bytes 100000 | tf_op jit(solution)/shard_map/cond/branch_1_fun/pallas_call | solution.py:170
  72.5 50.0 %all_to_all.28.parts_ref = f32[8,384,256]{2,1,0:T(8,128)S(1)} all-to-all(f32[8,384,256]{2,1,0:T(8,128)S(1)} %bitcast.21), channel_id=1, replica_groups=mesh['x'=4,'zl'=2,'core'=2,'y'=4,'zh'=2] {'y','zh'}, dimensions={0} | all-to-all | bytes 6291456 | tf_op jit(solution)/shard_map/cond/branch_1_fun/all_to_all | solution.py:254
  122.5 1.8 branch_1_fun.3
  124.4 1.3 collective-permute-start.5
  126.8 43.3 %conditional.3 = (f32[8,384,256]{2,1,0:T(8,128)}) conditional(s32[]{:T(128)} %bitcast.3, f32[384,256]{1,0:T(8,128)} %get-tuple-element.80, f32[384,256]{1,0:T(8,128)} %get-tuple-element.80), branch_computations={%region_2.3_spmd, %region_3.4_spmd} | conditional | bytes 9830408 | solution.py:323
  126.8 1.3 broadcast_in_dim.4
  128.0 42.0 %all_to_all.29 = f32[8,384,256]{2,1,0:T(8,128)} all-to-all(f32[8,384,256]{2,1,0:T(8,128)S(1)} %broadcast_in_dim.4), channel_id=1, replica_groups=mesh['x'=4,'zl'=2,'core'=2,'y'=4,'zh'=2] {'y','zh'}, dimensions={0} | all-to-all | bytes 6291456 | tf_op jit(solution)/shard_map/cond/branch_1_fun/all_to_all | solution.py:254
  170.0 8.3 %shard_map.105 = (f32[24,128,256]{2,1,0:T(8,128)S(1)}, f32[24,128,256]{2,1,0:T(8,128)S(1)}) custom-call(s32[1]{0:T(128)} %bitcast.20.live_ref, s32[256]{0:T(256)S(1)} %bitcast.30, s32[256]{0:T(256)S(1)} %get-tuple-element.91.place_ref, bf16[256,128,128]{2,1,0:T(8,128)(2,1)} %shard_map.104.tiles_ref, f32[24,128,256]{2,1,0:T(8,128)} %bitcast.22), custom_call_target="tpu_custom_call" | custom-call | flops 1000000 | bytes 100000 | tf_op jit(solution)/shard_map/pallas_call | solution.py:170
  178.7 5.6 %collective-permute-done.8 = f32[24,128,256]{2,1,0:T(8,128)S(1)} collective-permute-done((f32[24,128,256]{2,1,0:T(8,128)S(1)}, f32[24,128,256]{2,1,0:T(8,128)S(1)}, u32[]{:S(2)}, u32[]{:S(2)}) %collective-permute-start.8) | collective-permute-done | bytes 3145760 | tf_op jit(solution)/shard_map/ppermute | solution.py:262
  184.8 5.4 %shard_map.106 = (f32[320,256]{1,0:T(8,128)S(1)}, f32[320,256]{1,0:T(8,128)S(1)}) custom-call(f32[608,384]{1,0:T(8,128)S(1)} %pad.8.refs_0_, f32[608,384]{1,0:T(8,128)S(1)} %collective-permute-done.1.refs_1_, f32[608,384]{1,0:T(8,128)S(1)} %collective-permute-done.2.refs_2_, f32[608,384]{1,0:T(8,128)} %collective-permute-done.5.refs_3_, ...), custom_call_target="tpu_custom_call" | custom-call | flops 3019898880 | bytes 10000000 | tf_op jit(solution)/shard_map/pallas_call | solution.py:240
  190.4 1.5 collective-permute-done.9
  191.9 13.8 %all_to_all.31 = f32[8,40,256]{2,1,0:T(8,128)S(1)} all-to-all(f32[8,40,256]{2,1,0:T(8,128)S(1)} %bitcast.26), channel_id=1, replica_groups=mesh['x'=4,'zl'=2,'core'=2,'y'=4,'zh'=2] {'x','zl'}, dimensions={0} | all-to-all | bytes 655360 | tf_op jit(solution)/shard_map/all_to_all | solution.py:254
  205.8 10.4 %all_to_all.32 = f32[8,40,256]{2,1,0:T(8,128)S(1)} all-to-all(f32[8,40,256]{2,1,0:T(8,128)S(1)} %broadcast_in_dim.23), channel_id=1, replica_groups=mesh['x'=4,'zl'=2,'core'=2,'y'=4,'zh'=2] {'y','zh'}, dimensions={0} | all-to-all | bytes 655360 | tf_op jit(solution)/shard_map/all_to_all | solution.py:254
  216.2 9.1 %all_to_all.33 = f32[8,40,256]{2,1,0:T(8,128)S(1)} all-to-all(f32[8,40,256]{2,1,0:T(8,128)S(1)} %broadcast_in_dim.24), channel_id=1, replica_groups=mesh['x'=4,'zl'=2,'core'=2,'y'=4,'zh'=2] {'x','zl'}, dimensions={0} | all-to-all | bytes 655360 | tf_op jit(solution)/shard_map/all_to_all | solution.py:254
  225.3 4.0 %collective-permute-start.10 = (f32[320,256]{1,0:T(8,128)S(1)}, f32[320,256]{1,0:T(8,128)S(1)}, u32[]{:S(2)}, u32[]{:S(2)}) collective-permute-start(f32[320,256]{1,0:T(8,128)S(1)} %bitcast.24), channel_id=1, source_target_pairs={{0,8},{8,0},{1,9},{9,1},{2,10},{10,2},{3,11},{11,3},{4,12},{12,4},... | collective-permute-start | bytes 983048 | tf_op jit(solution)/shard_map/ppermute | solution.py:262
  229.4 1.3 collective-permute-done.10
  (54 shorter events, 6.7 us)
Async XLA Ops:
  0.6 2.0 copy-start
  5.6 48.3 %copy-start.2 = (f32[384,256]{1,0:T(8,128)}, f32[384,256]{1,0:T(8,128)S(1)}, u32[]{:S(2)}) copy-start(f32[384,256]{1,0:T(8,128)S(1)} %convolution_multiply_fusion) | copy-start | bytes 1179652
  49.9 12.4 %collective-permute-start = (f32[8,384,256]{2,1,0:T(8,128)}, f32[8,384,256]{2,1,0:T(8,128)}, u32[]{:S(2)}, u32[]{:S(2)}) collective-permute-start(f32[8,384,256]{2,1,0:T(8,128)} %all_to_all.30), channel_id=1, source_target_pairs={{0,8},{8,0},{1,9},{9,1},{2,10},{10,2},{3,11},{11,3},{4,12},{12,4},... | collective-permute-start | bytes 9437192 | tf_op jit(solution)/shard_map/ppermute | solution.py:262
  51.8 72.5 %collective-permute-start.1 = (f32[608,384]{1,0:T(8,128)S(1)}, f32[608,384]{1,0:T(8,128)S(1)}, u32[]{:S(2)}, u32[]{:S(2)}) collective-permute-start(f32[608,384]{1,0:T(8,128)S(1)} %pad.8.refs_0_), channel_id=1, source_target_pairs={{0,16},{16,0},{1,17},{17,1},{2,18},{18,2},{3,19},{19,3},{4,20},{20... | collective-permute-start | bytes 2801672 | tf_op jit(solution)/shard_map/ppermute | solution.py:262
  53.0 71.4 %collective-permute-start.2 = (f32[608,384]{1,0:T(8,128)S(1)}, f32[608,384]{1,0:T(8,128)S(1)}, u32[]{:S(2)}, u32[]{:S(2)}) collective-permute-start(f32[608,384]{1,0:T(8,128)S(1)} %pad.8.refs_0_), channel_id=1, source_target_pairs={{0,96},{32,0},{64,32},{96,64},{1,97},{33,1},{65,33},{97,65},{2,98}... | collective-permute-start | bytes 2801672 | tf_op jit(solution)/shard_map/ppermute | solution.py:267
  53.9 70.5 %collective-permute-start.3 = (f32[608,384]{1,0:T(8,128)S(1)}, f32[608,384]{1,0:T(8,128)}, u32[]{:S(2)}, u32[]{:S(2)}) collective-permute-start(f32[608,384]{1,0:T(8,128)S(1)} %pad.8.refs_0_), channel_id=1, source_target_pairs={{0,64},{32,96},{64,0},{96,32},{1,65},{33,97},{65,1},{97,33},{2,66}... | collective-permute-start | bytes 2801672 | tf_op jit(solution)/shard_map/ppermute | solution.py:267
  55.1 69.3 %collective-permute-start.4 = (f32[608,384]{1,0:T(8,128)S(1)}, f32[608,384]{1,0:T(8,128)}, u32[]{:S(2)}, u32[]{:S(2)}) collective-permute-start(f32[608,384]{1,0:T(8,128)S(1)} %pad.8.refs_0_), channel_id=1, source_target_pairs={{0,32},{32,64},{64,96},{96,0},{1,33},{33,65},{65,97},{97,1},{2,34}... | collective-permute-start | bytes 2801672 | tf_op jit(solution)/shard_map/ppermute | solution.py:267
  55.8 6.5 %copy-start.11 = (s32[1,1,256]{2,1,0:T(1,128)S(1)}, s32[1,1,256]{2,1,0:T(1,128)}, u32[]{:S(2)}) copy-start(s32[1,1,256]{2,1,0:T(1,128)} %param.18) | copy-start | bytes 3076
  55.8 6.6 %copy-start.3 = (f32[384,256]{1,0:T(8,128)S(1)}, f32[384,256]{1,0:T(8,128)}, u32[]{:S(2)}) copy-start(f32[384,256]{1,0:T(8,128)} %copy-done.2) | copy-start | bytes 1179652
  55.8 6.6 %copy-start.6 = (f32[384,256]{1,0:T(8,128)S(1)}, f32[384,256]{1,0:T(8,128)}, u32[]{:S(2)}) copy-start(f32[384,256]{1,0:T(8,128)} %param.15) | copy-start | bytes 1179652
  55.8 6.5 %copy-start.10 = (s32[1,1,256]{2,1,0:T(1,128)S(1)}, s32[1,1,256]{2,1,0:T(1,128)}, u32[]{:S(2)}) copy-start(s32[1,1,256]{2,1,0:T(1,128)} %param.17) | copy-start | bytes 3076
  62.4 0.7 copy-start.4
  62.4 10.1 %copy-start.7 = (f32[384,256]{1,0:T(8,128)}, f32[384,256]{1,0:T(8,128)S(1)}, u32[]{:S(2)}) copy-start(f32[384,256]{1,0:T(8,128)S(1)} %get-tuple-element.47.cotangent_ref) | copy-start | bytes 1179652 | tf_op jit(solution)/shard_map/cond
  72.5 50.0 %copy-start.5 = (f32[384,256]{1,0:T(8,128)S(1)}, f32[384,256]{1,0:T(8,128)}, u32[]{:S(2)}) copy-start(f32[384,256]{1,0:T(8,128)} %copy-done.4) | copy-start | bytes 1179652 | tf_op jit(solution)/shard_map/cond
  72.5 50.0 %copy-start.8 = (f32[384,256]{1,0:T(8,128)S(1)}, f32[384,256]{1,0:T(8,128)}, u32[]{:S(2)}) copy-start(f32[384,256]{1,0:T(8,128)} %copy-done.7) | copy-start | bytes 1179652 | tf_op jit(solution)/shard_map/cond
  72.5 50.0 %copy-start.9 = (f32[384,128]{1,0:T(8,128)S(1)}, f32[384,128]{1,0:T(8,128)}, u32[]{:S(2)}) copy-start(f32[384,128]{1,0:T(8,128)} %get-tuple-element.48.scales_ref) | copy-start | bytes 589828 | tf_op jit(solution)/shard_map/cond
  124.4 45.7 %collective-permute-start.5 = (f32[608,384]{1,0:T(8,128)S(1)}, f32[608,384]{1,0:T(8,128)}, u32[]{:S(2)}, u32[]{:S(2)}) collective-permute-start(f32[608,384]{1,0:T(8,128)S(1)} %collective-permute-done.1.refs_1_), channel_id=1, source_target_pairs={{0,96},{32,0},{64,32},{96,64},{1,97},{33,1},{65,33},{97,65},{2,98}... | collective-permute-start | bytes 2801672 | tf_op jit(solution)/shard_map/ppermute | solution.py:267
  125.7 44.3 %collective-permute-start.6 = (f32[608,384]{1,0:T(8,128)S(1)}, f32[608,384]{1,0:T(8,128)}, u32[]{:S(2)}, u32[]{:S(2)}) collective-permute-start(f32[608,384]{1,0:T(8,128)S(1)} %collective-permute-done.1.refs_1_), channel_id=1, source_target_pairs={{0,64},{32,96},{64,0},{96,32},{1,65},{33,97},{65,1},{97,33},{2,66}... | collective-permute-start | bytes 2801672 | tf_op jit(solution)/shard_map/ppermute | solution.py:267
  126.0 44.0 %collective-permute-start.7 = (f32[608,384]{1,0:T(8,128)S(1)}, f32[608,384]{1,0:T(8,128)}, u32[]{:S(2)}, u32[]{:S(2)}) collective-permute-start(f32[608,384]{1,0:T(8,128)S(1)} %collective-permute-done.1.refs_1_), channel_id=1, source_target_pairs={{0,32},{32,64},{64,96},{96,0},{1,33},{33,65},{65,97},{97,1},{2,34}... | collective-permute-start | bytes 2801672 | tf_op jit(solution)/shard_map/ppermute | solution.py:267
  170.0 14.3 %copy-start.1 = (f32[384,256]{1,0:T(8,128)S(1)}, f32[384,256]{1,0:T(8,128)}, u32[]{:S(2)}) copy-start(f32[384,256]{1,0:T(8,128)} %get-tuple-element.80) | copy-start | bytes 1179652
  178.4 5.9 %collective-permute-start.8 = (f32[24,128,256]{2,1,0:T(8,128)S(1)}, f32[24,128,256]{2,1,0:T(8,128)S(1)}, u32[]{:S(2)}, u32[]{:S(2)}) collective-permute-start(f32[24,128,256]{2,1,0:T(8,128)S(1)} %get-tuple-element.88), channel_id=1, source_target_pairs={{0,8},{8,0},{1,9},{9,1},{2,10},{10,2},{3,11},{11,3},{4,12},{12,4},... | collective-permute-start | bytes 9437192 | tf_op jit(solution)/shard_map/ppermute | solution.py:262
  190.2 1.7 collective-permute-start.9
  225.3 5.3 %collective-permute-start.10 = (f32[320,256]{1,0:T(8,128)S(1)}, f32[320,256]{1,0:T(8,128)S(1)}, u32[]{:S(2)}, u32[]{:S(2)}) collective-permute-start(f32[320,256]{1,0:T(8,128)S(1)} %bitcast.24), channel_id=1, source_target_pairs={{0,8},{8,0},{1,9},{9,1},{2,10},{10,2},{3,11},{11,3},{4,12},{12,4},... | collective-permute-start | bytes 983048 | tf_op jit(solution)/shard_map/ppermute | solution.py:262

commit v7 on v6

--- a/solution.py
+++ b/solution.py
@@ -12,8 +12,9 @@
 HIGH = lax.Precision.HIGHEST
 activation = partial(jax.nn.gelu, approximate=True)
 ROWS = 32
-PIECE = 6
+PIECE = 3
 PARTS = 2
+AHEAD = 2
 STRIP = 128
 UNROLL = 32
 VMEM_LIMIT = 32 * 1024 * 1024
@@ -41,7 +42,8 @@
     one, zero = jnp.ones((), jnp.bfloat16), jnp.zeros((), jnp.bfloat16)
 
     def one_hot(ids):
-        return jnp.where(ids.astype(jnp.float32).astype(jnp.bfloat16) == node_ids, one, zero)
+        hot = ids.astype(jnp.float32).astype(jnp.bfloat16) == node_ids
+        return jnp.where(hot, one, zero).astype(jnp.float8_e4m3fn)
 
     def copies_in(group):
         at = pl.ds(pl.multiple_of(group * ROWS, ROWS), ROWS)
@@ -101,7 +103,7 @@
     )(live, in_hbm(edge_dst), in_hbm(edge_src))
 
 
-def aggregate_kernel(transpose, parts, targets, live_ref, pick_ref, place_ref, tiles_ref, *refs):
+def aggregate_kernel(parts, targets, transpose, live_ref, pick_ref, place_ref, own_ref, tiles_ref, *refs):
     sources, outs = refs[:parts], refs[parts : parts + targets]
     split, landed, tiles, sems, tile_sems, *more = refs[parts + targets :]
     totals = more[0] if more else outs[0]
@@ -121,11 +123,17 @@
         )
         copy.start()
         copies.append(copy)
-    lax.fori_loop(0, groups, lambda group, carry: (tile_copy(group).start(), carry)[1], 0)
+    for group in range(AHEAD):
+        pl.when(group < groups)(tile_copy(group).start)
     totals[...] = jnp.zeros_like(totals)
 
     for n, copy in enumerate(copies):
         copy.wait()
+        if not transpose:
+
+            @pl.when(own_ref[1] == n * PIECE)
+            def _():
+                totals[pl.ds(own_ref[0], PIECE)] = landed[n * PIECE : (n + 1) * PIECE]
 
         def split_block(k, carry):
             value = landed[n * PIECE + k]
@@ -138,6 +146,7 @@
 
     def some_tiles(group, carry):
         tile_copy(group).wait()
+        pl.when(group + AHEAD < groups)(lambda: tile_copy(group + AHEAD).start())
         first = group * UNROLL
         products = []
         for k in range(UNROLL):
@@ -163,13 +172,13 @@
             out_ref[...] = totals[p * count : (p + 1) * count]
 
 
-def aggregate(tiles, live, pick_ids, place_ids, sources, target_blocks, transpose):
+def aggregate(tiles, live, pick_ids, place_ids, own, sources, target_blocks, transpose):
     slots = tiles.shape[0]
     source_blocks, _, width = sources[0].shape
     parts, targets = len(sources), len(target_blocks)
     return pl.pallas_call(
-        partial(aggregate_kernel, transpose, parts, targets),
-        in_specs=[SMEM] * 3 + [ANY] * (1 + parts),
+        partial(aggregate_kernel, parts, targets, transpose),
+        in_specs=[SMEM] * 4 + [ANY] * (1 + parts),
         out_specs=[VMEM] * targets,
         out_shape=[pltpu.VMEM((b, TILE, width), jnp.float32) for b in target_blocks],
         scratch_shapes=[
@@ -184,18 +193,18 @@
         cost_estimate=pl.CostEstimate(
             flops=10**6, bytes_accessed=10**5, transcendentals=0
         ),
-    )(live, pick_ids, place_ids, in_hbm(tiles), *sources)
-
-
-def activate_kernel(parts_ref, scaled_ref, cotangent_ref, scales_ref, hidden_ref, back_ref):
+    )(live, pick_ids, place_ids, own, in_hbm(tiles), *sources)
+
+
+def activate_kernel(parts_ref, cotangent_ref, scales_ref, hidden_ref, back_ref):
     scales = jnp.concatenate([scales_ref[...]] * (hidden_ref.shape[1] // TILE), axis=1)
-    pre = (parts_ref[...].sum(0) + scaled_ref[...]) * scales
+    pre = parts_ref[...].sum(0) * scales
     hidden, pull = jax.vjp(activation, pre)
     hidden_ref[...] = hidden
     back_ref[...] = pull(cotangent_ref[...])[0] * scales
 
 
-def activate(parts, scaled, cotangent, scales):
+def activate(parts, cotangent, scales):
     count, rows, width = parts.shape
     block = pl.BlockSpec((STRIP, width), lambda g: (g, 0))
     return pl.pallas_call(
@@ -204,31 +213,86 @@
         in_specs=[
             pl.BlockSpec((count, STRIP, width), lambda g: (0, g, 0)),
             block,
-            block,
             pl.BlockSpec((STRIP, TILE), lambda g: (g, 0)),
         ],
         out_specs=[block, block],
         out_shape=[jax.ShapeDtypeStruct((rows, width), jnp.float32)] * 2,
         compiler_params=pltpu.CompilerParams(vmem_limit_bytes=VMEM_LIMIT),
-    )(parts, scaled, cotangent, scales)
-
-
-def gradient_kernel(*refs):
-    features, (core_ref, rows_ref, mine_ref, other_ref, out_ref) = refs[:-5], refs[-5:]
+    )(parts, cotangent, scales)
+
+
+def project_kernel(features_ref, weight_ref, degree_ref, scaled_ref, turned_ref, scales_ref, padded):
+    height, in_width = turned_ref.shape[0], features_ref.shape[0]
+    scales = lax.rsqrt(degree_ref[...].astype(jnp.float32))
+    turned_ref[:in_width] = features_ref[...] * scales
+    turned_ref[in_width:] = jnp.zeros((height - in_width, turned_ref.shape[1]), jnp.float32)
+    padded[:in_width] = weight_ref[...]
+    padded[in_width:] = jnp.zeros((height - in_width, padded.shape[1]), jnp.float32)
+    left_high, left_low = two_terms(turned_ref[...])
+    right_high, right_low = two_terms(padded[...])
+    scaled_ref[...] = lax.dot_general(
+        jnp.concatenate([left_high, left_high, left_low]),
+        jnp.concatenate([right_high, right_low, right_high]),
+        (((0,), (0,)), ((), ())),
+        preferred_element_type=jnp.float32,
+    )
+    scales_ref[...] = jnp.broadcast_to(scales, (TILE, scales.shape[1])).T
+
+
+def two_terms(value):
+    high = value.astype(jnp.bfloat16)
+    return high, (value - high.astype(jnp.float32)).astype(jnp.bfloat16)
+
+
+def project(features, weight, degree, height):
+    in_width, rows = features.shape
+    width = weight.shape[1]
+    return pl.pallas_call(
+        project_kernel,
+        in_specs=[VMEM] * 3,
+        out_specs=[VMEM] * 3,
+        out_shape=[
+            jax.ShapeDtypeStruct((rows, width), jnp.float32),
+            jax.ShapeDtypeStruct((height, rows), jnp.float32),
+            jax.ShapeDtypeStruct((rows, TILE), jnp.float32),
+        ],
+        scratch_shapes=[pltpu.VMEM((height, width), jnp.float32)],
+        compiler_params=pltpu.CompilerParams(vmem_limit_bytes=VMEM_LIMIT),
+    )(features, weight, degree.reshape(1, rows))
+
+
+def split_features_kernel(*refs):
+    features, (high_ref, low_ref) = refs[:-2], refs[-2:]
+    nodes = features[0].shape[1]
+    for p, part_ref in enumerate(features):
+        at = pl.ds(p % PARTS * nodes, nodes)
+        high, low = two_terms(part_ref[...])
+        high_ref[p // PARTS, :, at] = high
+        low_ref[p // PARTS, :, at] = low
+
+
+def split_features(features):
     height, nodes = features[0].shape
-    blocks = PARTS * nodes // TILE
-    width = out_ref.shape[1]
+    shape = (len(features) // PARTS, height, PARTS * nodes)
+    return pl.pallas_call(
+        split_features_kernel,
+        in_specs=[VMEM] * len(features),
+        out_specs=[VMEM] * 2,
+        out_shape=[pltpu.VMEM(shape, jnp.bfloat16)] * 2,
+        compiler_params=pltpu.CompilerParams(vmem_limit_bytes=VMEM_LIMIT),
+        cost_estimate=pl.CostEstimate(flops=10**6, bytes_accessed=10**7, transcendentals=0),
+    )(*[in_vmem(f) for f in features])
+
+
+def gradient_kernel(core_ref, high_ref, low_ref, rows_ref, mine_ref, other_ref, out_ref):
+    parts, height, nodes = high_ref.shape
+    blocks = nodes // TILE
     out_ref[...] = jnp.zeros_like(out_ref)
-    for p in range(0, len(features), PARTS):
-        part = jnp.concatenate([f[...] for f in features[p : p + PARTS]], axis=1)
-        first = p * nodes // TILE
-        rows = rows_ref[first : first + blocks].reshape(blocks * TILE, width)
-        rows_high = rows.astype(jnp.bfloat16)
-        rows_low = (rows - rows_high.astype(jnp.float32)).astype(jnp.bfloat16)
+    for p in range(parts):
+        rows = rows_ref[p * blocks : (p + 1) * blocks].reshape(nodes, out_ref.shape[1])
+        rows_high, rows_low = two_terms(rows)
         right = jnp.concatenate([rows_high, rows_low, rows_high], axis=0)
-        high = part.astype(jnp.bfloat16)
-        low = (part - high.astype(jnp.float32)).astype(jnp.bfloat16)
-        left = jnp.concatenate([high, high, low], axis=1)
+        left = jnp.concatenate([high_ref[p], high_ref[p], low_ref[p]], axis=1)
         out_ref[:height] += jnp.dot(left, right, preferred_element_type=jnp.float32)
     half = mine_ref.shape[0]
     mine_ref[...] = out_ref[pl.ds(pl.multiple_of(core_ref[0] * half, half), half)]
@@ -236,10 +300,11 @@
 
 
 def gradient(features, core, rows, out_rows):
+    high, low = features
     width = rows.shape[2]
     return pl.pallas_call(
         gradient_kernel,
-        in_specs=[VMEM] * len(features) + [SMEM, VMEM],
+        in_specs=[SMEM] + [VMEM] * 3,
         out_specs=[VMEM] * 2,
         out_shape=[pltpu.VMEM((out_rows // 2, width), jnp.float32)] * 2,
         scratch_shapes=[pltpu.VMEM((out_rows, width), jnp.float32)],
@@ -247,7 +312,7 @@
         cost_estimate=pl.CostEstimate(
             flops=6 * out_rows * rows.shape[0] * TILE * width, bytes_accessed=10**7, transcendentals=0
         ),
-    )(*[in_vmem(f) for f in features], core.reshape(1), in_vmem(rows))
+    )(core.reshape(1), in_vmem(high), in_vmem(low), in_vmem(rows))
 
 
 def exchange(value, axes):
@@ -286,7 +351,6 @@
     group_blocks = own_blocks * lax.axis_size(REP)
     half_blocks = own_blocks * lax.axis_size(("x", "zl"))
     blocks = (-1, TILE, hidden_width)
-    scales = lax.rsqrt(degree.astype(jnp.float32))[:, None]
     row_ids = tile_row.reshape(-1)
     live = tile_live.reshape(1)
     slots, edges = edge_dst.shape[2:]
@@ -297,11 +361,9 @@
     other_z = owner // 2 % 2 ^ lax.axis_index("zl")
     to_ids = other_core * half_blocks + (x_ahead * 2 + other_z) * own_blocks + within
 
-    scaled = jnp.dot(features, weight, precision=HIGH, preferred_element_type=jnp.float32) * scales
     height = -(-in_width // 32) * 32
-    here = jnp.pad(features.T * scales.T, ((0, height - in_width), (0, 0)))
-    wide_scales = jnp.broadcast_to(scales, (own_rows, TILE))
-    scaled, here, wide_scales = lax.optimization_barrier((scaled, here, wide_scales))
+    scaled, here, scales = project(features.T, weight, degree, height)
+    scaled, here, scales = lax.optimization_barrier((scaled, here, scales))
     near = gather(scaled, ("x", "zl"))
     here, near = lax.optimization_barrier((here, near))
     far = swap(near, "core")
@@ -309,15 +371,18 @@
     here_x = [from_ahead(here, "x", steps) for steps in (1, 2, 3)]
     tiles = build_tiles(live, edge_dst.reshape(slots, edges), edge_src.reshape(slots, edges))
 
-    def forward(near, far, scaled, cotangent, wide_scales):
+    own_source = (lax.axis_index(("x", "zl")) * own_blocks).reshape(1)
+    own = jnp.concatenate([(lax.axis_index(REP) * own_blocks).reshape(1), own_source]).astype(jnp.int32)
+
+    def forward(near, far, cotangent, scales):
         sources = [near.reshape(blocks), far.reshape(blocks)]
-        (sums,) = aggregate(tiles, live, from_ids, row_ids, sources, [group_blocks], False)
-        return activate(exchange(sums.reshape(-1, own_rows, hidden_width), REP), scaled, cotangent, wide_scales)
-
-    def never(near, far, scaled, cotangent, wide_scales):
-        return scaled + cotangent, scaled - cotangent
-
-    hidden, back_own = lax.cond(live[0] > 0, forward, never, near, far, scaled, cotangent, wide_scales)
+        (sums,) = aggregate(tiles, live, from_ids, row_ids, own, sources, [group_blocks], False)
+        return activate(exchange(sums.reshape(-1, own_rows, hidden_width), REP), cotangent, scales)
+
+    def never(near, far, cotangent, scales):
+        return near[0] + cotangent, far[0] - cotangent
+
+    hidden, back_own = lax.cond(live[0] > 0, forward, never, near, far, cotangent, scales)
     across, here_x, back_own = lax.optimization_barrier((across, here_x, back_own))
     across_x = [from_ahead(across, "x", steps) for steps in (1, 2, 3)]
     back_group = lax.cond(
@@ -328,14 +393,14 @@
     )
     across_x, back_group = lax.optimization_barrier((across_x, back_group))
     kept, sent = aggregate(
-        tiles, live, row_ids, to_ids, [back_group.reshape(blocks)], [half_blocks] * 2, True
+        tiles, live, row_ids, to_ids, own, [back_group.reshape(blocks)], [half_blocks] * 2, True
     )
     kept = kept + swap(sent, "core")
     kept = kept + jnp.pad(back_own.reshape(blocks), ((0, half_blocks - own_blocks), (0, 0), (0, 0)))
     held = [part for pair in zip([here, *here_x], [across, *across_x]) for part in pair]
     parts = lax.axis_size(BLK)
     out_rows = -(-in_width // (8 * parts)) * 8 * parts
-    halves = gradient(held, lax.axis_index("core"), kept, out_rows)
+    halves = gradient(split_features(held), lax.axis_index("core"), kept, out_rows)
     return (hidden, sum_everywhere(*halves)[:in_width])
 
 

time: 231 us -> 224 us (0.970)
  starting transfers between devices: 12.1 us -> 23.1 us
  blocking collectives: 168 us -> 162 us
  Pallas kernels: 31.3 us -> 25.4 us
  matrix products: 2.92 us -> 0 us
    all_to_all x6, blocking collectives: 168 us -> 162 us  [exchange(): return lax.all_to_all(value, axes, 0, 0, tiled=True)]
    ppermute x6, starting transfers between devices: 4.51 us -> 10.1 us  [from_ahead(): lax.ppermute(value, axis, [(i, (i - steps) % size) for i in range(size)])]
    ppermute x5, starting transfers between devices: 7.55 us -> 13 us  [swap(): return lax.ppermute(value, axis, [(0, 1), (1, 0)])]
    ppermute x5, waiting for transfers between devices: 8.4 us -> 4.4 us  [swap(): return lax.ppermute(value, axis, [(0, 1), (1, 0)])]
    pallas_call x3 -> x5, Pallas kernels: 23.1 us -> 20 us  [the longest x2 12.8 us: aggregate(): pl.pallas_call(partial(aggregate_kernel, parts, targets, transpose), in_s...]
    dot_general x1 -> x0, matrix products: 2.92 us -> none  [local(): jnp.dot(features, weight, precision=HIGH, preferred_element_type=jnp.floa...]
    pallas_call x1, Pallas kernels: 6.4 us -> 3.69 us  [build_tiles(): pl.pallas_call(tile_kernel, in_specs=[SMEM, ANY, ANY], out_specs=ANY, out...]
  transfers between devices with their start and end apart: 11 -> 11, of which waited for: 3 -> 4; matrix products, arithmetic and copies ran while one was open for 1% -> 0% of each run, Pallas kernels for 8% -> 7%
where the time goes in v7:
time: 224 us
  blocking collectives  162 us (72%)
  Pallas kernels  25.4 us (11%)
  starting transfers between devices  23.1 us (10%)
  waiting for transfers between devices  6.56 us (3%)
  local copies, waits for them, and re-layouts  4.28 us (2%)
    all_to_all x6, blocking collectives, exchange(): return lax.all_to_all(value, axes, 0, 0, tiled=True)  162 us
    ppermute x5, starting transfers between devices, swap(): return lax.ppermute(value, axis, [(0, 1), (1, 0)])  13 us
    pallas_call x2, Pallas kernels, aggregate(): pl.pallas_call(partial(aggregate_kernel, parts, targets, transpose), in_s...  12.8 us
    ppermute x6, starting transfers between devices, from_ahead(): lax.ppermute(value, axis, [(i, (i - steps) % size) for i in range(size)])  10.1 us
  transfers between devices with their start and end apart: 11, of which 4 were waited for; matrix products, arithmetic and copies ran while one was open for 0% of the time, Pallas kernels for 7%

profile of v7, /device:TPU:1, one launch (start us, length us, event | category | flops | bytes accessed | tf_op | source)
XLA Modules:
  0.0 224.1 jit_solution(17444201093101348037)
XLA Ops:
  4.6 43.2 %all_to_all.30 = f32[8,384,256]{2,1,0:T(8,128)} all-to-all(f32[8,384,256]{2,1,0:T(8,128)S(1)} %broadcast_in_dim.15), channel_id=1, replica_groups=mesh['x'=4,'zl'=2,'core'=2,'y'=4,'zh'=2] {'x','zl'}, dimensions={0} | all-to-all | bytes 6291456 | tf_op jit(solution)/shard_map/all_to_all | solution.py:319
  47.8 1.9 collective-permute-start
  49.6 1.2 collective-permute-start.1
  51.7 1.2 collective-permute-start.3
  53.6 3.7 %shard_map.105.tiles_ref = bf16[256,128,128]{2,1,0:T(8,128)(2,1)} custom-call(s32[1]{0:T(128)} %bitcast.22.live_ref, s32[256,256]{1,0:T(8,128)} %bitcast.31, s32[256,256]{1,0:T(8,128)} %bitcast.32), custom_call_target="tpu_custom_call" | custom-call | flops 1000000 | bytes 100000 | tf_op jit(solution)/shard_map/pallas_call | solution.py:89
  57.5 56.7 %conditional.2 = ((f32[384,256]{1,0:T(8,128)}, f32[384,256]{1,0:T(8,128)S(1)})) conditional(s32[]{:T(128)} %bitcast.5, (f32[8,384,256]{2,1,0:T(8,128)}, f32[384,256]{1,0:T(8,128)S(1)}, f32[8,384,256]{2,1,0:T(8,128)}) %tuple.41, (s32[256]{0:T(256)S(1)}, s32[256]{0:T(256)S(1)}, s32[256]{0:T(256)S(1)}, f32[8,384,256]{2,1,0:T(8,128)}, ...), branch_computations={%region_0.1_spmd, %region_1.2_spmd} | conditional | flops 1000768 | bytes 9541344 | solution.py:385
  58.3 7.0 %branch_1_fun.2 = f32[24,128,256]{2,1,0:T(8,128)S(1)} custom-call(s32[1]{0:T(128)} %get-tuple-element.41.live_ref, s32[256]{0:T(256)S(1)} %add_add_fusion.pick_ref, s32[256]{0:T(256)S(1)} %get-tuple-element.45.place_ref, s32[2]{0:T(128)S(1)} %get-tuple-element.46.own_ref, bf16[256,128,128]{2,1,0:T(8,128)(2,1)} %get-tuple-element.47.tiles_ref, ...), custom_call_target="tpu_custom_call" | custom-call | flops 1000000 | bytes 100000 | tf_op jit(solution)/shard_map/cond/branch_1_fun/pallas_call | solution.py:179
  65.3 47.2 %all_to_all.28.parts_ref = f32[8,384,256]{2,1,0:T(8,128)S(1)} all-to-all(f32[8,384,256]{2,1,0:T(8,128)S(1)} %bitcast.24), channel_id=1, replica_groups=mesh['x'=4,'zl'=2,'core'=2,'y'=4,'zh'=2] {'y','zh'}, dimensions={0} | all-to-all | bytes 6291456 | tf_op jit(solution)/shard_map/cond/branch_1_fun/all_to_all | solution.py:319
  112.5 1.7 branch_1_fun.3
  114.2 6.8 %collective-permute-start.5 = (f32[608,384]{1,0:T(8,128)S(1)}, f32[608,384]{1,0:T(8,128)}, u32[]{:S(2)}, u32[]{:S(2)}) collective-permute-start(f32[608,384]{1,0:T(8,128)S(1)} %collective-permute-done.1.refs_1_), channel_id=1, source_target_pairs={{0,96},{32,0},{64,32},{96,64},{1,97},{33,1},{65,33},{97,65},{2,98}... | collective-permute-start | bytes 2801672 | tf_op jit(solution)/shard_map/ppermute | solution.py:332
  122.2 41.0 %conditional.3 = (f32[8,384,256]{2,1,0:T(8,128)}) conditional(s32[]{:T(128)} %bitcast.5, f32[384,256]{1,0:T(8,128)S(1)} %get-tuple-element.85, f32[384,256]{1,0:T(8,128)S(1)} %get-tuple-element.85), branch_computations={%region_2.3_spmd, %region_3.4_spmd} | conditional | bytes 9830408 | solution.py:388
  122.5 40.7 %all_to_all.29 = f32[8,384,256]{2,1,0:T(8,128)} all-to-all(f32[8,384,256]{2,1,0:T(8,128)S(1)} %broadcast_in_dim.11), channel_id=1, replica_groups=mesh['x'=4,'zl'=2,'core'=2,'y'=4,'zh'=2] {'y','zh'}, dimensions={0} | all-to-all | bytes 6291456 | tf_op jit(solution)/shard_map/cond/branch_1_fun/all_to_all | solution.py:319
  163.2 2.1 collective-permute-done.7.refs_7_
  165.3 5.8 %shard_map.107 = (f32[24,128,256]{2,1,0:T(8,128)S(1)}, f32[24,128,256]{2,1,0:T(8,128)S(1)}) custom-call(s32[1]{0:T(128)} %bitcast.23.live_ref, s32[256]{0:T(256)S(1)} %bitcast.34, s32[256]{0:T(256)S(1)} %get-tuple-element.98.place_ref, s32[2]{0:T(128)S(1)} %pad_add_fusion.1.own_ref, bf16[256,128,128]{2,1,0:T(8,128)(2,1)} %shard_map.105.tiles_ref, ...), custom_call_target="tpu_custom_call" | custom-call | flops 1000000 | bytes 100000 | tf_op jit(solution)/shard_map/pallas_call | solution.py:179
  171.2 5.2 %collective-permute-start.8 = (f32[24,128,256]{2,1,0:T(8,128)S(1)}, f32[24,128,256]{2,1,0:T(8,128)S(1)}, u32[]{:S(2)}, u32[]{:S(2)}) collective-permute-start(f32[24,128,256]{2,1,0:T(8,128)S(1)} %get-tuple-element.95), channel_id=1, source_target_pairs={{0,8},{8,0},{1,9},{9,1},{2,10},{10,2},{3,11},{11,3},{4,12},{12,4},... | collective-permute-start | bytes 9437192 | tf_op jit(solution)/shard_map/ppermute | solution.py:327
  176.3 3.4 %shard_map.106 = (bf16[4,608,768]{2,1,0:T(8,128)(2,1)S(1)}, bf16[4,608,768]{2,1,0:T(8,128)(2,1)S(1)}) custom-call(f32[608,384]{1,0:T(8,128)S(1)} %get-tuple-element.81.refs_0_, f32[608,384]{1,0:T(8,128)S(1)} %collective-permute-done.1.refs_1_, f32[608,384]{1,0:T(8,128)S(1)} %collective-permute-done.2.refs_2_, f32[608,384]{1,0:T(8,128)} %collective-permute-done.5.refs_3_, ...), custom_call_target="tpu_custom_call" | custom-call | flops 1000000 | bytes 10000000 | tf_op jit(solution)/shard_map/pallas_call | solution.py:277
  179.7 1.9 collective-permute-done.8
  182.2 3.1 %shard_map.108 = (f32[320,256]{1,0:T(8,128)S(1)}, f32[320,256]{1,0:T(8,128)S(1)}) custom-call(s32[1]{0:T(128)} %bitcast.15.core_ref, bf16[4,608,768]{2,1,0:T(8,128)(2,1)S(1)} %get-tuple-element.91.high_ref, bf16[4,608,768]{2,1,0:T(8,128)(2,1)S(1)} %get-tuple-element.92.low_ref, f32[24,128,256]{2,1,0:T(8,128)S(1)} %pad_add_fusion.rows_ref), custom_call_target="tpu_custom_call" | custom-call | flops 3019898880 | bytes 10000000 | tf_op jit(solution)/shard_map/pallas_call | solution.py:305
  185.7 1.3 collective-permute-done.9
  187.0 10.3 %all_to_all.31 = f32[8,40,256]{2,1,0:T(8,128)S(1)} all-to-all(f32[8,40,256]{2,1,0:T(8,128)S(1)} %bitcast.30), channel_id=1, replica_groups=mesh['x'=4,'zl'=2,'core'=2,'y'=4,'zh'=2] {'x','zl'}, dimensions={0} | all-to-all | bytes 655360 | tf_op jit(solution)/shard_map/all_to_all | solution.py:319
  197.4 11.1 %all_to_all.32 = f32[8,40,256]{2,1,0:T(8,128)S(1)} all-to-all(f32[8,40,256]{2,1,0:T(8,128)S(1)} %broadcast_in_dim.16), channel_id=1, replica_groups=mesh['x'=4,'zl'=2,'core'=2,'y'=4,'zh'=2] {'y','zh'}, dimensions={0} | all-to-all | bytes 655360 | tf_op jit(solution)/shard_map/all_to_all | solution.py:319
  208.6 9.0 %all_to_all.33 = f32[8,40,256]{2,1,0:T(8,128)S(1)} all-to-all(f32[8,40,256]{2,1,0:T(8,128)S(1)} %broadcast_in_dim.17), channel_id=1, replica_groups=mesh['x'=4,'zl'=2,'core'=2,'y'=4,'zh'=2] {'x','zl'}, dimensions={0} | all-to-all | bytes 655360 | tf_op jit(solution)/shard_map/all_to_all | solution.py:319
  217.6 4.3 %collective-permute-start.10 = (f32[320,256]{1,0:T(8,128)S(1)}, f32[320,256]{1,0:T(8,128)S(1)}, u32[]{:S(2)}, u32[]{:S(2)}) collective-permute-start(f32[320,256]{1,0:T(8,128)S(1)} %bitcast.28), channel_id=1, source_target_pairs={{0,8},{8,0},{1,9},{9,1},{2,10},{10,2},{3,11},{11,3},{4,12},{12,4},... | collective-permute-start | bytes 983048 | tf_op jit(solution)/shard_map/ppermute | solution.py:327
  221.9 1.3 collective-permute-done.10
  (43 shorter events, 9.1 us)
Async XLA Ops:
  1.3 1.2 copy-start
  2.5 1.1 copy-start.1
  47.8 9.7 %collective-permute-start = (f32[8,384,256]{2,1,0:T(8,128)}, f32[8,384,256]{2,1,0:T(8,128)}, u32[]{:S(2)}, u32[]{:S(2)}) collective-permute-start(f32[8,384,256]{2,1,0:T(8,128)} %all_to_all.30), channel_id=1, source_target_pairs={{0,8},{8,0},{1,9},{9,1},{2,10},{10,2},{3,11},{11,3},{4,12},{12,4},... | collective-permute-start | bytes 9437192 | tf_op jit(solution)/shard_map/ppermute | solution.py:327
  49.6 64.6 %collective-permute-start.1 = (f32[608,384]{1,0:T(8,128)S(1)}, f32[608,384]{1,0:T(8,128)S(1)}, u32[]{:S(2)}, u32[]{:S(2)}) collective-permute-start(f32[608,384]{1,0:T(8,128)S(1)} %get-tuple-element.81.refs_0_), channel_id=1, source_target_pairs={{0,16},{16,0},{1,17},{17,1},{2,18},{18,2},{3,19},{19,3},{4,20},{20... | collective-permute-start | bytes 2801672 | tf_op jit(solution)/shard_map/ppermute | solution.py:327
  50.8 63.4 %collective-permute-start.2 = (f32[608,384]{1,0:T(8,128)S(1)}, f32[608,384]{1,0:T(8,128)S(1)}, u32[]{:S(2)}, u32[]{:S(2)}) collective-permute-start(f32[608,384]{1,0:T(8,128)S(1)} %get-tuple-element.81.refs_0_), channel_id=1, source_target_pairs={{0,96},{32,0},{64,32},{96,64},{1,97},{33,1},{65,33},{97,65},{2,98}... | collective-permute-start | bytes 2801672 | tf_op jit(solution)/shard_map/ppermute | solution.py:332
  51.7 62.5 %collective-permute-start.3 = (f32[608,384]{1,0:T(8,128)S(1)}, f32[608,384]{1,0:T(8,128)}, u32[]{:S(2)}, u32[]{:S(2)}) collective-permute-start(f32[608,384]{1,0:T(8,128)S(1)} %get-tuple-element.81.refs_0_), channel_id=1, source_target_pairs={{0,64},{32,96},{64,0},{96,32},{1,65},{33,97},{65,1},{97,33},{2,66}... | collective-permute-start | bytes 2801672 | tf_op jit(solution)/shard_map/ppermute | solution.py:332
  52.9 61.3 %collective-permute-start.4 = (f32[608,384]{1,0:T(8,128)S(1)}, f32[608,384]{1,0:T(8,128)}, u32[]{:S(2)}, u32[]{:S(2)}) collective-permute-start(f32[608,384]{1,0:T(8,128)S(1)} %get-tuple-element.81.refs_0_), channel_id=1, source_target_pairs={{0,32},{32,64},{64,96},{96,0},{1,33},{33,65},{65,97},{97,1},{2,34}... | collective-permute-start | bytes 2801672 | tf_op jit(solution)/shard_map/ppermute | solution.py:332
  53.6 3.8 %copy-start.6 = (s32[1,1,256]{2,1,0:T(1,128)S(1)}, s32[1,1,256]{2,1,0:T(1,128)}, u32[]{:S(2)}) copy-start(s32[1,1,256]{2,1,0:T(1,128)} %param.18) | copy-start | bytes 3076
  53.6 3.9 %copy-start.2 = (f32[384,256]{1,0:T(8,128)S(1)}, f32[384,256]{1,0:T(8,128)}, u32[]{:S(2)}) copy-start(f32[384,256]{1,0:T(8,128)} %param.15) | copy-start | bytes 1179652
  53.6 3.9 %copy-start.5 = (s32[1,1,256]{2,1,0:T(1,128)S(1)}, s32[1,1,256]{2,1,0:T(1,128)}, u32[]{:S(2)}) copy-start(s32[1,1,256]{2,1,0:T(1,128)} %param.17) | copy-start | bytes 3076
  57.5 0.7 copy-start.3
  65.3 47.2 %copy-start.4 = (f32[384,256]{1,0:T(8,128)S(1)}, f32[384,256]{1,0:T(8,128)}, u32[]{:S(2)}) copy-start(f32[384,256]{1,0:T(8,128)} %copy-done.3) | copy-start | bytes 1179652 | tf_op jit(solution)/shard_map/cond
  114.2 48.9 %collective-permute-start.5 = (f32[608,384]{1,0:T(8,128)S(1)}, f32[608,384]{1,0:T(8,128)}, u32[]{:S(2)}, u32[]{:S(2)}) collective-permute-start(f32[608,384]{1,0:T(8,128)S(1)} %collective-permute-done.1.refs_1_), channel_id=1, source_target_pairs={{0,96},{32,0},{64,32},{96,64},{1,97},{33,1},{65,33},{97,65},{2,98}... | collective-permute-start | bytes 2801672 | tf_op jit(solution)/shard_map/ppermute | solution.py:332
  121.1 42.1 %collective-permute-start.6 = (f32[608,384]{1,0:T(8,128)S(1)}, f32[608,384]{1,0:T(8,128)}, u32[]{:S(2)}, u32[]{:S(2)}) collective-permute-start(f32[608,384]{1,0:T(8,128)S(1)} %collective-permute-done.1.refs_1_), channel_id=1, source_target_pairs={{0,64},{32,96},{64,0},{96,32},{1,65},{33,97},{65,1},{97,33},{2,66}... | collective-permute-start | bytes 2801672 | tf_op jit(solution)/shard_map/ppermute | solution.py:332
  121.4 43.9 %collective-permute-start.7 = (f32[608,384]{1,0:T(8,128)S(1)}, f32[608,384]{1,0:T(8,128)}, u32[]{:S(2)}, u32[]{:S(2)}) collective-permute-start(f32[608,384]{1,0:T(8,128)S(1)} %collective-permute-done.1.refs_1_), channel_id=1, source_target_pairs={{0,32},{32,64},{64,96},{96,0},{1,33},{33,65},{65,97},{97,1},{2,34}... | collective-permute-start | bytes 2801672 | tf_op jit(solution)/shard_map/ppermute | solution.py:332
  171.2 10.5 %collective-permute-start.8 = (f32[24,128,256]{2,1,0:T(8,128)S(1)}, f32[24,128,256]{2,1,0:T(8,128)S(1)}, u32[]{:S(2)}, u32[]{:S(2)}) collective-permute-start(f32[24,128,256]{2,1,0:T(8,128)S(1)} %get-tuple-element.95), channel_id=1, source_target_pairs={{0,8},{8,0},{1,9},{9,1},{2,10},{10,2},{3,11},{11,3},{4,12},{12,4},... | collective-permute-start | bytes 9437192 | tf_op jit(solution)/shard_map/ppermute | solution.py:327
  185.3 1.7 collective-permute-start.9
  217.6 5.6 %collective-permute-start.10 = (f32[320,256]{1,0:T(8,128)S(1)}, f32[320,256]{1,0:T(8,128)S(1)}, u32[]{:S(2)}, u32[]{:S(2)}) collective-permute-start(f32[320,256]{1,0:T(8,128)S(1)} %bitcast.28), channel_id=1, source_target_pairs={{0,8},{8,0},{1,9},{9,1},{2,10},{10,2},{3,11},{11,3},{4,12},{12,4},... | collective-permute-start | bytes 983048 | tf_op jit(solution)/shard_map/ppermute | solution.py:327

commit v8 on v7

--- a/solution.py
+++ b/solution.py
@@ -17,7 +17,7 @@
 AHEAD = 2
 STRIP = 128
 UNROLL = 32
-VMEM_LIMIT = 32 * 1024 * 1024
+VMEM_LIMIT = 28 * 1024 * 1024
 BLK = ("x", "zl", "core")
 REP = ("y", "zh")
 
@@ -221,11 +221,32 @@
     )(parts, cotangent, scales)
 
 
-def project_kernel(features_ref, weight_ref, degree_ref, scaled_ref, turned_ref, scales_ref, padded):
+def project_kernel(
+    features_hbm,
+    weight_hbm,
+    degree_hbm,
+    scaled_ref,
+    turned_ref,
+    scales_ref,
+    features_ref,
+    weight_ref,
+    degree_ref,
+    padded,
+    sems,
+):
     height, in_width = turned_ref.shape[0], features_ref.shape[0]
-    scales = lax.rsqrt(degree_ref[...].astype(jnp.float32))
+    features_in = pltpu.make_async_copy(features_hbm, features_ref, sems.at[0])
+    weight_in = pltpu.make_async_copy(weight_hbm, weight_ref, sems.at[1])
+    degree_in = pltpu.make_async_copy(degree_hbm, degree_ref, sems.at[2])
+    degree_in.start()
+    features_in.start()
+    weight_in.start()
+    degree_in.wait()
+    scales = lax.rsqrt(degree_ref[...].astype(jnp.float32)).reshape(1, -1)
+    features_in.wait()
     turned_ref[:in_width] = features_ref[...] * scales
     turned_ref[in_width:] = jnp.zeros((height - in_width, turned_ref.shape[1]), jnp.float32)
+    weight_in.wait()
     padded[:in_width] = weight_ref[...]
     padded[in_width:] = jnp.zeros((height - in_width, padded.shape[1]), jnp.float32)
     left_high, left_low = two_terms(turned_ref[...])
@@ -249,16 +270,22 @@
     width = weight.shape[1]
     return pl.pallas_call(
         project_kernel,
-        in_specs=[VMEM] * 3,
+        in_specs=[ANY] * 3,
         out_specs=[VMEM] * 3,
         out_shape=[
             jax.ShapeDtypeStruct((rows, width), jnp.float32),
             jax.ShapeDtypeStruct((height, rows), jnp.float32),
             jax.ShapeDtypeStruct((rows, TILE), jnp.float32),
         ],
-        scratch_shapes=[pltpu.VMEM((height, width), jnp.float32)],
-        compiler_params=pltpu.CompilerParams(vmem_limit_bytes=VMEM_LIMIT),
-    )(features, weight, degree.reshape(1, rows))
+        scratch_shapes=[
+            pltpu.VMEM(features.shape, jnp.float32),
+            pltpu.VMEM(weight.shape, jnp.float32),
+            pltpu.VMEM(degree.shape, jnp.int32),
+            pltpu.VMEM((height, width), jnp.float32),
+            pltpu.SemaphoreType.DMA((3,)),
+        ],
+        compiler_params=pltpu.CompilerParams(vmem_limit_bytes=VMEM_LIMIT),
+    )(in_hbm(features), in_hbm(weight), in_hbm(degree))
 
 
 def split_features_kernel(*refs):
@@ -284,12 +311,16 @@
     )(*[in_vmem(f) for f in features])
 
 
-def gradient_kernel(core_ref, high_ref, low_ref, rows_ref, mine_ref, other_ref, out_ref):
+def gradient_kernel(core_ref, high_ref, low_ref, kept_ref, came_ref, own_ref, mine_ref, other_ref, out_ref):
     parts, height, nodes = high_ref.shape
     blocks = nodes // TILE
     out_ref[...] = jnp.zeros_like(out_ref)
     for p in range(parts):
-        rows = rows_ref[p * blocks : (p + 1) * blocks].reshape(nodes, out_ref.shape[1])
+        rows = kept_ref[p * blocks : (p + 1) * blocks] + came_ref[p * blocks : (p + 1) * blocks]
+        if p == 0:
+            own = own_ref.shape[0]
+            rows = jnp.concatenate([rows[:own] + own_ref[...], rows[own:]])
+        rows = rows.reshape(nodes, out_ref.shape[1])
         rows_high, rows_low = two_terms(rows)
         right = jnp.concatenate([rows_high, rows_low, rows_high], axis=0)
         left = jnp.concatenate([high_ref[p], high_ref[p], low_ref[p]], axis=1)
@@ -299,20 +330,20 @@
     other_ref[...] = out_ref[pl.ds(pl.multiple_of((1 - core_ref[0]) * half, half), half)]
 
 
-def gradient(features, core, rows, out_rows):
+def gradient(features, core, kept, came, own, out_rows):
     high, low = features
-    width = rows.shape[2]
+    width = kept.shape[2]
     return pl.pallas_call(
         gradient_kernel,
-        in_specs=[SMEM] + [VMEM] * 3,
+        in_specs=[SMEM] + [VMEM] * 5,
         out_specs=[VMEM] * 2,
         out_shape=[pltpu.VMEM((out_rows // 2, width), jnp.float32)] * 2,
         scratch_shapes=[pltpu.VMEM((out_rows, width), jnp.float32)],
         compiler_params=pltpu.CompilerParams(vmem_limit_bytes=VMEM_LIMIT),
         cost_estimate=pl.CostEstimate(
-            flops=6 * out_rows * rows.shape[0] * TILE * width, bytes_accessed=10**7, transcendentals=0
+            flops=6 * out_rows * kept.shape[0] * TILE * width, bytes_accessed=10**7, transcendentals=0
         ),
-    )(core.reshape(1), in_vmem(high), in_vmem(low), in_vmem(rows))
+    )(core.reshape(1), *[in_vmem(v) for v in (high, low, kept, came, own)])
 
 
 def exchange(value, axes):
@@ -395,12 +426,11 @@
     kept, sent = aggregate(
         tiles, live, row_ids, to_ids, own, [back_group.reshape(blocks)], [half_blocks] * 2, True
     )
-    kept = kept + swap(sent, "core")
-    kept = kept + jnp.pad(back_own.reshape(blocks), ((0, half_blocks - own_blocks), (0, 0), (0, 0)))
+    came = swap(sent, "core")
     held = [part for pair in zip([here, *here_x], [across, *across_x]) for part in pair]
     parts = lax.axis_size(BLK)
     out_rows = -(-in_width // (8 * parts)) * 8 * parts
-    halves = gradient(split_features(held), lax.axis_index("core"), kept, out_rows)
+    halves = gradient(split_features(held), lax.axis_index("core"), kept, came, back_own.reshape(blocks), out_rows)
     return (hidden, sum_everywhere(*halves)[:in_width])
 
 

time: 224 us -> 223 us (level)
  starting transfers between devices: 23.1 us -> 14.6 us
  Pallas kernels: 25.4 us -> 31.2 us
  blocking collectives: 162 us -> 166 us
  local copies, waits for them, and re-layouts: 4.28 us -> 1.34 us
    ppermute x5, starting transfers between devices: 13 us -> 7.73 us  [swap(): return lax.ppermute(value, axis, [(0, 1), (1, 0)])]
    all_to_all x6, blocking collectives: 162 us -> 166 us  [exchange(): return lax.all_to_all(value, axes, 0, 0, tiled=True)]
    pallas_call x2, Pallas kernels: 12.8 us -> 16.1 us  [aggregate(): pl.pallas_call(partial(aggregate_kernel, parts, targets, transpose), in_s...]
    ppermute x6, starting transfers between devices: 10.1 us -> 6.84 us  [from_ahead(): lax.ppermute(value, axis, [(i, (i - steps) % size) for i in range(size)])]
    unnamed x10 -> x6, local copies, waits for them, and re-layouts: 2.28 us -> 0.02 us
  transfers between devices with their start and end apart: 11 -> 11, of which waited for: 4 -> 4; matrix products, arithmetic and copies ran while one was open for 0% -> 0% of each run, Pallas kernels for 7% -> 8%
where the time goes in v8:
time: 223 us
  blocking collectives  166 us (74%)
  Pallas kernels  31.2 us (14%)
  starting transfers between devices  14.6 us (7%)
  waiting for transfers between devices  6.89 us (3%)
    all_to_all x6, blocking collectives, exchange(): return lax.all_to_all(value, axes, 0, 0, tiled=True)  166 us
    pallas_call x2, Pallas kernels, aggregate(): pl.pallas_call(partial(aggregate_kernel, parts, targets, transpose), in_s...  16.1 us
    ppermute x5, starting transfers between devices, swap(): return lax.ppermute(value, axis, [(0, 1), (1, 0)])  7.73 us
    ppermute x6, starting transfers between devices, from_ahead(): lax.ppermute(value, axis, [(i, (i - steps) % size) for i in range(size)])  6.84 us
    ppermute x5, waiting for transfers between devices, swap(): return lax.ppermute(value, axis, [(0, 1), (1, 0)])  4.97 us
    pallas_call x1, Pallas kernels, build_tiles(): pl.pallas_call(tile_kernel, in_specs=[SMEM, ANY, ANY], out_specs=ANY, out...  4.8 us
  transfers between devices with their start and end apart: 11, of which 4 were waited for; matrix products, arithmetic and copies ran while one was open for 0% of the time, Pallas kernels for 8%

profile of v8, /device:TPU:1, one launch (start us, length us, event | category | flops | bytes accessed | tf_op | source)
XLA Modules:
  0.0 222.7 jit_solution(4809502667572041430)
XLA Ops:
  0.6 2.0 shard_map.104
  2.9 43.2 %all_to_all.30 = f32[8,384,256]{2,1,0:T(8,128)} all-to-all(f32[8,384,256]{2,1,0:T(8,128)S(1)} %broadcast_in_dim.15), channel_id=1, replica_groups=mesh['x'=4,'zl'=2,'core'=2,'y'=4,'zh'=2] {'x','zl'}, dimensions={0} | all-to-all | bytes 6291456 | tf_op jit(solution)/shard_map/all_to_all | solution.py:350
  46.1 1.9 collective-permute-start
  48.0 1.2 collective-permute-start.1
  50.1 1.2 collective-permute-start.3
  52.0 4.8 %shard_map.105.tiles_ref = bf16[256,128,128]{2,1,0:T(8,128)(2,1)} custom-call(s32[1]{0:T(128)} %bitcast.22.live_ref, s32[256,256]{1,0:T(8,128)} %bitcast.31, s32[256,256]{1,0:T(8,128)} %bitcast.32), custom_call_target="tpu_custom_call" | custom-call | flops 1000000 | bytes 100000 | tf_op jit(solution)/shard_map/pallas_call | solution.py:89
  57.0 60.1 %conditional.2 = ((f32[384,256]{1,0:T(8,128)}, f32[384,256]{1,0:T(8,128)S(1)})) conditional(s32[]{:T(128)} %bitcast.5, (f32[8,384,256]{2,1,0:T(8,128)}, f32[384,256]{1,0:T(8,128)S(1)}, f32[8,384,256]{2,1,0:T(8,128)}) %tuple.41, (s32[256]{0:T(256)S(1)}, s32[256]{0:T(256)S(1)}, s32[256]{0:T(256)S(1)}, f32[8,384,256]{2,1,0:T(8,128)}, ...), branch_computations={%region_0.1_spmd, %region_1.2_spmd} | conditional | flops 1000768 | bytes 9541344 | solution.py:416
  57.8 8.6 %branch_1_fun.2 = f32[24,128,256]{2,1,0:T(8,128)S(1)} custom-call(s32[1]{0:T(128)} %get-tuple-element.41.live_ref, s32[256]{0:T(256)S(1)} %add_add_fusion.pick_ref, s32[256]{0:T(256)S(1)} %get-tuple-element.45.place_ref, s32[2]{0:T(128)S(1)} %get-tuple-element.46.own_ref, bf16[256,128,128]{2,1,0:T(8,128)(2,1)} %get-tuple-element.47.tiles_ref, ...), custom_call_target="tpu_custom_call" | custom-call | flops 1000000 | bytes 100000 | tf_op jit(solution)/shard_map/cond/branch_1_fun/pallas_call | solution.py:179
  66.4 49.0 %all_to_all.28.parts_ref = f32[8,384,256]{2,1,0:T(8,128)S(1)} all-to-all(f32[8,384,256]{2,1,0:T(8,128)S(1)} %bitcast.24), channel_id=1, replica_groups=mesh['x'=4,'zl'=2,'core'=2,'y'=4,'zh'=2] {'y','zh'}, dimensions={0} | all-to-all | bytes 6291456 | tf_op jit(solution)/shard_map/cond/branch_1_fun/all_to_all | solution.py:350
  115.4 1.7 branch_1_fun.3
  117.1 4.1 %collective-permute-start.5 = (f32[608,384]{1,0:T(8,128)S(1)}, f32[608,384]{1,0:T(8,128)}, u32[]{:S(2)}, u32[]{:S(2)}) collective-permute-start(f32[608,384]{1,0:T(8,128)S(1)} %collective-permute-done.1.refs_1_), channel_id=1, source_target_pairs={{0,96},{32,0},{64,32},{96,64},{1,97},{33,1},{65,33},{97,65},{2,98}... | collective-permute-start | bytes 2801672 | tf_op jit(solution)/shard_map/ppermute | solution.py:363
  121.9 41.0 %conditional.3 = (f32[8,384,256]{2,1,0:T(8,128)}) conditional(s32[]{:T(128)} %bitcast.5, f32[384,256]{1,0:T(8,128)S(1)} %get-tuple-element.85, f32[384,256]{1,0:T(8,128)S(1)} %get-tuple-element.85), branch_computations={%region_2.3_spmd, %region_3.4_spmd} | conditional | bytes 9830408 | solution.py:419
  122.1 40.7 %all_to_all.29 = f32[8,384,256]{2,1,0:T(8,128)} all-to-all(f32[8,384,256]{2,1,0:T(8,128)S(1)} %broadcast_in_dim.11), channel_id=1, replica_groups=mesh['x'=4,'zl'=2,'core'=2,'y'=4,'zh'=2] {'y','zh'}, dimensions={0} | all-to-all | bytes 6291456 | tf_op jit(solution)/shard_map/cond/branch_1_fun/all_to_all | solution.py:350
  162.9 1.9 collective-permute-done.7.refs_7_
  164.8 7.5 %shard_map.107 = (f32[24,128,256]{2,1,0:T(8,128)S(1)}, f32[24,128,256]{2,1,0:T(8,128)S(1)}) custom-call(s32[1]{0:T(128)} %bitcast.23.live_ref, s32[256]{0:T(256)S(1)} %bitcast.34, s32[256]{0:T(256)S(1)} %get-tuple-element.98.place_ref, s32[2]{0:T(128)S(1)} %pad_add_fusion.own_ref, bf16[256,128,128]{2,1,0:T(8,128)(2,1)} %shard_map.105.tiles_ref, ...), custom_call_target="tpu_custom_call" | custom-call | flops 1000000 | bytes 100000 | tf_op jit(solution)/shard_map/pallas_call | solution.py:179
  172.6 3.4 %shard_map.106 = (bf16[4,608,768]{2,1,0:T(8,128)(2,1)S(1)}, bf16[4,608,768]{2,1,0:T(8,128)(2,1)S(1)}) custom-call(f32[608,384]{1,0:T(8,128)S(1)} %get-tuple-element.81.refs_0_, f32[608,384]{1,0:T(8,128)S(1)} %collective-permute-done.1.refs_1_, f32[608,384]{1,0:T(8,128)S(1)} %collective-permute-done.2.refs_2_, f32[608,384]{1,0:T(8,128)} %collective-permute-done.5.refs_3_, ...), custom_call_target="tpu_custom_call" | custom-call | flops 1000000 | bytes 10000000 | tf_op jit(solution)/shard_map/pallas_call | solution.py:304
  176.0 2.2 collective-permute-done.8.came_ref
  178.3 3.2 %shard_map.108 = (f32[320,256]{1,0:T(8,128)S(1)}, f32[320,256]{1,0:T(8,128)S(1)}) custom-call(s32[1]{0:T(128)} %bitcast.15.core_ref, bf16[4,608,768]{2,1,0:T(8,128)(2,1)S(1)} %get-tuple-element.91.high_ref, bf16[4,608,768]{2,1,0:T(8,128)(2,1)S(1)} %get-tuple-element.92.low_ref, f32[24,128,256]{2,1,0:T(8,128)S(1)} %get-tuple-element.94.kept_ref, ...), custom_call_target="tpu_custom_call" | custom-call | flops 3019898880 | bytes 10000000 | tf_op jit(solution)/shard_map/pallas_call | solution.py:336
  181.6 1.5 collective-permute-done.9
  183.2 12.7 %all_to_all.31 = f32[8,40,256]{2,1,0:T(8,128)S(1)} all-to-all(f32[8,40,256]{2,1,0:T(8,128)S(1)} %bitcast.29), channel_id=1, replica_groups=mesh['x'=4,'zl'=2,'core'=2,'y'=4,'zh'=2] {'x','zl'}, dimensions={0} | all-to-all | bytes 655360 | tf_op jit(solution)/shard_map/all_to_all | solution.py:350
  196.0 11.3 %all_to_all.32 = f32[8,40,256]{2,1,0:T(8,128)S(1)} all-to-all(f32[8,40,256]{2,1,0:T(8,128)S(1)} %broadcast_in_dim.16), channel_id=1, replica_groups=mesh['x'=4,'zl'=2,'core'=2,'y'=4,'zh'=2] {'y','zh'}, dimensions={0} | all-to-all | bytes 655360 | tf_op jit(solution)/shard_map/all_to_all | solution.py:350
  207.3 9.2 %all_to_all.33 = f32[8,40,256]{2,1,0:T(8,128)S(1)} all-to-all(f32[8,40,256]{2,1,0:T(8,128)S(1)} %broadcast_in_dim.17), channel_id=1, replica_groups=mesh['x'=4,'zl'=2,'core'=2,'y'=4,'zh'=2] {'x','zl'}, dimensions={0} | all-to-all | bytes 655360 | tf_op jit(solution)/shard_map/all_to_all | solution.py:350
  216.4 4.2 %collective-permute-start.10 = (f32[320,256]{1,0:T(8,128)S(1)}, f32[320,256]{1,0:T(8,128)S(1)}, u32[]{:S(2)}, u32[]{:S(2)}) collective-permute-start(f32[320,256]{1,0:T(8,128)S(1)} %bitcast.27), channel_id=1, source_target_pairs={{0,8},{8,0},{1,9},{9,1},{2,10},{10,2},{3,11},{11,3},{4,12},{12,4},... | collective-permute-start | bytes 983048 | tf_op jit(solution)/shard_map/ppermute | solution.py:358
  220.6 1.3 collective-permute-done.10
  (37 shorter events, 4.6 us)
Async XLA Ops:
  46.1 10.8 %collective-permute-start = (f32[8,384,256]{2,1,0:T(8,128)}, f32[8,384,256]{2,1,0:T(8,128)}, u32[]{:S(2)}, u32[]{:S(2)}) collective-permute-start(f32[8,384,256]{2,1,0:T(8,128)} %all_to_all.30), channel_id=1, source_target_pairs={{0,8},{8,0},{1,9},{9,1},{2,10},{10,2},{3,11},{11,3},{4,12},{12,4},... | collective-permute-start | bytes 9437192 | tf_op jit(solution)/shard_map/ppermute | solution.py:358
  48.0 69.1 %collective-permute-start.1 = (f32[608,384]{1,0:T(8,128)S(1)}, f32[608,384]{1,0:T(8,128)S(1)}, u32[]{:S(2)}, u32[]{:S(2)}) collective-permute-start(f32[608,384]{1,0:T(8,128)S(1)} %get-tuple-element.81.refs_0_), channel_id=1, source_target_pairs={{0,16},{16,0},{1,17},{17,1},{2,18},{18,2},{3,19},{19,3},{4,20},{20... | collective-permute-start | bytes 2801672 | tf_op jit(solution)/shard_map/ppermute | solution.py:358
  49.2 67.9 %collective-permute-start.2 = (f32[608,384]{1,0:T(8,128)S(1)}, f32[608,384]{1,0:T(8,128)S(1)}, u32[]{:S(2)}, u32[]{:S(2)}) collective-permute-start(f32[608,384]{1,0:T(8,128)S(1)} %get-tuple-element.81.refs_0_), channel_id=1, source_target_pairs={{0,96},{32,0},{64,32},{96,64},{1,97},{33,1},{65,33},{97,65},{2,98}... | collective-permute-start | bytes 2801672 | tf_op jit(solution)/shard_map/ppermute | solution.py:363
  50.1 67.0 %collective-permute-start.3 = (f32[608,384]{1,0:T(8,128)S(1)}, f32[608,384]{1,0:T(8,128)}, u32[]{:S(2)}, u32[]{:S(2)}) collective-permute-start(f32[608,384]{1,0:T(8,128)S(1)} %get-tuple-element.81.refs_0_), channel_id=1, source_target_pairs={{0,64},{32,96},{64,0},{96,32},{1,65},{33,97},{65,1},{97,33},{2,66}... | collective-permute-start | bytes 2801672 | tf_op jit(solution)/shard_map/ppermute | solution.py:363
  51.3 65.8 %collective-permute-start.4 = (f32[608,384]{1,0:T(8,128)S(1)}, f32[608,384]{1,0:T(8,128)}, u32[]{:S(2)}, u32[]{:S(2)}) collective-permute-start(f32[608,384]{1,0:T(8,128)S(1)} %get-tuple-element.81.refs_0_), channel_id=1, source_target_pairs={{0,32},{32,64},{64,96},{96,0},{1,33},{33,65},{65,97},{97,1},{2,34}... | collective-permute-start | bytes 2801672 | tf_op jit(solution)/shard_map/ppermute | solution.py:363
  52.0 4.9 %copy-start.4 = (s32[1,1,256]{2,1,0:T(1,128)S(1)}, s32[1,1,256]{2,1,0:T(1,128)}, u32[]{:S(2)}) copy-start(s32[1,1,256]{2,1,0:T(1,128)} %param.18) | copy-start | bytes 3076
  52.0 5.0 %copy-start = (f32[384,256]{1,0:T(8,128)S(1)}, f32[384,256]{1,0:T(8,128)}, u32[]{:S(2)}) copy-start(f32[384,256]{1,0:T(8,128)} %param.15) | copy-start | bytes 1179652
  52.0 5.0 %copy-start.3 = (s32[1,1,256]{2,1,0:T(1,128)S(1)}, s32[1,1,256]{2,1,0:T(1,128)}, u32[]{:S(2)}) copy-start(s32[1,1,256]{2,1,0:T(1,128)} %param.17) | copy-start | bytes 3076
  57.0 0.7 copy-start.1
  66.4 49.0 %copy-start.2 = (f32[384,256]{1,0:T(8,128)S(1)}, f32[384,256]{1,0:T(8,128)}, u32[]{:S(2)}) copy-start(f32[384,256]{1,0:T(8,128)} %copy-done.1) | copy-start | bytes 1179652 | tf_op jit(solution)/shard_map/cond
  117.1 45.7 %collective-permute-start.5 = (f32[608,384]{1,0:T(8,128)S(1)}, f32[608,384]{1,0:T(8,128)}, u32[]{:S(2)}, u32[]{:S(2)}) collective-permute-start(f32[608,384]{1,0:T(8,128)S(1)} %collective-permute-done.1.refs_1_), channel_id=1, source_target_pairs={{0,96},{32,0},{64,32},{96,64},{1,97},{33,1},{65,33},{97,65},{2,98}... | collective-permute-start | bytes 2801672 | tf_op jit(solution)/shard_map/ppermute | solution.py:363
  121.2 41.7 %collective-permute-start.6 = (f32[608,384]{1,0:T(8,128)S(1)}, f32[608,384]{1,0:T(8,128)}, u32[]{:S(2)}, u32[]{:S(2)}) collective-permute-start(f32[608,384]{1,0:T(8,128)S(1)} %collective-permute-done.1.refs_1_), channel_id=1, source_target_pairs={{0,64},{32,96},{64,0},{96,32},{1,65},{33,97},{65,1},{97,33},{2,66}... | collective-permute-start | bytes 2801672 | tf_op jit(solution)/shard_map/ppermute | solution.py:363
  121.2 43.6 %collective-permute-start.7 = (f32[608,384]{1,0:T(8,128)S(1)}, f32[608,384]{1,0:T(8,128)}, u32[]{:S(2)}, u32[]{:S(2)}) collective-permute-start(f32[608,384]{1,0:T(8,128)S(1)} %collective-permute-done.1.refs_1_), channel_id=1, source_target_pairs={{0,32},{32,64},{64,96},{96,0},{1,33},{33,65},{65,97},{97,1},{2,34}... | collective-permute-start | bytes 2801672 | tf_op jit(solution)/shard_map/ppermute | solution.py:363
  172.3 5.9 %collective-permute-start.8 = (f32[24,128,256]{2,1,0:T(8,128)S(1)}, f32[24,128,256]{2,1,0:T(8,128)S(1)}, u32[]{:S(2)}, u32[]{:S(2)}) collective-permute-start(f32[24,128,256]{2,1,0:T(8,128)S(1)} %get-tuple-element.95), channel_id=1, source_target_pairs={{0,8},{8,0},{1,9},{9,1},{2,10},{10,2},{3,11},{11,3},{4,12},{12,4},... | collective-permute-start | bytes 9437192 | tf_op jit(solution)/shard_map/ppermute | solution.py:358
  181.4 1.7 collective-permute-start.9
  216.4 5.4 %collective-permute-start.10 = (f32[320,256]{1,0:T(8,128)S(1)}, f32[320,256]{1,0:T(8,128)S(1)}, u32[]{:S(2)}, u32[]{:S(2)}) collective-permute-start(f32[320,256]{1,0:T(8,128)S(1)} %bitcast.27), channel_id=1, source_target_pairs={{0,8},{8,0},{1,9},{9,1},{2,10},{10,2},{3,11},{11,3},{4,12},{12,4},... | collective-permute-start | bytes 983048 | tf_op jit(solution)/shard_map/ppermute | solution.py:358

commit v9 on v8

--- a/solution.py
+++ b/solution.py
@@ -249,12 +249,11 @@
     weight_in.wait()
     padded[:in_width] = weight_ref[...]
     padded[in_width:] = jnp.zeros((height - in_width, padded.shape[1]), jnp.float32)
-    left_high, left_low = two_terms(turned_ref[...])
-    right_high, right_low = two_terms(padded[...])
     scaled_ref[...] = lax.dot_general(
-        jnp.concatenate([left_high, left_high, left_low]),
-        jnp.concatenate([right_high, right_low, right_high]),
+        turned_ref[...],
+        padded[...],
         (((0,), (0,)), ((), ())),
+        precision=HIGH,
         preferred_element_type=jnp.float32,
     )
     scales_ref[...] = jnp.broadcast_to(scales, (TILE, scales.shape[1])).T
@@ -384,6 +383,7 @@
     blocks = (-1, TILE, hidden_width)
     row_ids = tile_row.reshape(-1)
     live = tile_live.reshape(1)
+    always = live[0] >= 0
     slots, edges = edge_dst.shape[2:]
     owner, within = tile_col.reshape(-1) // own_blocks, tile_col.reshape(-1) % own_blocks
     other_core = owner % 2 ^ lax.axis_index("core")
@@ -413,11 +413,11 @@
     def never(near, far, cotangent, scales):
         return near[0] + cotangent, far[0] - cotangent
 
-    hidden, back_own = lax.cond(live[0] > 0, forward, never, near, far, cotangent, scales)
+    hidden, back_own = lax.cond(always, forward, never, near, far, cotangent, scales)
     across, here_x, back_own = lax.optimization_barrier((across, here_x, back_own))
     across_x = [from_ahead(across, "x", steps) for steps in (1, 2, 3)]
     back_group = lax.cond(
-        live[0] > 0,
+        always,
         lambda back: gather(back, REP),
         lambda back: jnp.broadcast_to(back, (lax.axis_size(REP),) + back.shape),
         back_own,

time: 223 us -> 222 us (level)
  blocking collectives: 166 us -> 157 us
  starting transfers between devices: 14.6 us -> 20.6 us
  Pallas kernels: 31.2 us -> 34 us
    all_to_all x6, blocking collectives: 166 us -> 157 us  [exchange(): return lax.all_to_all(value, axes, 0, 0, tiled=True)]
    ppermute x6, starting transfers between devices: 6.84 us -> 10.8 us  [from_ahead(): lax.ppermute(value, axis, [(i, (i - steps) % size) for i in range(size)])]
  transfers between devices with their start and end apart: 11 -> 11, of which waited for: 4 -> 4; matrix products, arithmetic and copies ran while one was open for 0% -> 0% of each run, Pallas kernels for 8% -> 9%
where the time goes in v9:
time: 222 us
  blocking collectives  157 us (71%)
  Pallas kernels  34 us (15%)
  starting transfers between devices  20.6 us (9%)
  waiting for transfers between devices  6.07 us (3%)
    all_to_all x6, blocking collectives, exchange(): return lax.all_to_all(value, axes, 0, 0, tiled=True)  157 us
    pallas_call x2, Pallas kernels, aggregate(): pl.pallas_call(partial(aggregate_kernel, parts, targets, transpose), in_s...  17.8 us
    ppermute x6, starting transfers between devices, from_ahead(): lax.ppermute(value, axis, [(i, (i - steps) % size) for i in range(size)])  10.8 us
    ppermute x5, starting transfers between devices, swap(): return lax.ppermute(value, axis, [(0, 1), (1, 0)])  9.71 us
    pallas_call x1, Pallas kernels, build_tiles(): pl.pallas_call(tile_kernel, in_specs=[SMEM, ANY, ANY], out_specs=ANY, out...  5.38 us
  transfers between devices with their start and end apart: 11, of which 4 were waited for; matrix products, arithmetic and copies ran while one was open for 0% of the time, Pallas kernels for 9%

profile of v9, /device:TPU:1, one launch (start us, length us, event | category | flops | bytes accessed | tf_op | source)
XLA Modules:
  0.0 221.7 jit_solution(1018240415257060736)
XLA Ops:
  0.6 2.6 %shard_map.104 = (f32[384,256]{1,0:T(8,128)S(1)}, f32[608,384]{1,0:T(8,128)S(1)}, f32[384,128]{1,0:T(8,128)S(1)}) custom-call(f32[602,384]{1,0:T(8,128)} %bitcast.30, f32[602,256]{1,0:T(8,128)} %weight_hbm.1, s32[384]{0:T(512)} %degree_hbm.1), custom_call_target="tpu_custom_call" | custom-call | tf_op jit(solution)/shard_map/pallas_call | solution.py:270
  3.5 43.2 %all_to_all.30 = f32[8,384,256]{2,1,0:T(8,128)} all-to-all(f32[8,384,256]{2,1,0:T(8,128)S(1)} %broadcast_in_dim.15), channel_id=1, replica_groups=mesh['x'=4,'zl'=2,'core'=2,'y'=4,'zh'=2] {'x','zl'}, dimensions={0} | all-to-all | bytes 6291456 | tf_op jit(solution)/shard_map/all_to_all | solution.py:349
  46.7 1.9 collective-permute-start
  52.6 5.4 %shard_map.105.tiles_ref = bf16[256,128,128]{2,1,0:T(8,128)(2,1)} custom-call(s32[1]{0:T(128)} %bitcast.22.live_ref, s32[256,256]{1,0:T(8,128)} %bitcast.31, s32[256,256]{1,0:T(8,128)} %bitcast.32), custom_call_target="tpu_custom_call" | custom-call | flops 1000000 | bytes 100000 | tf_op jit(solution)/shard_map/pallas_call | solution.py:89
  58.2 52.4 %conditional.2 = ((f32[384,256]{1,0:T(8,128)}, f32[384,256]{1,0:T(8,128)S(1)})) conditional(s32[]{:T(128)} %bitcast.5, (f32[8,384,256]{2,1,0:T(8,128)}, f32[384,256]{1,0:T(8,128)S(1)}, f32[8,384,256]{2,1,0:T(8,128)}) %tuple.41, (s32[256]{0:T(256)S(1)}, s32[256]{0:T(256)S(1)}, s32[256]{0:T(256)S(1)}, f32[8,384,256]{2,1,0:T(8,128)}, ...), branch_computations={%region_0.1_spmd, %region_1.2_spmd} | conditional | flops 1000768 | bytes 9541344 | solution.py:416
  58.9 9.4 %branch_1_fun.2 = f32[24,128,256]{2,1,0:T(8,128)S(1)} custom-call(s32[1]{0:T(128)} %get-tuple-element.41.live_ref, s32[256]{0:T(256)S(1)} %add_add_fusion.pick_ref, s32[256]{0:T(256)S(1)} %get-tuple-element.45.place_ref, s32[2]{0:T(128)S(1)} %get-tuple-element.46.own_ref, bf16[256,128,128]{2,1,0:T(8,128)(2,1)} %get-tuple-element.47.tiles_ref, ...), custom_call_target="tpu_custom_call" | custom-call | flops 1000000 | bytes 100000 | tf_op jit(solution)/shard_map/cond/branch_1_fun/pallas_call | solution.py:179
  68.4 40.5 %all_to_all.28.parts_ref = f32[8,384,256]{2,1,0:T(8,128)S(1)} all-to-all(f32[8,384,256]{2,1,0:T(8,128)S(1)} %bitcast.24), channel_id=1, replica_groups=mesh['x'=4,'zl'=2,'core'=2,'y'=4,'zh'=2] {'y','zh'}, dimensions={0} | all-to-all | bytes 6291456 | tf_op jit(solution)/shard_map/cond/branch_1_fun/all_to_all | solution.py:349
  108.9 1.7 branch_1_fun.3
  110.6 4.1 %collective-permute-start.5 = (f32[608,384]{1,0:T(8,128)S(1)}, f32[608,384]{1,0:T(8,128)}, u32[]{:S(2)}, u32[]{:S(2)}) collective-permute-start(f32[608,384]{1,0:T(8,128)S(1)} %collective-permute-done.1.refs_1_), channel_id=1, source_target_pairs={{0,96},{32,0},{64,32},{96,64},{1,97},{33,1},{65,33},{97,65},{2,98}... | collective-permute-start | bytes 2801672 | tf_op jit(solution)/shard_map/ppermute | solution.py:362
  114.7 3.8 %collective-permute-start.6 = (f32[608,384]{1,0:T(8,128)S(1)}, f32[608,384]{1,0:T(8,128)}, u32[]{:S(2)}, u32[]{:S(2)}) collective-permute-start(f32[608,384]{1,0:T(8,128)S(1)} %collective-permute-done.1.refs_1_), channel_id=1, source_target_pairs={{0,64},{32,96},{64,0},{96,32},{1,65},{33,97},{65,1},{97,33},{2,66}... | collective-permute-start | bytes 2801672 | tf_op jit(solution)/shard_map/ppermute | solution.py:362
  119.3 38.9 %conditional.3 = (f32[8,384,256]{2,1,0:T(8,128)}) conditional(s32[]{:T(128)} %bitcast.5, f32[384,256]{1,0:T(8,128)S(1)} %get-tuple-element.85, f32[384,256]{1,0:T(8,128)S(1)} %get-tuple-element.85), branch_computations={%region_2.3_spmd, %region_3.4_spmd} | conditional | bytes 9830408 | solution.py:419
  119.6 38.6 %all_to_all.29 = f32[8,384,256]{2,1,0:T(8,128)} all-to-all(f32[8,384,256]{2,1,0:T(8,128)S(1)} %broadcast_in_dim.11), channel_id=1, replica_groups=mesh['x'=4,'zl'=2,'core'=2,'y'=4,'zh'=2] {'y','zh'}, dimensions={0} | all-to-all | bytes 6291456 | tf_op jit(solution)/shard_map/cond/branch_1_fun/all_to_all | solution.py:349
  158.2 1.7 collective-permute-done.7.refs_7_
  159.8 8.4 %shard_map.107 = (f32[24,128,256]{2,1,0:T(8,128)S(1)}, f32[24,128,256]{2,1,0:T(8,128)S(1)}) custom-call(s32[1]{0:T(128)} %bitcast.23.live_ref, s32[256]{0:T(256)S(1)} %bitcast.34, s32[256]{0:T(256)S(1)} %get-tuple-element.98.place_ref, s32[2]{0:T(128)S(1)} %pad_add_fusion.own_ref, bf16[256,128,128]{2,1,0:T(8,128)(2,1)} %shard_map.105.tiles_ref, ...), custom_call_target="tpu_custom_call" | custom-call | flops 1000000 | bytes 100000 | tf_op jit(solution)/shard_map/pallas_call | solution.py:179
  168.2 1.9 collective-permute-start.8
  170.1 3.4 %shard_map.106 = (bf16[4,608,768]{2,1,0:T(8,128)(2,1)S(1)}, bf16[4,608,768]{2,1,0:T(8,128)(2,1)S(1)}) custom-call(f32[608,384]{1,0:T(8,128)S(1)} %get-tuple-element.81.refs_0_, f32[608,384]{1,0:T(8,128)S(1)} %collective-permute-done.1.refs_1_, f32[608,384]{1,0:T(8,128)S(1)} %collective-permute-done.2.refs_2_, f32[608,384]{1,0:T(8,128)} %collective-permute-done.5.refs_3_, ...), custom_call_target="tpu_custom_call" | custom-call | flops 1000000 | bytes 10000000 | tf_op jit(solution)/shard_map/pallas_call | solution.py:303
  173.5 1.9 collective-permute-done.8.came_ref
  175.4 3.2 %shard_map.108 = (f32[320,256]{1,0:T(8,128)S(1)}, f32[320,256]{1,0:T(8,128)S(1)}) custom-call(s32[1]{0:T(128)} %bitcast.15.core_ref, bf16[4,608,768]{2,1,0:T(8,128)(2,1)S(1)} %get-tuple-element.91.high_ref, bf16[4,608,768]{2,1,0:T(8,128)(2,1)S(1)} %get-tuple-element.92.low_ref, f32[24,128,256]{2,1,0:T(8,128)S(1)} %get-tuple-element.94.kept_ref, ...), custom_call_target="tpu_custom_call" | custom-call | flops 3019898880 | bytes 10000000 | tf_op jit(solution)/shard_map/pallas_call | solution.py:335
  179.0 1.3 collective-permute-done.9
  180.3 14.8 %all_to_all.31 = f32[8,40,256]{2,1,0:T(8,128)S(1)} all-to-all(f32[8,40,256]{2,1,0:T(8,128)S(1)} %bitcast.29), channel_id=1, replica_groups=mesh['x'=4,'zl'=2,'core'=2,'y'=4,'zh'=2] {'x','zl'}, dimensions={0} | all-to-all | bytes 655360 | tf_op jit(solution)/shard_map/all_to_all | solution.py:349
  195.2 11.0 %all_to_all.32 = f32[8,40,256]{2,1,0:T(8,128)S(1)} all-to-all(f32[8,40,256]{2,1,0:T(8,128)S(1)} %broadcast_in_dim.16), channel_id=1, replica_groups=mesh['x'=4,'zl'=2,'core'=2,'y'=4,'zh'=2] {'y','zh'}, dimensions={0} | all-to-all | bytes 655360 | tf_op jit(solution)/shard_map/all_to_all | solution.py:349
  206.2 9.0 %all_to_all.33 = f32[8,40,256]{2,1,0:T(8,128)S(1)} all-to-all(f32[8,40,256]{2,1,0:T(8,128)S(1)} %broadcast_in_dim.17), channel_id=1, replica_groups=mesh['x'=4,'zl'=2,'core'=2,'y'=4,'zh'=2] {'x','zl'}, dimensions={0} | all-to-all | bytes 655360 | tf_op jit(solution)/shard_map/all_to_all | solution.py:349
  215.2 4.3 %collective-permute-start.10 = (f32[320,256]{1,0:T(8,128)S(1)}, f32[320,256]{1,0:T(8,128)S(1)}, u32[]{:S(2)}, u32[]{:S(2)}) collective-permute-start(f32[320,256]{1,0:T(8,128)S(1)} %bitcast.27), channel_id=1, source_target_pairs={{0,8},{8,0},{1,9},{9,1},{2,10},{10,2},{3,11},{11,3},{4,12},{12,4},... | collective-permute-start | bytes 983048 | tf_op jit(solution)/shard_map/ppermute | solution.py:357
  219.6 1.3 collective-permute-done.10
  (37 shorter events, 7.0 us)
Async XLA Ops:
  46.7 11.4 %collective-permute-start = (f32[8,384,256]{2,1,0:T(8,128)}, f32[8,384,256]{2,1,0:T(8,128)}, u32[]{:S(2)}, u32[]{:S(2)}) collective-permute-start(f32[8,384,256]{2,1,0:T(8,128)} %all_to_all.30), channel_id=1, source_target_pairs={{0,8},{8,0},{1,9},{9,1},{2,10},{10,2},{3,11},{11,3},{4,12},{12,4},... | collective-permute-start | bytes 9437192 | tf_op jit(solution)/shard_map/ppermute | solution.py:357
  48.6 62.0 %collective-permute-start.1 = (f32[608,384]{1,0:T(8,128)S(1)}, f32[608,384]{1,0:T(8,128)S(1)}, u32[]{:S(2)}, u32[]{:S(2)}) collective-permute-start(f32[608,384]{1,0:T(8,128)S(1)} %get-tuple-element.81.refs_0_), channel_id=1, source_target_pairs={{0,16},{16,0},{1,17},{17,1},{2,18},{18,2},{3,19},{19,3},{4,20},{20... | collective-permute-start | bytes 2801672 | tf_op jit(solution)/shard_map/ppermute | solution.py:357
  49.8 60.8 %collective-permute-start.2 = (f32[608,384]{1,0:T(8,128)S(1)}, f32[608,384]{1,0:T(8,128)S(1)}, u32[]{:S(2)}, u32[]{:S(2)}) collective-permute-start(f32[608,384]{1,0:T(8,128)S(1)} %get-tuple-element.81.refs_0_), channel_id=1, source_target_pairs={{0,96},{32,0},{64,32},{96,64},{1,97},{33,1},{65,33},{97,65},{2,98}... | collective-permute-start | bytes 2801672 | tf_op jit(solution)/shard_map/ppermute | solution.py:362
  50.7 59.9 %collective-permute-start.3 = (f32[608,384]{1,0:T(8,128)S(1)}, f32[608,384]{1,0:T(8,128)}, u32[]{:S(2)}, u32[]{:S(2)}) collective-permute-start(f32[608,384]{1,0:T(8,128)S(1)} %get-tuple-element.81.refs_0_), channel_id=1, source_target_pairs={{0,64},{32,96},{64,0},{96,32},{1,65},{33,97},{65,1},{97,33},{2,66}... | collective-permute-start | bytes 2801672 | tf_op jit(solution)/shard_map/ppermute | solution.py:362
  51.9 58.7 %collective-permute-start.4 = (f32[608,384]{1,0:T(8,128)S(1)}, f32[608,384]{1,0:T(8,128)}, u32[]{:S(2)}, u32[]{:S(2)}) collective-permute-start(f32[608,384]{1,0:T(8,128)S(1)} %get-tuple-element.81.refs_0_), channel_id=1, source_target_pairs={{0,32},{32,64},{64,96},{96,0},{1,33},{33,65},{65,97},{97,1},{2,34}... | collective-permute-start | bytes 2801672 | tf_op jit(solution)/shard_map/ppermute | solution.py:362
  52.5 5.5 %copy-start.4 = (s32[1,1,256]{2,1,0:T(1,128)S(1)}, s32[1,1,256]{2,1,0:T(1,128)}, u32[]{:S(2)}) copy-start(s32[1,1,256]{2,1,0:T(1,128)} %param.18) | copy-start | bytes 3076
  52.6 5.6 %copy-start = (f32[384,256]{1,0:T(8,128)S(1)}, f32[384,256]{1,0:T(8,128)}, u32[]{:S(2)}) copy-start(f32[384,256]{1,0:T(8,128)} %param.15) | copy-start | bytes 1179652
  52.6 5.6 %copy-start.3 = (s32[1,1,256]{2,1,0:T(1,128)S(1)}, s32[1,1,256]{2,1,0:T(1,128)}, u32[]{:S(2)}) copy-start(s32[1,1,256]{2,1,0:T(1,128)} %param.17) | copy-start | bytes 3076
  58.2 0.7 copy-start.1
  68.3 40.5 %copy-start.2 = (f32[384,256]{1,0:T(8,128)S(1)}, f32[384,256]{1,0:T(8,128)}, u32[]{:S(2)}) copy-start(f32[384,256]{1,0:T(8,128)} %copy-done.1) | copy-start | bytes 1179652 | tf_op jit(solution)/shard_map/cond
  110.6 47.6 %collective-permute-start.5 = (f32[608,384]{1,0:T(8,128)S(1)}, f32[608,384]{1,0:T(8,128)}, u32[]{:S(2)}, u32[]{:S(2)}) collective-permute-start(f32[608,384]{1,0:T(8,128)S(1)} %collective-permute-done.1.refs_1_), channel_id=1, source_target_pairs={{0,96},{32,0},{64,32},{96,64},{1,97},{33,1},{65,33},{97,65},{2,98}... | collective-permute-start | bytes 2801672 | tf_op jit(solution)/shard_map/ppermute | solution.py:362
  114.7 43.5 %collective-permute-start.6 = (f32[608,384]{1,0:T(8,128)S(1)}, f32[608,384]{1,0:T(8,128)}, u32[]{:S(2)}, u32[]{:S(2)}) collective-permute-start(f32[608,384]{1,0:T(8,128)S(1)} %collective-permute-done.1.refs_1_), channel_id=1, source_target_pairs={{0,64},{32,96},{64,0},{96,32},{1,65},{33,97},{65,1},{97,33},{2,66}... | collective-permute-start | bytes 2801672 | tf_op jit(solution)/shard_map/ppermute | solution.py:362
  118.6 41.3 %collective-permute-start.7 = (f32[608,384]{1,0:T(8,128)S(1)}, f32[608,384]{1,0:T(8,128)}, u32[]{:S(2)}, u32[]{:S(2)}) collective-permute-start(f32[608,384]{1,0:T(8,128)S(1)} %collective-permute-done.1.refs_1_), channel_id=1, source_target_pairs={{0,32},{32,64},{64,96},{96,0},{1,33},{33,65},{65,97},{97,1},{2,34}... | collective-permute-start | bytes 2801672 | tf_op jit(solution)/shard_map/ppermute | solution.py:362
  168.2 7.2 %collective-permute-start.8 = (f32[24,128,256]{2,1,0:T(8,128)S(1)}, f32[24,128,256]{2,1,0:T(8,128)S(1)}, u32[]{:S(2)}, u32[]{:S(2)}) collective-permute-start(f32[24,128,256]{2,1,0:T(8,128)S(1)} %get-tuple-element.95), channel_id=1, source_target_pairs={{0,8},{8,0},{1,9},{9,1},{2,10},{10,2},{3,11},{11,3},{4,12},{12,4},... | collective-permute-start | bytes 9437192 | tf_op jit(solution)/shard_map/ppermute | solution.py:357
  178.5 1.7 collective-permute-start.9
  215.2 5.6 %collective-permute-start.10 = (f32[320,256]{1,0:T(8,128)S(1)}, f32[320,256]{1,0:T(8,128)S(1)}, u32[]{:S(2)}, u32[]{:S(2)}) collective-permute-start(f32[320,256]{1,0:T(8,128)S(1)} %bitcast.27), channel_id=1, source_target_pairs={{0,8},{8,0},{1,9},{9,1},{2,10},{10,2},{3,11},{11,3},{4,12},{12,4},... | collective-permute-start | bytes 983048 | tf_op jit(solution)/shard_map/ppermute | solution.py:357

commit v10 on v9

--- a/solution.py
+++ b/solution.py
@@ -411,7 +411,7 @@
         return activate(exchange(sums.reshape(-1, own_rows, hidden_width), REP), cotangent, scales)
 
     def never(near, far, cotangent, scales):
-        return near[0] + cotangent, far[0] - cotangent
+        return near[0] + far[0], near[0] - far[0]
 
     hidden, back_own = lax.cond(always, forward, never, near, far, cotangent, scales)
     across, here_x, back_own = lax.optimization_barrier((across, here_x, back_own))

time: 222 us -> 223 us (level)
  blocking collectives: 157 us -> 172 us
  starting transfers between devices: 20.6 us -> 12.7 us
  Pallas kernels: 34 us -> 27.3 us
    all_to_all x6, blocking collectives: 157 us -> 172 us  [exchange(): return lax.all_to_all(value, axes, 0, 0, tiled=True)]
    ppermute x6, starting transfers between devices: 10.8 us -> 3.64 us  [from_ahead(): lax.ppermute(value, axis, [(i, (i - steps) % size) for i in range(size)])]
    pallas_call x2, Pallas kernels: 17.8 us -> 12.8 us  [aggregate(): pl.pallas_call(partial(aggregate_kernel, parts, targets, transpose), in_s...]
  transfers between devices with their start and end apart: 11 -> 11, of which waited for: 4 -> 4; matrix products, arithmetic and copies ran while one was open for 0% -> 0% of each run, Pallas kernels for 9% -> 7%
where the time goes in v10:
time: 223 us
  blocking collectives  172 us (77%)
  Pallas kernels  27.3 us (12%)
  starting transfers between devices  12.7 us (6%)
  waiting for transfers between devices  7.27 us (3%)
    all_to_all x6, blocking collectives, exchange(): return lax.all_to_all(value, axes, 0, 0, tiled=True)  172 us
    pallas_call x2, Pallas kernels, aggregate(): pl.pallas_call(partial(aggregate_kernel, parts, targets, transpose), in_s...  12.8 us
    ppermute x5, starting transfers between devices, swap(): return lax.ppermute(value, axis, [(0, 1), (1, 0)])  9.09 us
  transfers between devices with their start and end apart: 11, of which 4 were waited for; matrix products, arithmetic and copies ran while one was open for 0% of the time, Pallas kernels for 7%

profile of v10, /device:TPU:1, one launch (start us, length us, event | category | flops | bytes accessed | tf_op | source)
XLA Modules:
  0.0 222.6 jit_solution(2849525119122559979)
XLA Ops:
  0.6 2.6 %shard_map.105 = (f32[384,256]{1,0:T(8,128)S(1)}, f32[608,384]{1,0:T(8,128)S(1)}, f32[384,128]{1,0:T(8,128)S(1)}) custom-call(f32[602,384]{1,0:T(8,128)} %bitcast.30, f32[602,256]{1,0:T(8,128)} %weight_hbm.1, s32[384]{0:T(512)} %degree_hbm.1), custom_call_target="tpu_custom_call" | custom-call | tf_op jit(solution)/shard_map/pallas_call | solution.py:270
  3.5 43.2 %all_to_all.30 = f32[8,384,256]{2,1,0:T(8,128)} all-to-all(f32[8,384,256]{2,1,0:T(8,128)S(1)} %broadcast_in_dim.15), channel_id=1, replica_groups=mesh['x'=4,'zl'=2,'core'=2,'y'=4,'zh'=2] {'x','zl'}, dimensions={0} | all-to-all | bytes 6291456 | tf_op jit(solution)/shard_map/all_to_all | solution.py:349
  46.7 1.9 collective-permute-start
  50.7 1.2 collective-permute-start.3
  52.6 3.6 %shard_map.106.tiles_ref = bf16[256,128,128]{2,1,0:T(8,128)(2,1)} custom-call(s32[1]{0:T(128)} %bitcast.22.live_ref, s32[256,256]{1,0:T(8,128)} %bitcast.31, s32[256,256]{1,0:T(8,128)} %bitcast.32), custom_call_target="tpu_custom_call" | custom-call | flops 1000000 | bytes 100000 | tf_op jit(solution)/shard_map/pallas_call | solution.py:89
  56.4 61.1 %conditional.2 = ((f32[384,256]{1,0:T(8,128)}, f32[384,256]{1,0:T(8,128)S(1)})) conditional(s32[]{:T(128)} %bitcast.5, (f32[8,384,256]{2,1,0:T(8,128)}, f32[8,384,256]{2,1,0:T(8,128)}) %tuple.25, (s32[256]{0:T(256)S(1)}, s32[256]{0:T(256)S(1)}, s32[256]{0:T(256)S(1)}, f32[8,384,256]{2,1,0:T(8,128)}, f32[8,384,256]{2,1,0:T(8,128)}, ...), branch_computations={%region_0.1_spmd, %region_1.2_spmd} | conditional | flops 1000768 | bytes 7968452 | solution.py:416
  56.4 7.0 %branch_1_fun.2 = f32[24,128,256]{2,1,0:T(8,128)S(1)} custom-call(s32[1]{0:T(128)} %get-tuple-element.38.live_ref, s32[256]{0:T(256)S(1)} %add_add_fusion.pick_ref, s32[256]{0:T(256)S(1)} %get-tuple-element.42.place_ref, s32[2]{0:T(128)S(1)} %get-tuple-element.43.own_ref, bf16[256,128,128]{2,1,0:T(8,128)(2,1)} %get-tuple-element.44.tiles_ref, ...), custom_call_target="tpu_custom_call" | custom-call | flops 1000000 | bytes 100000 | tf_op jit(solution)/shard_map/cond/branch_1_fun/pallas_call | solution.py:179
  63.4 52.3 %all_to_all.28.parts_ref = f32[8,384,256]{2,1,0:T(8,128)S(1)} all-to-all(f32[8,384,256]{2,1,0:T(8,128)S(1)} %bitcast.24), channel_id=1, replica_groups=mesh['x'=4,'zl'=2,'core'=2,'y'=4,'zh'=2] {'y','zh'}, dimensions={0} | all-to-all | bytes 6291456 | tf_op jit(solution)/shard_map/cond/branch_1_fun/all_to_all | solution.py:349
  115.8 1.7 branch_1_fun.3
  117.7 1.4 collective-permute-start.7
  119.0 40.0 %conditional.3 = (f32[8,384,256]{2,1,0:T(8,128)}) conditional(s32[]{:T(128)} %bitcast.5, f32[384,256]{1,0:T(8,128)S(1)} %get-tuple-element.82, f32[384,256]{1,0:T(8,128)S(1)} %get-tuple-element.82), branch_computations={%region_2.3_spmd, %region_3.4_spmd} | conditional | bytes 9830408 | solution.py:419
  119.3 39.7 %all_to_all.29 = f32[8,384,256]{2,1,0:T(8,128)} all-to-all(f32[8,384,256]{2,1,0:T(8,128)S(1)} %broadcast_in_dim.11), channel_id=1, replica_groups=mesh['x'=4,'zl'=2,'core'=2,'y'=4,'zh'=2] {'y','zh'}, dimensions={0} | all-to-all | bytes 6291456 | tf_op jit(solution)/shard_map/cond/branch_1_fun/all_to_all | solution.py:349
  159.0 2.9 %collective-permute-done.7.refs_7_ = f32[608,384]{1,0:T(8,128)} collective-permute-done((f32[608,384]{1,0:T(8,128)S(1)}, f32[608,384]{1,0:T(8,128)}, u32[]{:S(2)}, u32[]{:S(2)}) %collective-permute-start.7) | collective-permute-done | bytes 933920 | tf_op jit(solution)/shard_map/ppermute | solution.py:362
  161.9 5.8 %shard_map.108 = (f32[24,128,256]{2,1,0:T(8,128)S(1)}, f32[24,128,256]{2,1,0:T(8,128)S(1)}) custom-call(s32[1]{0:T(128)} %bitcast.23.live_ref, s32[256]{0:T(256)S(1)} %bitcast.34, s32[256]{0:T(256)S(1)} %get-tuple-element.97.place_ref, s32[2]{0:T(128)S(1)} %pad_add_fusion.own_ref, bf16[256,128,128]{2,1,0:T(8,128)(2,1)} %shard_map.106.tiles_ref, ...), custom_call_target="tpu_custom_call" | custom-call | flops 1000000 | bytes 100000 | tf_op jit(solution)/shard_map/pallas_call | solution.py:179
  167.7 1.3 collective-permute-start.8
  169.0 3.4 %shard_map.107 = (bf16[4,608,768]{2,1,0:T(8,128)(2,1)S(1)}, bf16[4,608,768]{2,1,0:T(8,128)(2,1)S(1)}) custom-call(f32[608,384]{1,0:T(8,128)S(1)} %get-tuple-element.78.refs_0_, f32[608,384]{1,0:T(8,128)S(1)} %collective-permute-done.1.refs_1_, f32[608,384]{1,0:T(8,128)S(1)} %collective-permute-done.2.refs_2_, f32[608,384]{1,0:T(8,128)} %collective-permute-done.5.refs_3_, ...), custom_call_target="tpu_custom_call" | custom-call | flops 1000000 | bytes 10000000 | tf_op jit(solution)/shard_map/pallas_call | solution.py:303
  172.4 1.9 collective-permute-done.8.came_ref
  174.3 3.2 %shard_map.109 = (f32[320,256]{1,0:T(8,128)S(1)}, f32[320,256]{1,0:T(8,128)S(1)}) custom-call(s32[1]{0:T(128)} %bitcast.15.core_ref, bf16[4,608,768]{2,1,0:T(8,128)(2,1)S(1)} %get-tuple-element.88.high_ref, bf16[4,608,768]{2,1,0:T(8,128)(2,1)S(1)} %get-tuple-element.89.low_ref, f32[24,128,256]{2,1,0:T(8,128)S(1)} %get-tuple-element.91.kept_ref, ...), custom_call_target="tpu_custom_call" | custom-call | flops 3019898880 | bytes 10000000 | tf_op jit(solution)/shard_map/pallas_call | solution.py:335
  177.9 1.3 collective-permute-done.9
  179.2 16.0 %all_to_all.31 = f32[8,40,256]{2,1,0:T(8,128)S(1)} all-to-all(f32[8,40,256]{2,1,0:T(8,128)S(1)} %bitcast.29), channel_id=1, replica_groups=mesh['x'=4,'zl'=2,'core'=2,'y'=4,'zh'=2] {'x','zl'}, dimensions={0} | all-to-all | bytes 655360 | tf_op jit(solution)/shard_map/all_to_all | solution.py:349
  195.3 11.7 %all_to_all.32 = f32[8,40,256]{2,1,0:T(8,128)S(1)} all-to-all(f32[8,40,256]{2,1,0:T(8,128)S(1)} %broadcast_in_dim.16), channel_id=1, replica_groups=mesh['x'=4,'zl'=2,'core'=2,'y'=4,'zh'=2] {'y','zh'}, dimensions={0} | all-to-all | bytes 655360 | tf_op jit(solution)/shard_map/all_to_all | solution.py:349
  207.1 9.0 %all_to_all.33 = f32[8,40,256]{2,1,0:T(8,128)S(1)} all-to-all(f32[8,40,256]{2,1,0:T(8,128)S(1)} %broadcast_in_dim.17), channel_id=1, replica_groups=mesh['x'=4,'zl'=2,'core'=2,'y'=4,'zh'=2] {'x','zl'}, dimensions={0} | all-to-all | bytes 655360 | tf_op jit(solution)/shard_map/all_to_all | solution.py:349
  216.1 4.3 %collective-permute-start.10 = (f32[320,256]{1,0:T(8,128)S(1)}, f32[320,256]{1,0:T(8,128)S(1)}, u32[]{:S(2)}, u32[]{:S(2)}) collective-permute-start(f32[320,256]{1,0:T(8,128)S(1)} %bitcast.27), channel_id=1, source_target_pairs={{0,8},{8,0},{1,9},{9,1},{2,10},{10,2},{3,11},{11,3},{4,12},{12,4},... | collective-permute-start | bytes 983048 | tf_op jit(solution)/shard_map/ppermute | solution.py:357
  220.4 1.3 collective-permute-done.10
  (33 shorter events, 4.4 us)
Async XLA Ops:
  46.7 9.7 %collective-permute-start = (f32[8,384,256]{2,1,0:T(8,128)}, f32[8,384,256]{2,1,0:T(8,128)}, u32[]{:S(2)}, u32[]{:S(2)}) collective-permute-start(f32[8,384,256]{2,1,0:T(8,128)} %all_to_all.30), channel_id=1, source_target_pairs={{0,8},{8,0},{1,9},{9,1},{2,10},{10,2},{3,11},{11,3},{4,12},{12,4},... | collective-permute-start | bytes 9437192 | tf_op jit(solution)/shard_map/ppermute | solution.py:357
  48.6 68.9 %collective-permute-start.1 = (f32[608,384]{1,0:T(8,128)S(1)}, f32[608,384]{1,0:T(8,128)S(1)}, u32[]{:S(2)}, u32[]{:S(2)}) collective-permute-start(f32[608,384]{1,0:T(8,128)S(1)} %get-tuple-element.78.refs_0_), channel_id=1, source_target_pairs={{0,16},{16,0},{1,17},{17,1},{2,18},{18,2},{3,19},{19,3},{4,20},{20... | collective-permute-start | bytes 2801672 | tf_op jit(solution)/shard_map/ppermute | solution.py:357
  49.8 67.7 %collective-permute-start.2 = (f32[608,384]{1,0:T(8,128)S(1)}, f32[608,384]{1,0:T(8,128)S(1)}, u32[]{:S(2)}, u32[]{:S(2)}) collective-permute-start(f32[608,384]{1,0:T(8,128)S(1)} %get-tuple-element.78.refs_0_), channel_id=1, source_target_pairs={{0,96},{32,0},{64,32},{96,64},{1,97},{33,1},{65,33},{97,65},{2,98}... | collective-permute-start | bytes 2801672 | tf_op jit(solution)/shard_map/ppermute | solution.py:362
  50.7 66.8 %collective-permute-start.3 = (f32[608,384]{1,0:T(8,128)S(1)}, f32[608,384]{1,0:T(8,128)}, u32[]{:S(2)}, u32[]{:S(2)}) collective-permute-start(f32[608,384]{1,0:T(8,128)S(1)} %get-tuple-element.78.refs_0_), channel_id=1, source_target_pairs={{0,64},{32,96},{64,0},{96,32},{1,65},{33,97},{65,1},{97,33},{2,66}... | collective-permute-start | bytes 2801672 | tf_op jit(solution)/shard_map/ppermute | solution.py:362
  51.9 65.6 %collective-permute-start.4 = (f32[608,384]{1,0:T(8,128)S(1)}, f32[608,384]{1,0:T(8,128)}, u32[]{:S(2)}, u32[]{:S(2)}) collective-permute-start(f32[608,384]{1,0:T(8,128)S(1)} %get-tuple-element.78.refs_0_), channel_id=1, source_target_pairs={{0,32},{32,64},{64,96},{96,0},{1,33},{33,65},{65,97},{97,1},{2,34}... | collective-permute-start | bytes 2801672 | tf_op jit(solution)/shard_map/ppermute | solution.py:362
  52.5 3.8 %copy-start.2 = (s32[1,1,256]{2,1,0:T(1,128)S(1)}, s32[1,1,256]{2,1,0:T(1,128)}, u32[]{:S(2)}) copy-start(s32[1,1,256]{2,1,0:T(1,128)} %param.18) | copy-start | bytes 3076
  52.6 3.8 %copy-start.1 = (s32[1,1,256]{2,1,0:T(1,128)S(1)}, s32[1,1,256]{2,1,0:T(1,128)}, u32[]{:S(2)}) copy-start(s32[1,1,256]{2,1,0:T(1,128)} %param.17) | copy-start | bytes 3076
  63.4 52.3 %copy-start = (f32[384,256]{1,0:T(8,128)S(1)}, f32[384,256]{1,0:T(8,128)}, u32[]{:S(2)}) copy-start(f32[384,256]{1,0:T(8,128)} %get-tuple-element.96.cotangent_ref) | copy-start | bytes 1179652 | tf_op jit(solution)/shard_map/cond
  117.5 41.5 %collective-permute-start.5 = (f32[608,384]{1,0:T(8,128)S(1)}, f32[608,384]{1,0:T(8,128)}, u32[]{:S(2)}, u32[]{:S(2)}) collective-permute-start(f32[608,384]{1,0:T(8,128)S(1)} %collective-permute-done.1.refs_1_), channel_id=1, source_target_pairs={{0,96},{32,0},{64,32},{96,64},{1,97},{33,1},{65,33},{97,65},{2,98}... | collective-permute-start | bytes 2801672 | tf_op jit(solution)/shard_map/ppermute | solution.py:362
  117.6 41.5 %collective-permute-start.6 = (f32[608,384]{1,0:T(8,128)S(1)}, f32[608,384]{1,0:T(8,128)}, u32[]{:S(2)}, u32[]{:S(2)}) collective-permute-start(f32[608,384]{1,0:T(8,128)S(1)} %collective-permute-done.1.refs_1_), channel_id=1, source_target_pairs={{0,64},{32,96},{64,0},{96,32},{1,65},{33,97},{65,1},{97,33},{2,66}... | collective-permute-start | bytes 2801672 | tf_op jit(solution)/shard_map/ppermute | solution.py:362
  117.7 44.2 %collective-permute-start.7 = (f32[608,384]{1,0:T(8,128)S(1)}, f32[608,384]{1,0:T(8,128)}, u32[]{:S(2)}, u32[]{:S(2)}) collective-permute-start(f32[608,384]{1,0:T(8,128)S(1)} %collective-permute-done.1.refs_1_), channel_id=1, source_target_pairs={{0,32},{32,64},{64,96},{96,0},{1,33},{33,65},{65,97},{97,1},{2,34}... | collective-permute-start | bytes 2801672 | tf_op jit(solution)/shard_map/ppermute | solution.py:362
  167.7 6.5 %collective-permute-start.8 = (f32[24,128,256]{2,1,0:T(8,128)S(1)}, f32[24,128,256]{2,1,0:T(8,128)S(1)}, u32[]{:S(2)}, u32[]{:S(2)}) collective-permute-start(f32[24,128,256]{2,1,0:T(8,128)S(1)} %get-tuple-element.92), channel_id=1, source_target_pairs={{0,8},{8,0},{1,9},{9,1},{2,10},{10,2},{3,11},{11,3},{4,12},{12,4},... | collective-permute-start | bytes 9437192 | tf_op jit(solution)/shard_map/ppermute | solution.py:357
  177.5 1.7 collective-permute-start.9
  216.1 5.6 %collective-permute-start.10 = (f32[320,256]{1,0:T(8,128)S(1)}, f32[320,256]{1,0:T(8,128)S(1)}, u32[]{:S(2)}, u32[]{:S(2)}) collective-permute-start(f32[320,256]{1,0:T(8,128)S(1)} %bitcast.27), channel_id=1, source_target_pairs={{0,8},{8,0},{1,9},{9,1},{2,10},{10,2},{3,11},{11,3},{4,12},{12,4},... | collective-permute-start | bytes 983048 | tf_op jit(solution)/shard_map/ppermute | solution.py:357
